TPU v7x, 128 devices: a whole 4x4x4 slice. The times are simulated.
128 devices in a mesh: grp: 4 (over x_hi, core), dev: 32 (over y, x_lo, z).
Axes of the slice: x: 4 (x_hi: 2, x_lo: 2; x = x_hi * 2 + x_lo), y: 4, z: 4, core: 2. Of those that a mesh axis runs over, the one named last changes fastest.
Arguments:
- queries: bfloat16 [512, 4, 8192], P(('grp', 'dev')), may hold values from -6 to 6
- prefix_kv: bfloat16 [4, 16384, 2, 512], P('grp', 'dev'), may hold values from -8 to 8
- pool: bfloat16 [3072, 2, 128, 512], P(('grp', 'dev')), may hold values from -8 to 8
- new_kv: bfloat16 [512, 4, 2, 512], P(('grp', 'dev')), may hold values from -16 to 16
- unique_len: int32 [512], P(('grp', 'dev')), may hold values from 1 to 768, as said below
- page_table: int32 [128, 24], P(('grp', 'dev')), may hold values from 0 to 23, each once within a row
- send_slots: int32 [128, 24], P(('grp', 'dev')), may hold values from 0 to 23, each once within a row
Outputs:
- attended: bfloat16 [512, 4, 8192], P(('grp', 'dev'))
Inputs may be any that keep to these rules, and one draw needn't show every extreme that they name: `unique_len`: some request has exactly 768 tokens. `page_table`: each row is a permutation. `send_slots`: each row is a permutation.
All inputs are finite; a program needn't handle non-finite values.
Results may differ from a plain program's by a relative error of at most 0.024.
Values may be sent and summed in bfloat16 or wider, within the bound.
No kernel may reach another device: no remote copies, remote signals or barrier semaphores. Data moves between devices by JAX's collectives and lax.ppermute only.
A program may use at most 192 MiB of HBM per device.

v0:
```python
import math

import jax
import jax.numpy as jnp
from jax import lax
from jax.sharding import PartitionSpec as P

HQ = 64
KVH = 4
HD = 128
GQA = 16
STEPS = 4
PAGE = 128
MAXP = 6


LOWEST_SCORE = -1e30


def arrange(asked):
    request_count = asked.shape[0]
    heads_split = asked.reshape(request_count, STEPS, KVH, GQA, HD).transpose(2, 0, 1, 3, 4)
    return heads_split.reshape(KVH, request_count, STEPS * GQA, HD)


def partial_softmax(queried, key_rows, value_rows, alive, scaling):
    score = (
        jnp.einsum("krqd,rtkd->krqt", queried, key_rows, preferred_element_type=jnp.float32)
        * scaling
    )
    score = jnp.where(alive, score, LOWEST_SCORE)
    highest = score.max(-1)
    weights = jnp.where(alive, jnp.exp(score - highest[..., None]), 0.0)
    weight_sum = weights.sum(-1)
    weighted = jnp.einsum(
        "krqt,rtkd->krqd",
        weights.astype(jnp.bfloat16),
        value_rows,
        preferred_element_type=jnp.float32,
    )
    return (highest, weight_sum, weighted)


def combine(first_part, second_part):
    highest = jnp.maximum(first_part[0], second_part[0])
    fade_first = jnp.exp(first_part[0] - highest)
    fade_second = jnp.exp(second_part[0] - highest)
    weight_sum = first_part[1] * fade_first + second_part[1] * fade_second
    weighted = first_part[2] * fade_first[..., None] + second_part[2] * fade_second[..., None]
    return (highest, weight_sum, weighted)


def local(queries, prefix_kv, pool, new_kv, unique_len, page_table, send_slots):
    groups = lax.axis_size("grp")
    request_count = queries.shape[0]
    row_count = STEPS * GQA
    scaling = 1.0 / math.sqrt(HD)
    span = MAXP * PAGE
    queried = arrange(queries)
    token_ids = jnp.arange(span, dtype=jnp.int32)
    start_state = (
        jnp.full((KVH, request_count, row_count), LOWEST_SCORE, jnp.float32),
        jnp.zeros((KVH, request_count, row_count), jnp.float32),
        jnp.zeros((KVH, request_count, row_count, HD), jnp.float32),
    )
    running = start_state
    shard_piece = lax.all_gather(prefix_kv, "dev", axis=1, tiled=True)
    token_count = shard_piece.shape[1]
    width = math.gcd(token_count, 1024)
    key_blocks = shard_piece[0].reshape(token_count // width, width, 2, KVH, HD)

    def advance(state, key_block):
        highest, weight_sum, weighted = state
        score = (
            jnp.einsum(
                "krqd,tkd->krqt", queried, key_block[:, 0], preferred_element_type=jnp.float32
            )
            * scaling
        )
        new_high = jnp.maximum(highest, score.max(-1))
        fading = jnp.exp(highest - new_high)
        weights = jnp.exp(score - new_high[..., None])
        weight_sum = weight_sum * fading + weights.sum(-1)
        weighted = weighted * fading[..., None] + jnp.einsum(
            "krqt,tkd->krqd",
            weights.astype(jnp.bfloat16),
            key_block[:, 1],
            preferred_element_type=jnp.float32,
        )
        return ((new_high, weight_sum, weighted), None)

    running, unused = lax.scan(advance, running, key_blocks)
    capacity = send_slots.shape[1] // groups
    outgoing = pool[send_slots[0]].reshape(groups, capacity, 2, PAGE, KVH * HD)
    arrived = lax.all_to_all(outgoing, "grp", split_axis=0, concat_axis=0, tiled=True)
    arrived = arrived.reshape(groups * capacity, 2, PAGE, KVH * HD)
    fetched = arrived[page_table[0].reshape(request_count, MAXP)]
    key_rows = fetched[:, :, 0].reshape(request_count, span, KVH, HD)
    value_rows = fetched[:, :, 1].reshape(request_count, span, KVH, HD)
    alive = token_ids[None, :] < unique_len[:, None]
    unique_part = partial_softmax(queried, key_rows, value_rows, alive[None, :, None, :], scaling)
    fresh_keys = new_kv[:, :, 0].reshape(request_count, STEPS, KVH, HD)
    fresh_vals = new_kv[:, :, 1].reshape(request_count, STEPS, KVH, HD)
    causal = (
        jnp.arange(row_count, dtype=jnp.int32)[:, None] // GQA
        >= jnp.arange(STEPS, dtype=jnp.int32)[None, :]
    )
    fresh_part = partial_softmax(queried, fresh_keys, fresh_vals, causal[None, None], scaling)
    highest, weight_sum, weighted = combine(combine(running, unique_part), fresh_part)
    result = weighted / weight_sum[..., None]
    result = result.reshape(KVH, request_count, STEPS, GQA, HD).transpose(1, 2, 0, 3, 4)
    return result.reshape(request_count, STEPS, HQ * HD).astype(jnp.bfloat16)


def solution(mesh):
    placed = (
        P(("grp", "dev"), None, None),
        P("grp", "dev", None, None),
        P(("grp", "dev"), None, None, None),
        P(("grp", "dev"), None, None, None),
        P(("grp", "dev")),
        P(("grp", "dev"), None),
        P(("grp", "dev"), None),
    )
    return jax.shard_map(
        local, mesh=mesh, in_specs=placed, out_specs=P(("grp", "dev"), None, None), check_vma=False
    )
```

profile of v0, /device:TPU:1, one launch (start us, length us, event | category | flops | bytes accessed | tf_op | source)
XLA Modules:
  0.0 612.7 jit_solution(6311091498580333666)
XLA Ops:
  7.9 7.2 %gather_fusion = bf16[24,2,128,512]{3,2,1,0:T(8,128)(2,1)} fusion(bf16[24,2,128,512]{3,2,1,0:T(8,128)(2,1)} %param.11, s32[1024]{0:T(1024)S(1)} %pad_clamp_fusion.1), kind=kCustom, calls=%fused_computation | custom fusion | bytes 12583008 | tf_op jit(solution)/shard_map/gather | solution.py:94
  15.1 6.7 %all-to-all-start = ((bf16[4,6,2,128,512]{4,3,2,1,0:T(8,128)(2,1)}), bf16[4,6,2,128,512]{4,3,2,1,0:T(8,128)(2,1)}, u32[]{:S(2)}, u32[]{:S(2)}) async-start(bf16[4,6,2,128,512]{4,3,2,1,0:T(8,128)(2,1)} %bitcast.125), calls=%async_computation | async-start | bytes 12582912 | tf_op jit(solution)/shard_map/all_to_all | solution.py:95
  24.1 136.7 %all-to-all-done = bf16[4,6,2,128,512]{4,3,2,1,0:T(8,128)(2,1)} async-done(((bf16[4,6,2,128,512]{4,3,2,1,0:T(8,128)(2,1)}), bf16[4,6,2,128,512]{4,3,2,1,0:T(8,128)(2,1)}, u32[]{:S(2)}, u32[]{:S(2)}) %all-to-all-start) | async-done | bytes 6291488 | tf_op jit(solution)/shard_map/all_to_all | solution.py:95
  160.8 7.2 %gather_fusion.1 = bf16[24,2,128,512]{3,2,1,0:T(8,128)(2,1)} fusion(bf16[24,2,128,512]{3,2,1,0:T(8,128)(2,1)} %bitcast.6, s32[1024]{0:T(1024)S(1)} %pad_clamp_fusion), kind=kCustom, calls=%fused_computation.1 | custom fusion | bytes 12583008 | tf_op jit(solution)/shard_map/gather | solution.py:97
  168.0 5.2 slice_bitcast_fusion.5
  173.2 5.5 reshape_squeeze.20
  178.7 3.0 reshape_squeeze.21
  181.7 3.2 bitcast_reduce_fusion.1
  184.9 1.7 copy-done.1
  187.7 256.9 %all-gather.2.cloned.1.call-done = bf16[1,16384,2,512]{3,2,0,1:T(2,128)(2,1)} async-done(((bf16[1,512,2,512]{3,2,0,1:T(2,128)(2,1)}), bf16[1,16384,2,512]{3,2,0,1:T(2,128)(2,1)}) %all-gather.2.cloned.1.call-update) | async-done | bytes 33554448 | tf_op jit(solution)/shard_map/all_gather | solution.py:67
  444.6 52.7 %reshape.178 = bf16[16,1024,2,4,128]{4,3,2,1,0:T(4,128)(2,1)} reshape(bf16[1,16384,2,512]{3,2,0,1:T(2,128)(2,1)} %all-gather.2.cloned.1.call-done) | data formatting | bytes 67108864 | tf_op jit(solution)/shard_map/reshape;squeeze | solution.py:70
  497.3 103.9 %while.15 = (s32[]{:T(128)}, f32[4,4,64]{2,1,0:T(4,128)S(1)}, f32[4,4,64]{2,1,0:T(4,128)S(1)}, f32[4,4,64,128]{3,2,1,0:T(8,128)}, bf16[16,1024,2,4,128]{4,3,2,1,...) while((s32[]{:T(128)}, f32[4,4,64]{2,1,0:T(4,128)S(1)}, ...), condition=%wide.region_3.4_spmd.clone, body=%wide.region_0.3_spmd.clone.sunk | while | flops 545657856 | bytes 28647588 | solution.py:92
  497.3 2.5 constant_dynamic-slice_fusion.2
  503.9 2.3 constant_dynamic-slice_fusion.2
  510.4 2.3 constant_dynamic-slice_fusion.2
  514.8 1.2 fusion.81
  516.9 2.3 constant_dynamic-slice_fusion.2
  521.3 1.2 fusion.81
  523.4 2.3 constant_dynamic-slice_fusion.2
  527.8 1.2 fusion.81
  529.9 2.3 constant_dynamic-slice_fusion.2
  536.3 2.3 constant_dynamic-slice_fusion.2
  542.8 2.3 constant_dynamic-slice_fusion.2
  549.3 2.3 constant_dynamic-slice_fusion.2
  555.8 2.3 constant_dynamic-slice_fusion.2
  562.3 2.3 constant_dynamic-slice_fusion.2
  568.8 2.3 constant_dynamic-slice_fusion.2
  575.2 2.3 constant_dynamic-slice_fusion.2
  581.7 2.3 constant_dynamic-slice_fusion.2
  588.2 2.3 constant_dynamic-slice_fusion.2
  594.7 2.3 constant_dynamic-slice_fusion.2
  601.2 3.4 fusion.40
  (210 shorter events, 68.1 us)
Async XLA Ops:
  6.5 438.1 %all-gather.2.cloned.1.call-start = ((), (), s32[]{:S(2)}) async-start(), calls=%async_computation.1 | async-start | bytes 34603008 | tf_op jit(solution)/shard_map/all_gather | solution.py:67
  15.1 7.3 %copy-start.5 = (s32[1,24]{1,0:T(1,128)S(1)}, s32[1,24]{1,0:T(1,128)}, u32[]{:S(2)}) copy-start(s32[1,24]{1,0:T(1,128)} %param.14) | copy-start | bytes 292
  15.1 8.1 %copy-start.2 = (bf16[4,4,8192]{2,1,0:T(4,128)(2,1)S(1)}, bf16[4,4,8192]{2,1,0:T(4,128)(2,1)}, u32[]{:S(2)}) copy-start(bf16[4,4,8192]{2,1,0:T(4,128)(2,1)} %param.9) | copy-start | bytes 786436
  15.1 8.5 %copy-start.3 = (bf16[4,4,2,512]{3,2,1,0:T(2,128)(2,1)S(1)}, bf16[4,4,2,512]{3,2,1,0:T(2,128)(2,1)}, u32[]{:S(2)}) copy-start(bf16[4,4,2,512]{3,2,1,0:T(2,128)(2,1)} %param.12) | copy-start | bytes 98308
  15.1 8.9 %copy-start.4 = (s32[4]{0:T(128)S(1)}, s32[4]{0:T(128)}, u32[]{:S(2)}) copy-start(s32[4]{0:T(128)} %param.13) | copy-start | bytes 52
  15.1 145.7 %all-to-all-start = ((bf16[4,6,2,128,512]{4,3,2,1,0:T(8,128)(2,1)}), bf16[4,6,2,128,512]{4,3,2,1,0:T(8,128)(2,1)}, u32[]{:S(2)}, u32[]{:S(2)}) async-start(bf16[4,6,2,128,512]{4,3,2,1,0:T(8,128)(2,1)} %bitcast.125), calls=%async_computation | async-start | bytes 12582912 | tf_op jit(solution)/shard_map/all_to_all | solution.py:95
  184.9 1.7 copy-start.1
  497.3 103.9 %copy-start = (bf16[4,768,4,128]{3,2,1,0:T(4,128)(2,1)S(1)}, bf16[4,768,4,128]{3,2,1,0:T(4,128)(2,1)}, u32[]{:S(2)}) copy-start(bf16[4,768,4,128]{3,2,1,0:T(4,128)(2,1)} %reshape_squeeze.21) | copy-start | bytes 9437188
  500.8 1.0 copy-start.6
  507.3 1.0 copy-start.6
  509.6 0.8 copy-start.7
  513.8 1.0 copy-start.6
  516.1 0.8 copy-start.7
  520.3 1.0 copy-start.6
  522.6 0.8 copy-start.7
  526.8 1.0 copy-start.6
  529.1 0.8 copy-start.7
  533.3 1.0 copy-start.6
  535.5 0.8 copy-start.7
  539.7 1.0 copy-start.6
  546.2 1.0 copy-start.6
  548.5 0.8 copy-start.7
  552.7 1.0 copy-start.6
  559.2 1.0 copy-start.6
  561.5 0.8 copy-start.7
  565.7 1.0 copy-start.6
  572.2 1.0 copy-start.6
  574.4 0.8 copy-start.7
  578.6 1.0 copy-start.6
  585.1 1.0 copy-start.6
  591.6 1.0 copy-start.6
  598.1 1.0 copy-start.6
  (8 other events, 6.4 us)
Sparse Core Ops, SparseCore 0:
  9.0 435.5 all-gather.1
where the time goes:
time: 616 us; the launch traced here: 613 us
  waiting for transfers between devices  394 us (64%)
  local copies, waits for them, and re-layouts  140 us (23%)
  matrix products  39.9 us (6%)
  other arithmetic  17.6 us (3%)
  between operations  13.5 us (2%)
  starting transfers between devices  6.75 us (1%)
    all_gather x1, waiting for transfers between devices, local(): shard_piece = lax.all_gather(prefix_kv, 'dev', axis=1, tiled=True)  257 us
    all_to_all x1, waiting for transfers between devices, local(): lax.all_to_all(outgoing, 'grp', split_axis=0, concat_axis=0, tiled=True)  137 us
    another operation x1, local copies, waits for them, and re-layouts, local(): key_blocks = shard_piece[0].reshape(token_count // width, width, 2, KVH, HD)  52.7 us
    dynamic_slice x32, local copies, waits for them, and re-layouts, local(): running, unused = lax.scan(advance, running, key_blocks)  41.5 us
    dot_general x16, matrix products, advance(): jnp.einsum('krqt,tkd->krqd', weights.astype(jnp.bfloat16), key_block[:, 1...  19.7 us
    reduce_sum x16, other arithmetic, advance(): weight_sum = weight_sum * fading + weights.sum(-1)  14.6 us
    while x80, local copies, waits for them, and re-layouts  13.9 us
    dot_general x16, matrix products, advance(): jnp.einsum('krqd,tkd->krqt', queried, key_block[:, 0], preferred_element_...  12.8 us
  transfers between devices with their start and end apart: 2, of which 2 were waited for; matrix products, arithmetic and copies ran while one was open for 6% of the time, Pallas kernels for 0%

commit v1 on v0

v1 whole, which is shorter than its diff:
```python
import functools
import math

import jax
import jax.numpy as jnp
from jax import lax
from jax.experimental import pallas as pl
from jax.experimental.pallas import tpu as pltpu
from jax.sharding import Mesh, PartitionSpec as P

HQ = 64
KVH = 4
HD = 128
GQA = 16
STEPS = 4
PAGE = 128
MAXP = 6
REQ = 4
RS = REQ * STEPS
ROWS = RS * GQA
PACK = ROWS + 16
FLOOR = -1e29
LOWEST = -1e30
LOG2 = math.log2(math.e) / math.sqrt(HD)
AXES = ("grp", "y", "xl", "z")
F32 = jnp.float32
BF16 = jnp.bfloat16


def dot_t(a, b):
    return lax.dot_general(a, b, (((1,), (1,)), ((), ())), preferred_element_type=F32)


def split3(x):
    hi = x.astype(BF16).astype(F32)
    rest = x - hi
    mid = rest.astype(BF16).astype(F32)
    return hi, mid, rest - mid


def pack_stats(m, l):
    lane = lax.broadcasted_iota(jnp.int32, (128, 128), 1)
    parts = []
    for half in range(2):
        rows = slice(half * 128, half * 128 + 128)
        cols = split3(m[rows]) + split3(l[rows])
        stats = jnp.zeros((128, 128), F32)
        for i, col in enumerate(cols):
            stats = jnp.where(lane == i, jnp.broadcast_to(col, (128, 128)), stats)
        parts.append(stats.T[:8])
    return jnp.concatenate(parts, axis=0).astype(BF16)


def unpack_stats(packed):
    wide = packed.astype(F32)
    ms, ls = [], []
    for half in range(2):
        tall = jnp.concatenate(
            [wide[half * 8 : half * 8 + 8], jnp.zeros((120, 128), F32)], axis=0
        ).T
        ms.append(tall[:, 0:1] + tall[:, 1:2] + tall[:, 2:3])
        ls.append(tall[:, 3:4] + tall[:, 4:5] + tall[:, 5:6])
    return jnp.concatenate(ms, axis=0), jnp.concatenate(ls, axis=0)


def online(q, kv_ref, state, tile):
    m, l, o = state
    blocks, _, tokens, _ = kv_ref.shape
    for b in range(blocks):
        for t in range(0, tokens, tile):
            k = kv_ref[b, 0, t : t + tile, :]
            v = kv_ref[b, 1, t : t + tile, :]
            s = dot_t(q, k)
            top = jnp.max(s, axis=-1, keepdims=True)
            new = top if m is None else jnp.maximum(m, top)
            p = jnp.exp2(s * LOG2 - new * LOG2)
            pv = jnp.dot(
                p.astype(BF16),
                jnp.concatenate([v, jnp.ones_like(v)], axis=1),
                preferred_element_type=F32,
            )
            if m is None:
                l, o = pv[:, HD:], pv[:, :HD]
            else:
                fade = jnp.exp2((m - new) * LOG2)
                l, o = l * fade + pv[:, HD:], o * fade + pv[:, :HD]
            m = new
    return m, l, o


def first_kernel(q_ref, kv_ref, o_ref, st_ref, *, tile):
    m, l, o = online(q_ref[...], kv_ref, (None, None, None), tile)
    lane = lax.broadcasted_iota(jnp.int32, o.shape, 1)
    o_ref[...] = o
    st_ref[...] = jnp.where(lane < 64, jnp.broadcast_to(m, o.shape), l)


def second_kernel(q_ref, kv_ref, o_ref, st_ref, out_ref, *, tile):
    st = st_ref[...]
    m, l, o = online(q_ref[...], kv_ref, (st[:, 0:1], st[:, 64:65], o_ref[...]), tile)
    for i in range(q_ref.shape[0] // ROWS):
        rows = slice(i * ROWS, (i + 1) * ROWS)
        out_ref[i, :ROWS, :] = o[rows].astype(BF16)
        out_ref[i, ROWS:, :] = pack_stats(m[rows] * LOG2, l[rows, 0:1])


def prefix_first(q, kv, block, tile):
    n = q.shape[0]
    return pl.pallas_call(
        functools.partial(first_kernel, tile=tile),
        grid=(n // block,),
        in_specs=[
            pl.BlockSpec((block, HD), lambda i: (i, 0)),
            pl.BlockSpec(kv.shape, lambda i: (0, 0, 0, 0)),
        ],
        out_specs=[pl.BlockSpec((block, HD), lambda i: (i, 0))] * 2,
        out_shape=[jax.ShapeDtypeStruct((n, HD), F32)] * 2,
        compiler_params=pltpu.CompilerParams(vmem_limit_bytes=48 << 20),
        cost_estimate=pl.CostEstimate(
            flops=n * 2048 * HD * 4, bytes_accessed=8 << 20, transcendentals=n * 2048
        ),
        name="prefix_first",
    )(q, kv)


def prefix_second(q, kv, o, st, block, tile):
    n = q.shape[0]
    per = block // ROWS
    return pl.pallas_call(
        functools.partial(second_kernel, tile=tile),
        grid=(n // block,),
        in_specs=[
            pl.BlockSpec((block, HD), lambda i: (i, 0)),
            pl.BlockSpec(kv.shape, lambda i: (0, 0, 0, 0)),
            pl.BlockSpec((block, HD), lambda i: (i, 0)),
            pl.BlockSpec((block, HD), lambda i: (i, 0)),
        ],
        out_specs=pl.BlockSpec((per, PACK, HD), lambda i: (i, 0, 0)),
        out_shape=jax.ShapeDtypeStruct((n // ROWS, PACK, HD), BF16),
        compiler_params=pltpu.CompilerParams(vmem_limit_bytes=48 << 20),
        cost_estimate=pl.CostEstimate(
            flops=n * 2048 * HD * 4, bytes_accessed=8 << 20, transcendentals=n * 2048
        ),
        name="prefix_second",
    )(q, kv, o, st)


def softmax_part(s, v):
    m = jnp.maximum(jnp.max(s, axis=-1, keepdims=True), FLOOR)
    p = jnp.exp2(s * LOG2 - m * LOG2)
    l = jnp.sum(p, axis=-1, keepdims=True)
    o = jnp.dot(p.astype(BF16), v, preferred_element_type=F32)
    return m * LOG2, l, o


def page_kernel(slot_ref, req_ref, len_ref, q_ref, *rest):
    pages, out_ref = rest[:MAXP], rest[MAXP]
    t = pl.program_id(0)
    row = lax.broadcasted_iota(jnp.int32, (ROWS, PAGE), 0)
    token = lax.broadcasted_iota(jnp.int32, (ROWS, PAGE), 1)
    owner = lax.div(lax.rem(row, RS), STEPS)
    alive = jnp.concatenate(
        [
            (owner == req_ref[t * MAXP + c]) & (token < len_ref[t * MAXP + c])
            for c in range(MAXP)
        ],
        axis=1,
    )
    for k in range(KVH):
        cols = slice(k * HD, (k + 1) * HD)
        keys = jnp.concatenate([page[0, 0, :, cols] for page in pages], axis=0)
        vals = jnp.concatenate([page[0, 1, :, cols] for page in pages], axis=0)
        s = jnp.where(alive, dot_t(q_ref[0, k], keys), LOWEST)
        m, l, o = softmax_part(s, vals)
        out_ref[0, k, :ROWS, :] = o.astype(BF16)
        out_ref[0, k, ROWS:, :] = pack_stats(m, l)


def page_part(slots, reqs, lens, q, pool):
    n = q.shape[0]

    def page_spec(c):
        return pl.BlockSpec(
            (1, 2, PAGE, KVH * HD), lambda t, slot, req, size: (slot[t * MAXP + c], 0, 0, 0)
        )

    return pl.pallas_call(
        page_kernel,
        grid_spec=pltpu.PrefetchScalarGridSpec(
            num_scalar_prefetch=3,
            grid=(n,),
            in_specs=[pl.BlockSpec((1, KVH, ROWS, HD), lambda t, *_: (t, 0, 0, 0))]
            + [page_spec(c) for c in range(MAXP)],
            out_specs=pl.BlockSpec((1, KVH, PACK, HD), lambda t, *_: (t, 0, 0, 0)),
        ),
        out_shape=jax.ShapeDtypeStruct((n, KVH, PACK, HD), BF16),
        compiler_params=pltpu.CompilerParams(vmem_limit_bytes=48 << 20),
        cost_estimate=pl.CostEstimate(
            flops=n * KVH * ROWS * MAXP * PAGE * HD * 4,
            bytes_accessed=8 << 20,
            transcendentals=n * KVH * ROWS * MAXP * PAGE,
        ),
        name="page_part",
    )(slots, reqs, lens, q, *([pool] * MAXP))


def merge_kernel(q_ref, fresh_ref, part_ref, page_ref, out_ref):
    row = lax.broadcasted_iota(jnp.int32, (ROWS, RS), 0)
    col = lax.broadcasted_iota(jnp.int32, (ROWS, RS), 1)
    rs = lax.rem(row, RS)
    alive = (lax.div(rs, STEPS) == lax.div(col, STEPS)) & (
        lax.rem(col, STEPS) <= lax.rem(rs, STEPS)
    )
    s = jnp.where(alive, dot_t(q_ref[0], fresh_ref[0]), LOWEST)
    found = [softmax_part(s, fresh_ref[1])]
    for ref in (part_ref, page_ref):
        for i in range(ref.shape[0]):
            m, l = unpack_stats(ref[i, 0, ROWS:, :])
            found.append((m, l, ref[i, 0, :ROWS, :].astype(F32)))
    top = functools.reduce(jnp.maximum, [m for m, _, _ in found])
    weight_sum = jnp.zeros((ROWS, 1), F32)
    weighted = jnp.zeros((ROWS, HD), F32)
    for m, l, o in found:
        fade = jnp.exp2(m - top)
        weight_sum = weight_sum + l * fade
        weighted = weighted + o * fade
    result = (weighted / weight_sum).astype(BF16)
    for j in range(GQA):
        out_ref[:, j * HD : (j + 1) * HD] = result[j * RS : (j + 1) * RS]


def merge(q, fresh, parts, pages):
    return pl.pallas_call(
        merge_kernel,
        grid=(KVH,),
        in_specs=[
            pl.BlockSpec((1, ROWS, HD), lambda k: (k, 0, 0)),
            pl.BlockSpec((2, RS, HD), lambda k: (0, 0, k)),
            pl.BlockSpec((parts.shape[0], 1, PACK, HD), lambda k: (0, k, 0, 0)),
            pl.BlockSpec((pages.shape[0], 1, PACK, HD), lambda k: (0, k, 0, 0)),
        ],
        out_specs=pl.BlockSpec((RS, GQA * HD), lambda k: (0, k)),
        out_shape=jax.ShapeDtypeStruct((RS, HQ * HD), BF16),
        compiler_params=pltpu.CompilerParams(vmem_limit_bytes=48 << 20),
        name="merge",
    )(q, fresh, parts, pages)


def shift(x, axis, by):
    n = lax.axis_size(axis)
    return lax.ppermute(x, axis, [((i + by) % n, i) for i in range(n)])


def swap(x, axis, mask):
    return lax.ppermute(x, axis, [(i, i ^ mask) for i in range(lax.axis_size(axis))])


def page_places(unique_len, page_table):
    slot = jnp.arange(REQ * MAXP, dtype=jnp.int32)
    alive = jnp.clip(
        jnp.repeat(unique_len, MAXP) - (slot % MAXP) * PAGE, 0, PAGE
    )
    hit = page_table[0][:, None] == slot[None, :]
    req = jnp.sum(jnp.where(hit, (slot // MAXP)[:, None], 0), axis=0)
    size = jnp.sum(jnp.where(hit, alive[:, None], 0), axis=0)
    return jnp.stack([req, size])


def local(queries, prefix_kv, pool, new_kv, unique_len, page_table, send_slots):
    me = lax.axis_index("grp")
    q = queries.reshape(RS, KVH, GQA, HD).transpose(1, 2, 0, 3).reshape(KVH, ROWS, HD)

    places = page_places(unique_len, page_table).astype(BF16)
    places = jnp.pad(places, ((0, 14), (0, HD - REQ * MAXP)))
    asked = jnp.concatenate([q.reshape(KVH * ROWS, HD), places], axis=0)[None]
    asked = jnp.concatenate([asked, swap(asked, "grp", 2)], axis=0)
    asked = jnp.concatenate([asked, swap(asked, "grp", 1)], axis=0)
    rel = jnp.asarray([0, 2, 1, 3], jnp.int32)
    target = me ^ rel
    slots = send_slots[0].reshape(4, MAXP)[target].reshape(-1)
    info = asked[:, KVH * ROWS : KVH * ROWS + 2, : REQ * MAXP].reshape(4, 2, 4, MAXP)
    info = lax.dynamic_index_in_dim(info, me, 2, keepdims=False).astype(jnp.int32)
    q_all = asked[:, : KVH * ROWS].reshape(4, KVH, ROWS, HD)
    page_out = page_part(slots, info[:, 0].reshape(-1), info[:, 1].reshape(-1), q_all, pool)
    pages = jnp.stack(
        [page_out[0]] + [swap(page_out[i], "grp", g) for i, g in ((1, 2), (2, 1), (3, 3))]
    )

    kv = prefix_kv[0].reshape(-1, 2, KVH, HD).transpose(2, 1, 0, 3)
    tokens = kv.shape[2]
    sent = jnp.concatenate([q, kv.reshape(KVH, 2 * tokens, HD)], axis=1)
    came = lax.all_to_all(sent, "z", 0, 0, tiled=True)
    q_mine = came[:, :ROWS].reshape(4 * ROWS, HD)
    kv_mine = came[:, ROWS:].reshape(4, 2, tokens, HD)
    kv_other = swap(kv_mine, "xl", 1)
    copies = jnp.broadcast_to(q_mine[None], (4, 4 * ROWS, HD))
    q_rows = lax.all_to_all(copies, "y", 0, 0, tiled=True).reshape(16 * ROWS, HD)
    o, st = prefix_first(q_rows, kv_mine, 1024, 512)
    part = prefix_second(q_rows, kv_other, o, st, 1024, 512)
    part = lax.all_to_all(part, ("y", "z"), 0, 0, tiled=True)
    part = part.reshape(4, KVH, PACK, HD)

    fresh = new_kv.transpose(2, 0, 1, 3).reshape(2, RS, KVH * HD)
    result = merge(q, fresh, part, pages)
    return result.reshape(REQ, STEPS, HQ * HD)


def solution(mesh):
    fine = Mesh(mesh.devices.reshape(4, 4, 2, 4), AXES)
    every = P(AXES)
    dev = ("y", "xl", "z")
    placed = (every, P("grp", dev), every, every, every, every, every)
    return jax.shard_map(local, mesh=fine, in_specs=placed, out_specs=every, check_vma=False)
```

time: 616 us -> 140 us (0.23)
  waiting for transfers between devices: 394 us -> 34.3 us
  local copies, waits for them, and re-layouts: 140 us -> 8.58 us
  Pallas kernels: 0 us -> 65.7 us
  matrix products: 39.9 us -> 0 us
  starting transfers between devices: 6.75 us -> 26 us
  between operations: 13.5 us -> 0.19 us
  other arithmetic: 17.6 us -> 4.88 us
    all_gather x1 -> x0, waiting for transfers between devices: 257 us -> none  [local(): shard_piece = lax.all_gather(prefix_kv, 'dev', axis=1, tiled=True)]
    all_to_all x1 -> x3, waiting for transfers between devices: 137 us -> 18.2 us  [the longest x1 13.8 us: local(): came = lax.all_to_all(sent, 'z', 0, 0, tiled=True)]
    pallas_call x0 -> x4, Pallas kernels: none -> 65.7 us  [the longest x1 34.2 us: prefix_second(): pl.pallas_call(functools.partial(second_kernel, tile=tile), grid=(n // bl...]
    another operation x4, local copies, waits for them, and re-layouts: 61.3 us -> 1.99 us  [the longest x1 1.74 us: local(): kv = prefix_kv[0].reshape(-1, 2, KVH, HD).transpose(2, 1, 0, 3)]
    dynamic_slice x32 -> x0, local copies, waits for them, and re-layouts: 41.5 us -> none  [local(): running, unused = lax.scan(advance, running, key_blocks)]
    dot_general x36 -> x0, matrix products: 39.9 us -> none  [the longest x16 19.7 us: advance(): jnp.einsum('krqt,tkd->krqd', weights.astype(jnp.bfloat16), key_block[:, 1...]
    ppermute x0 -> x6, waiting for transfers between devices: none -> 16.1 us  [swap(): lax.ppermute(x, axis, [(i, i ^ mask) for i in range(lax.axis_size(axis))])]
    reduce_sum x18 -> x1, other arithmetic: 15.8 us -> 0.09 us  [page_places(): req = jnp.sum(jnp.where(hit, (slot // MAXP)[:, None], 0), axis=0)]
  transfers between devices with their start and end apart: 2 -> 9, of which waited for: 2 -> 5; matrix products, arithmetic and copies ran while one was open for 6% -> 6% of each run, Pallas kernels for 0% -> 17%
where the time goes in v1:
time: 140 us
  Pallas kernels  65.7 us (47%)
  waiting for transfers between devices  34.3 us (24%)
  starting transfers between devices  26 us (19%)
  local copies, waits for them, and re-layouts  8.58 us (6%)
  other arithmetic  4.88 us (3%)
    pallas_call x1, Pallas kernels, prefix_second(): pl.pallas_call(functools.partial(second_kernel, tile=tile), grid=(n // bl...  34.2 us
    ppermute x6, waiting for transfers between devices, swap(): lax.ppermute(x, axis, [(i, i ^ mask) for i in range(lax.axis_size(axis))])  16.1 us
    all_to_all x1, waiting for transfers between devices, local(): came = lax.all_to_all(sent, 'z', 0, 0, tiled=True)  13.8 us
    pallas_call x1, Pallas kernels, prefix_first(): pl.pallas_call(functools.partial(first_kernel, tile=tile), grid=(n // blo...  13.4 us
    ppermute x6, starting transfers between devices, swap(): lax.ppermute(x, axis, [(i, i ^ mask) for i in range(lax.axis_size(axis))])  10.5 us
    pallas_call x1, Pallas kernels, page_part(): pl.pallas_call(page_kernel, grid_spec=pltpu.PrefetchScalarGridSpec(num_sc...  10.1 us
    pallas_call x1, Pallas kernels, merge(): pl.pallas_call(merge_kernel, grid=(KVH,), in_specs=[pl.BlockSpec((1, ROWS...  8.12 us
    all_to_all x1, starting transfers between devices, local(): came = lax.all_to_all(sent, 'z', 0, 0, tiled=True)  5.99 us
  transfers between devices with their start and end apart: 9, of which 5 were waited for; matrix products, arithmetic and copies ran while one was open for 6% of the time, Pallas kernels for 17%

profile of v1, /device:TPU:1, one launch (start us, length us, event | category | flops | bytes accessed | tf_op | source)
XLA Modules:
  0.0 139.8 jit_solution(12034429800500198852)
XLA Ops:
  0.0 1.2 reshape.66
  1.2 0.2 copy.15
  1.4 1.7 %reshape_squeeze.12 = bf16[512,2,4,128]{3,2,1,0:T(4,128)(2,1)S(1)} reshape(bf16[1,512,2,512]{3,2,1,0:T(2,128)(2,1)} %param.9) | data formatting | bytes 2097152 | tf_op jit(solution)/shard_map/reshape;squeeze | solution.py:289
  3.3 1.2 pad_maximum_fusion
  4.5 6.0 %all-to-all-start = ((bf16[4,1280,128]{2,1,0:T(8,128)(2,1)}), bf16[4,1280,128]{2,1,0:T(8,128)(2,1)S(1)}, u32[]{:S(2)}, u32[]{:S(2)}) async-start(bf16[4,1280,128]{2,1,0:T(8,128)(2,1)} %pad_maximum_fusion), calls=%async_computation | async-start | bytes 2621440 | tf_op jit(solution)/shard_map/all_to_all | solution.py:292
  10.8 2.8 %collective-permute-start.1 = (bf16[1,1040,128]{2,1,0:T(8,128)(2,1)S(1)}, bf16[1,1040,128]{2,1,0:T(8,128)(2,1)S(1)}, u32[]{:S(2)}, u32[]{:S(2)}) collective-permute-start(bf16[1,1040,128]{2,1,0:T(8,128)(2,1)S(1)} %maximum_bitcast_fusion), channel_id=1, source_target_pairs={{0,64},{32,96},{64,0},{96,32},{1,65},{33,97},{65,1},{97,33},{2,66}... | collective-permute-start | bytes 798728 | tf_op jit(solution)/shard_map/ppermute | solution.py:255
  13.7 13.8 %all-to-all-done = bf16[4,1280,128]{2,1,0:T(8,128)(2,1)S(1)} async-done(((bf16[4,1280,128]{2,1,0:T(8,128)(2,1)}), bf16[4,1280,128]{2,1,0:T(8,128)(2,1)S(1)}, u32[]{:S(2)}, u32[]{:S(2)}) %all-to-all-start) | async-done | bytes 1310752 | tf_op jit(solution)/shard_map/all_to_all | solution.py:292
  27.5 1.2 broadcast_in_dim.38
  28.7 0.2 copy-done
  28.9 4.2 %all-to-all-start.1 = ((bf16[4,1024,128]{2,1,0:T(8,128)(2,1)}), bf16[4,1024,128]{2,1,0:T(8,128)(2,1)S(1)}, u32[]{:S(2)}, u32[]{:S(2)}) async-start(bf16[4,1024,128]{2,1,0:T(8,128)(2,1)} %broadcast_in_dim.38), calls=%async_computation.1 | async-start | bytes 2097152 | tf_op jit(solution)/shard_map/all_to_all | solution.py:297
  33.1 0.9 pad_maximum_fusion.4
  34.0 2.1 %collective-permute-start.2 = (bf16[2,1040,128]{2,1,0:T(8,128)(2,1)}, bf16[2,1040,128]{2,1,0:T(8,128)(2,1)}, u32[]{:S(2)}, u32[]{:S(2)}) collective-permute-start(bf16[2,1040,128]{2,1,0:T(8,128)(2,1)} %pad_maximum_fusion.4), channel_id=1, source_target_pairs={{0,32},{32,0},{64,96},{96,64},{1,33},{33,1},{65,97},{97,65},{2,34}... | collective-permute-start | bytes 1597448 | tf_op jit(solution)/shard_map/ppermute | solution.py:255
  36.1 1.3 slice.43
  37.5 1.5 %collective-permute-start = (bf16[4,2,512,128]{3,2,1,0:T(8,128)(2,1)S(1)}, bf16[4,2,512,128]{3,2,1,0:T(8,128)(2,1)S(1)}, u32[]{:S(2)}, u32[]{:S(2)}) collective-permute-start(bf16[4,2,512,128]{3,2,1,0:T(8,128)(2,1)S(1)} %bitcast.39), channel_id=1, source_target_pairs={{0,4},{4,0},{1,5},{5,1},{2,6},{6,2},{3,7},{7,3},{8,12},{12,8},{9,1... | collective-permute-start | bytes 3145736 | tf_op jit(solution)/shard_map/ppermute | solution.py:255
  38.9 0.5 broadcast.90
  39.4 0.7 reduce.11
  40.2 0.6 gather_fusion
  40.9 0.7 pad_maximum_fusion.5
  41.7 4.4 %all-to-all-done.1 = bf16[4,1024,128]{2,1,0:T(8,128)(2,1)S(1)} async-done(((bf16[4,1024,128]{2,1,0:T(8,128)(2,1)}), bf16[4,1024,128]{2,1,0:T(8,128)(2,1)S(1)}, u32[]{:S(2)}, u32[]{:S(2)}) %all-to-all-start.1) | async-done | bytes 1048608 | tf_op jit(solution)/shard_map/all_to_all | solution.py:297
  46.1 13.4 %prefix_first.1 = (f32[4096,128]{1,0:T(8,128)S(1)}, f32[4096,128]{1,0:T(8,128)}) custom-call(bf16[4096,128]{1,0:T(8,128)(2,1)S(1)} %bitcast.37, bf16[4,2,512,128]{3,2,1,0:T(8,128)(2,1)S(1)} %bitcast.40), custom_call_target="tpu_custom_call" | custom-call | flops 4294967296 | bytes 8388608 | tf_op jit(solution)/shard_map/prefix_first/pallas_call | solution.py:109
  59.4 3.0 %collective-permute-done.kv_ref = bf16[4,2,512,128]{3,2,1,0:T(8,128)(2,1)S(1)} collective-permute-done((bf16[4,2,512,128]{3,2,1,0:T(8,128)(2,1)S(1)}, bf16[4,2,512,128]{3,2,1,0:T(8,128)(2,1)S(1)}, u32[]{:S(2)}, u32[]{:S(2)}) %collective-permute-start) | collective-permute-done | bytes 1048608 | tf_op jit(solution)/shard_map/ppermute | solution.py:255
  62.5 34.2 %prefix_second.1 = bf16[16,272,128]{2,1,0:T(8,128)(2,1)} custom-call(bf16[4096,128]{1,0:T(8,128)(2,1)S(1)} %bitcast.38, bf16[4,2,512,128]{3,2,1,0:T(8,128)(2,1)S(1)} %collective-permute-done.kv_ref, f32[4096,128]{1,0:T(8,128)S(1)} %get-tuple-element.7.o_ref, f32[4096,128]{1,0:T(8,128)} %get-tuple-element.8.st_ref), custom_call_target="tpu_custom_call" | custom-call | flops 4294967296 | bytes 8388608 | tf_op jit(solution)/shard_map/prefix_second/pallas_call | solution.py:129
  96.7 5.4 %all-to-all-start.2 = ((bf16[16,272,128]{2,1,0:T(8,128)(2,1)}), bf16[16,272,128]{2,1,0:T(8,128)(2,1)S(1)}, u32[]{:S(2)}, u32[]{:S(2)}) async-start(bf16[16,272,128]{2,1,0:T(8,128)(2,1)} %prefix_second.1), calls=%async_computation.2 | async-start | bytes 2228224 | tf_op jit(solution)/shard_map/all_to_all | solution.py:300
  102.2 1.1 pad_maximum_fusion.2
  103.4 10.1 %page_part.1 = bf16[4,4,272,128]{3,2,1,0:T(8,128)(2,1)S(1)} custom-call(s32[24]{0:T(128)S(1)} %reshape.73.slot_ref, s32[24]{0:T(128)S(1)} %reshape_squeeze.14.req_ref, s32[24]{0:T(128)S(1)} %reshape_squeeze.15.len_ref, bf16[4,4,256,128]{3,2,1,0:T(8,128)(2,1)S(1)} %bitcast.33, bf16[24,2,128,512]{3,2,1,0:T(8,128)(2,1)} %rest_5_.1, ...), custom_call_target="tpu_custom_call" | custom-call | flops 1610612736 | bytes 8388608 | tf_op jit(solution)/shard_map/page_part/pallas_call | solution.py:187
  113.5 3.8 %collective-permute-start.5 = (bf16[4,272,128]{2,1,0:T(8,128)(2,1)S(1)}, bf16[4,272,128]{2,1,0:T(8,128)(2,1)S(1)}, u32[]{:S(2)}, u32[]{:S(2)}) collective-permute-start(bf16[4,272,128]{2,1,0:T(8,128)(2,1)S(1)} %get-tuple-element.14), channel_id=1, source_target_pairs={{0,96},{32,64},{64,32},{96,0},{1,97},{33,65},{65,33},{97,1},{2,98}... | collective-permute-start | bytes 835592 | tf_op jit(solution)/shard_map/ppermute | solution.py:255
  117.3 0.2 collective-permute-start.3
  117.6 7.1 %collective-permute-done.5 = bf16[4,272,128]{2,1,0:T(8,128)(2,1)S(1)} collective-permute-done((bf16[4,272,128]{2,1,0:T(8,128)(2,1)S(1)}, bf16[4,272,128]{2,1,0:T(8,128)(2,1)S(1)}, u32[]{:S(2)}, u32[]{:S(2)}) %collective-permute-start.5) | collective-permute-done | bytes 278560 | tf_op jit(solution)/shard_map/ppermute | solution.py:255
  124.7 6.0 %collective-permute-done.3 = bf16[4,272,128]{2,1,0:T(8,128)(2,1)S(1)} collective-permute-done((bf16[4,272,128]{2,1,0:T(8,128)(2,1)S(1)}, bf16[4,272,128]{2,1,0:T(8,128)(2,1)S(1)}, u32[]{:S(2)}, u32[]{:S(2)}) %collective-permute-start.3) | collective-permute-done | bytes 278560 | tf_op jit(solution)/shard_map/ppermute | solution.py:255
  130.7 0.1 pad_maximum_fusion.1.page_ref
  130.8 8.1 %merge.1 = bf16[16,8192]{1,0:T(8,128)(2,1)S(1)} custom-call(bf16[4,256,128]{2,1,0:T(8,128)(2,1)S(1)} %bitcast.36, bf16[2,16,512]{2,1,0:T(8,128)(2,1)S(1)} %copy.18.fresh_ref, bf16[4,4,272,128]{3,2,1,0:T(8,128)(2,1)S(1)} %bitcast.32, bf16[4,4,272,128]{3,2,1,0:T(8,128)(2,1)S(1)} %pad_maximum_fusion.1.page_ref), custom_call_target="tpu_custom_call" | custom-call | tf_op jit(solution)/shard_map/merge/pallas_call | solution.py:233
  138.9 0.8 reshape.77
  (45 shorter events, 1.1 us)
Async XLA Ops:
  4.5 6.0 %copy-start.6 = (s32[4]{0:T(128)S(1)}, s32[4]{0:T(128)}, u32[]{:S(2)}) copy-start(s32[4]{0:T(128)} %param.12) | copy-start | bytes 52
  4.5 6.2 %copy-start.7 = (s32[1,24]{1,0:T(1,128)S(1)}, s32[1,24]{1,0:T(1,128)}, u32[]{:S(2)}) copy-start(s32[1,24]{1,0:T(1,128)} %param.13) | copy-start | bytes 292
  4.5 23.0 %all-to-all-start = ((bf16[4,1280,128]{2,1,0:T(8,128)(2,1)}), bf16[4,1280,128]{2,1,0:T(8,128)(2,1)S(1)}, u32[]{:S(2)}, u32[]{:S(2)}) async-start(bf16[4,1280,128]{2,1,0:T(8,128)(2,1)} %pad_maximum_fusion), calls=%async_computation | async-start | bytes 2621440 | tf_op jit(solution)/shard_map/all_to_all | solution.py:292
  10.8 22.3 %copy-start.1 = (bf16[1,1040,128]{2,1,0:T(8,128)(2,1)}, bf16[1,1040,128]{2,1,0:T(8,128)(2,1)S(1)}, u32[]{:S(2)}) copy-start(bf16[1,1040,128]{2,1,0:T(8,128)(2,1)S(1)} %maximum_bitcast_fusion) | copy-start | bytes 798724
  10.8 22.2 %collective-permute-start.1 = (bf16[1,1040,128]{2,1,0:T(8,128)(2,1)S(1)}, bf16[1,1040,128]{2,1,0:T(8,128)(2,1)S(1)}, u32[]{:S(2)}, u32[]{:S(2)}) collective-permute-start(bf16[1,1040,128]{2,1,0:T(8,128)(2,1)S(1)} %maximum_bitcast_fusion), channel_id=1, source_target_pairs={{0,64},{32,96},{64,0},{96,32},{1,65},{33,97},{65,1},{97,33},{2,66}... | collective-permute-start | bytes 798728 | tf_op jit(solution)/shard_map/ppermute | solution.py:255
  27.5 1.4 %copy-start = (bf16[4,1280,128]{2,1,0:T(8,128)(2,1)}, bf16[4,1280,128]{2,1,0:T(8,128)(2,1)S(1)}, u32[]{:S(2)}) copy-start(bf16[4,1280,128]{2,1,0:T(8,128)(2,1)S(1)} %all-to-all-done) | copy-start | bytes 3932164
  28.9 17.2 %all-to-all-start.1 = ((bf16[4,1024,128]{2,1,0:T(8,128)(2,1)}), bf16[4,1024,128]{2,1,0:T(8,128)(2,1)S(1)}, u32[]{:S(2)}, u32[]{:S(2)}) async-start(bf16[4,1024,128]{2,1,0:T(8,128)(2,1)} %broadcast_in_dim.38), calls=%async_computation.1 | async-start | bytes 2097152 | tf_op jit(solution)/shard_map/all_to_all | solution.py:297
  33.1 4.4 %copy-start.3 = (bf16[1,1040,128]{2,1,0:T(8,128)(2,1)}, bf16[1,1040,128]{2,1,0:T(8,128)(2,1)S(1)}, u32[]{:S(2)}) copy-start(bf16[1,1040,128]{2,1,0:T(8,128)(2,1)S(1)} %collective-permute-done.1) | copy-start | bytes 798724
  34.0 5.4 %copy-start.8 = (s32[1,24]{1,0:T(1,128)S(1)}, s32[1,24]{1,0:T(1,128)}, u32[]{:S(2)}) copy-start(s32[1,24]{1,0:T(1,128)} %param.14) | copy-start | bytes 292
  34.0 6.2 %copy-start.9 = (s32[4]{0:T(128)S(1)}, s32[4]{0:T(128)}, u32[]{:S(2)}) copy-start(s32[4]{0:T(128)} %constant.41.clone) | copy-start | bytes 52
  34.0 6.9 %collective-permute-start.2 = (bf16[2,1040,128]{2,1,0:T(8,128)(2,1)}, bf16[2,1040,128]{2,1,0:T(8,128)(2,1)}, u32[]{:S(2)}, u32[]{:S(2)}) collective-permute-start(bf16[2,1040,128]{2,1,0:T(8,128)(2,1)} %pad_maximum_fusion.4), channel_id=1, source_target_pairs={{0,32},{32,0},{64,96},{96,64},{1,33},{33,1},{65,97},{97,65},{2,34}... | collective-permute-start | bytes 1597448 | tf_op jit(solution)/shard_map/ppermute | solution.py:255
  37.5 25.0 %collective-permute-start = (bf16[4,2,512,128]{3,2,1,0:T(8,128)(2,1)S(1)}, bf16[4,2,512,128]{3,2,1,0:T(8,128)(2,1)S(1)}, u32[]{:S(2)}, u32[]{:S(2)}) collective-permute-start(bf16[4,2,512,128]{3,2,1,0:T(8,128)(2,1)S(1)} %bitcast.39), channel_id=1, source_target_pairs={{0,4},{4,0},{1,5},{5,1},{2,6},{6,2},{3,7},{7,3},{8,12},{12,8},{9,1... | collective-permute-start | bytes 3145736 | tf_op jit(solution)/shard_map/ppermute | solution.py:255
  96.7 5.6 %copy-start.2 = (bf16[1,1040,128]{2,1,0:T(8,128)(2,1)S(1)}, bf16[1,1040,128]{2,1,0:T(8,128)(2,1)}, u32[]{:S(2)}) copy-start(bf16[1,1040,128]{2,1,0:T(8,128)(2,1)} %copy-done.1) | copy-start | bytes 798724
  96.7 5.6 %copy-start.4 = (bf16[1,1040,128]{2,1,0:T(8,128)(2,1)S(1)}, bf16[1,1040,128]{2,1,0:T(8,128)(2,1)}, u32[]{:S(2)}) copy-start(bf16[1,1040,128]{2,1,0:T(8,128)(2,1)} %copy-done.3) | copy-start | bytes 798724
  96.7 34.2 %all-to-all-start.2 = ((bf16[16,272,128]{2,1,0:T(8,128)(2,1)}), bf16[16,272,128]{2,1,0:T(8,128)(2,1)S(1)}, u32[]{:S(2)}, u32[]{:S(2)}) async-start(bf16[16,272,128]{2,1,0:T(8,128)(2,1)} %prefix_second.1), calls=%async_computation.2 | async-start | bytes 2228224 | tf_op jit(solution)/shard_map/all_to_all | solution.py:300
  113.4 4.1 %copy-start.5 = (bf16[4,4,2,512]{3,2,1,0:T(2,128)(2,1)S(1)}, bf16[4,4,2,512]{3,2,1,0:T(2,128)(2,1)}, u32[]{:S(2)}) copy-start(bf16[4,4,2,512]{3,2,1,0:T(2,128)(2,1)} %param.11) | copy-start | bytes 98308
  113.5 11.2 %collective-permute-start.5 = (bf16[4,272,128]{2,1,0:T(8,128)(2,1)S(1)}, bf16[4,272,128]{2,1,0:T(8,128)(2,1)S(1)}, u32[]{:S(2)}, u32[]{:S(2)}) collective-permute-start(bf16[4,272,128]{2,1,0:T(8,128)(2,1)S(1)} %get-tuple-element.14), channel_id=1, source_target_pairs={{0,96},{32,64},{64,32},{96,0},{1,97},{33,65},{65,33},{97,1},{2,98}... | collective-permute-start | bytes 835592 | tf_op jit(solution)/shard_map/ppermute | solution.py:255
  117.3 7.4 %collective-permute-start.4 = (bf16[4,272,128]{2,1,0:T(8,128)(2,1)S(1)}, bf16[4,272,128]{2,1,0:T(8,128)(2,1)S(1)}, u32[]{:S(2)}, u32[]{:S(2)}) collective-permute-start(bf16[4,272,128]{2,1,0:T(8,128)(2,1)S(1)} %get-tuple-element.15), channel_id=1, source_target_pairs={{0,32},{32,0},{64,96},{96,64},{1,33},{33,1},{65,97},{97,65},{2,34}... | collective-permute-start | bytes 835592 | tf_op jit(solution)/shard_map/ppermute | solution.py:255
  117.3 13.3 %collective-permute-start.3 = (bf16[4,272,128]{2,1,0:T(8,128)(2,1)S(1)}, bf16[4,272,128]{2,1,0:T(8,128)(2,1)S(1)}, u32[]{:S(2)}, u32[]{:S(2)}) collective-permute-start(bf16[4,272,128]{2,1,0:T(8,128)(2,1)S(1)} %get-tuple-element.16), channel_id=1, source_target_pairs={{0,64},{32,96},{64,0},{96,32},{1,65},{33,97},{65,1},{97,33},{2,66}... | collective-permute-start | bytes 835592 | tf_op jit(solution)/shard_map/ppermute | solution.py:255

commit v2 on v1

v2 whole, which is shorter than its diff:
```python
import functools
import math

import jax
import jax.numpy as jnp
from jax import lax
from jax.experimental import pallas as pl
from jax.experimental.pallas import tpu as pltpu
from jax.sharding import Mesh, PartitionSpec as P

HQ = 64
KVH = 4
HD = 128
GQA = 16
STEPS = 4
PAGE = 128
MAXP = 6
REQ = 4
RS = REQ * STEPS
ROWS = RS * GQA
PACK = ROWS + 16
FLOOR = -1e29
LOWEST = -1e30
LOG2 = math.log2(math.e) / math.sqrt(HD)
AXES = ("grp", "y", "xl", "z")
F32 = jnp.float32
BF16 = jnp.bfloat16


def dot_t(a, b):
    return lax.dot_general(a, b, (((1,), (1,)), ((), ())), preferred_element_type=F32)


def split3(x):
    hi = x.astype(BF16).astype(F32)
    rest = x - hi
    mid = rest.astype(BF16).astype(F32)
    return hi, mid, rest - mid


def pack_stats(m, l):
    lane = lax.broadcasted_iota(jnp.int32, (128, 128), 1)
    row = lax.broadcasted_iota(jnp.int32, (8, 128), 0)
    parts = []
    for half in range(ROWS // 128):
        rows = slice(half * 128, half * 128 + 128)
        both = jnp.where(lane < 64, m[rows], l[rows]).T
        stats = jnp.zeros((8, 128), F32)
        for i, found in enumerate(split3(both[:8]) + split3(both[64:72])):
            stats = jnp.where(row == i, found, stats)
        parts.append(stats)
    return jnp.concatenate(parts, axis=0).astype(BF16)


def unpack_stats(packed, half):
    wide = packed.astype(F32)[half * 8 : half * 8 + 8]
    return wide[0:1] + wide[1:2] + wide[2:3], wide[3:4] + wide[4:5] + wide[5:6]


def widen(x, width):
    return jnp.concatenate([x] * (width // HD), axis=1)


def online(q, kv_ref, state, tile):
    m, l, o = state
    blocks, _, tokens, _ = kv_ref.shape
    for b in range(blocks):
        for t in range(0, tokens, tile):
            k = kv_ref[b, 0, t : t + tile, :]
            v = kv_ref[b, 1, t : t + tile, :]
            s = dot_t(q, k)
            top = jnp.broadcast_to(jnp.max(s, axis=-1, keepdims=True), (q.shape[0], HD))
            new = top if m is None else jnp.maximum(m, top)
            p = jnp.exp2(s * LOG2 - widen(new * LOG2, tile))
            pv = jnp.dot(
                p.astype(BF16),
                jnp.concatenate([v, jnp.ones_like(v)], axis=1),
                preferred_element_type=F32,
            )
            if m is None:
                l, o = pv[:, HD:], pv[:, :HD]
            else:
                fade = jnp.exp2((m - new) * LOG2)
                l, o = l * fade + pv[:, HD:], o * fade + pv[:, :HD]
            m = new
    return m, l, o


def first_kernel(q_ref, kv_ref, o_ref, m_ref, l_ref, *, tile):
    m_ref[...], l_ref[...], o_ref[...] = online(q_ref[...], kv_ref, (None, None, None), tile)


def second_kernel(q_ref, kv_ref, o_ref, m_ref, l_ref, out_ref, *, tile):
    m, l, o = online(q_ref[...], kv_ref, (m_ref[...], l_ref[...], o_ref[...]), tile)
    for i in range(q_ref.shape[0] // ROWS):
        rows = slice(i * ROWS, (i + 1) * ROWS)
        out_ref[i, :ROWS, :] = o[rows].astype(BF16)
        out_ref[i, ROWS:, :] = pack_stats(m[rows] * LOG2, l[rows])


def prefix_cost(n):
    return pl.CostEstimate(
        flops=n * 2048 * HD * 16, bytes_accessed=16 << 20, transcendentals=n * 2048
    )


def prefix_first(q, kv, block, tile):
    n = q.shape[0]
    rows = pl.BlockSpec((block, HD), lambda i: (i, 0))
    return pl.pallas_call(
        functools.partial(first_kernel, tile=tile),
        grid=(n // block,),
        in_specs=[rows, pl.BlockSpec(kv.shape, lambda i: (0, 0, 0, 0))],
        out_specs=[rows] * 3,
        out_shape=[jax.ShapeDtypeStruct((n, HD), F32)] * 3,
        compiler_params=pltpu.CompilerParams(vmem_limit_bytes=48 << 20),
        cost_estimate=prefix_cost(n),
        name="prefix_first",
    )(q, kv)


def prefix_second(q, kv, state, block, tile):
    n = q.shape[0]
    per = block // ROWS
    rows = pl.BlockSpec((block, HD), lambda i: (i, 0))
    return pl.pallas_call(
        functools.partial(second_kernel, tile=tile),
        grid=(n // block,),
        in_specs=[rows, pl.BlockSpec(kv.shape, lambda i: (0, 0, 0, 0)), rows, rows, rows],
        out_specs=pl.BlockSpec((per, PACK, HD), lambda i: (i, 0, 0)),
        out_shape=jax.ShapeDtypeStruct((n // ROWS, PACK, HD), BF16),
        compiler_params=pltpu.CompilerParams(vmem_limit_bytes=48 << 20),
        cost_estimate=prefix_cost(n),
        name="prefix_second",
    )(q, kv, *state)


def page_kernel(slot_ref, req_ref, len_ref, q_ref, fresh_ref, *rest):
    pages, out_ref = rest[:MAXP], rest[MAXP]
    t = pl.program_id(0)
    row = lax.broadcasted_iota(jnp.int32, (ROWS, PAGE), 0)
    token = lax.broadcasted_iota(jnp.int32, (ROWS, PAGE), 1)
    step = lax.rem(row, RS)
    owner = lax.div(step, STEPS)
    bounds = [
        jnp.where(owner == req_ref[t * MAXP + c], len_ref[t * MAXP + c], 0) for c in range(MAXP)
    ]

    def attend(own):
        for k in range(KVH):
            cols = slice(k * HD, (k + 1) * HD)
            keys = [page[0, 0, :, cols] for page in pages]
            vals = [page[0, 1, :, cols] for page in pages]
            if own:
                keys.append(fresh_ref[0, :, cols])
                vals.append(fresh_ref[1, :, cols])
            s = dot_t(q_ref[0, k], jnp.concatenate(keys, axis=0))
            parts = [
                jnp.where(token < bounds[c], s[:, c * PAGE : (c + 1) * PAGE], LOWEST)
                for c in range(MAXP)
            ]
            if own:
                alive = (
                    (lax.div(token, STEPS) == owner)
                    & (lax.rem(token, STEPS) <= lax.rem(step, STEPS))
                    & (token < RS)
                )
                parts.append(jnp.where(alive, s[:, MAXP * PAGE :], LOWEST))
            top = jnp.max(functools.reduce(jnp.maximum, parts), axis=-1, keepdims=True)
            m = jnp.maximum(jnp.broadcast_to(top, (ROWS, HD)), FLOOR) * LOG2
            p = [jnp.exp2(part * LOG2 - m).astype(BF16) for part in parts]
            v = jnp.concatenate(vals, axis=0)
            pv = jnp.dot(
                jnp.concatenate(p, axis=1),
                jnp.concatenate([v, jnp.ones_like(v)], axis=1),
                preferred_element_type=F32,
            )
            out_ref[0, k, :ROWS, :] = pv[:, :HD].astype(BF16)
            out_ref[0, k, ROWS:, :] = pack_stats(m, pv[:, HD:])

    @pl.when(t == 0)
    def _():
        attend(True)

    @pl.when(t != 0)
    def _():
        attend(False)


def page_part(slots, reqs, lens, q, fresh, pool):
    n = q.shape[0]

    def page_spec(c):
        return pl.BlockSpec(
            (1, 2, PAGE, KVH * HD), lambda t, slot, req, size: (slot[t * MAXP + c], 0, 0, 0)
        )

    return pl.pallas_call(
        page_kernel,
        grid_spec=pltpu.PrefetchScalarGridSpec(
            num_scalar_prefetch=3,
            grid=(n,),
            in_specs=[
                pl.BlockSpec((1, KVH, ROWS, HD), lambda t, *_: (t, 0, 0, 0)),
                pl.BlockSpec(fresh.shape, lambda t, *_: (0, 0, 0)),
            ]
            + [page_spec(c) for c in range(MAXP)],
            out_specs=pl.BlockSpec((1, KVH, PACK, HD), lambda t, *_: (t, 0, 0, 0)),
        ),
        out_shape=jax.ShapeDtypeStruct((n, KVH, PACK, HD), BF16),
        compiler_params=pltpu.CompilerParams(vmem_limit_bytes=48 << 20),
        cost_estimate=pl.CostEstimate(
            flops=n * KVH * ROWS * MAXP * PAGE * HD * 16,
            bytes_accessed=8 << 20,
            transcendentals=n * KVH * ROWS * MAXP * PAGE,
        ),
        name="page_part",
    )(slots, reqs, lens, q, fresh, *([pool] * MAXP))


def merge_kernel(part_ref, *rest):
    page_refs, out_ref = rest[:-1], rest[-1]
    found = [part_ref.at[i, 0] for i in range(part_ref.shape[0])]
    found += [ref.at[0] for ref in page_refs]
    for half in range(ROWS // 128):
        stats = [unpack_stats(ref[ROWS:, :], half) for ref in found]
        top = functools.reduce(jnp.maximum, [m for m, _ in stats])
        fades = [jnp.exp2(m - top) for m, _ in stats]
        weight_sum = functools.reduce(jnp.add, [l * f for (_, l), f in zip(stats, fades)])
        gains = jnp.concatenate(
            [f / weight_sum for f in fades] + [jnp.zeros((128 - len(fades), 128), F32)], axis=0
        ).T
        total = jnp.zeros((128, HD), F32)
        for i, ref in enumerate(found):
            gain = jnp.broadcast_to(gains[:, i : i + 1], (128, HD))
            total = total + ref[half * 128 : half * 128 + 128, :].astype(F32) * gain
        total = total.astype(BF16)
        for j in range(128 // RS):
            col = half * 128 // RS + j
            out_ref[:, col * HD : (col + 1) * HD] = total[j * RS : (j + 1) * RS]


def merge(parts, pages):
    return pl.pallas_call(
        merge_kernel,
        grid=(KVH,),
        in_specs=[pl.BlockSpec((parts.shape[0], 1, PACK, HD), lambda k: (0, k, 0, 0))]
        + [pl.BlockSpec((1, PACK, HD), lambda k: (k, 0, 0))] * len(pages),
        out_specs=pl.BlockSpec((RS, GQA * HD), lambda k: (0, k)),
        out_shape=jax.ShapeDtypeStruct((RS, HQ * HD), BF16),
        compiler_params=pltpu.CompilerParams(vmem_limit_bytes=48 << 20),
        name="merge",
    )(parts, *pages)


def swap(x, axis, mask):
    return lax.ppermute(x, axis, [(i, i ^ mask) for i in range(lax.axis_size(axis))])


def page_places(unique_len, page_table):
    slot = jnp.arange(REQ * MAXP, dtype=jnp.int32)
    alive = jnp.clip(
        jnp.repeat(unique_len, MAXP) - (slot % MAXP) * PAGE, 0, PAGE
    )
    hit = page_table[0][:, None] == slot[None, :]
    req = jnp.sum(jnp.where(hit, (slot // MAXP)[:, None], 0), axis=0)
    size = jnp.sum(jnp.where(hit, alive[:, None], 0), axis=0)
    return jnp.stack([req, size])


def after(x, *done):
    return lax.optimization_barrier((x, *done))[0]


def local(queries, prefix_kv, pool, new_kv, unique_len, page_table, send_slots):
    me = lax.axis_index("grp")
    kv = prefix_kv[0].reshape(-1, 2, KVH, HD).transpose(2, 1, 0, 3)
    tokens = kv.shape[2]
    kv_near = swap(kv, "xl", 1)
    kv_mine = lax.all_to_all(kv, "z", 0, 0, tiled=True)

    q = queries.reshape(RS, KVH, GQA, HD).transpose(1, 2, 0, 3).reshape(KVH, ROWS, HD)
    copies = jnp.broadcast_to(q[None], (4, KVH, ROWS, HD)).reshape(4 * KVH, ROWS, HD)
    q_rows = lax.all_to_all(copies, ("y", "z"), 0, 0, tiled=True).reshape(16 * ROWS, HD)

    places = page_places(unique_len, page_table).astype(BF16)
    places = jnp.pad(places, ((0, 14), (0, HD - REQ * MAXP)))
    asked = jnp.concatenate([q.reshape(KVH * ROWS, HD), places], axis=0)[None]
    asked = jnp.concatenate([asked, swap(asked, "grp", 2)], axis=0)
    asked = jnp.concatenate([asked, swap(asked, "grp", 1)], axis=0)
    rel = jnp.asarray([0, 2, 1, 3], jnp.int32)
    target = me ^ rel
    slots = send_slots[0].reshape(4, MAXP)[target].reshape(-1)
    info = asked[:, KVH * ROWS : KVH * ROWS + 2, : REQ * MAXP].reshape(4, 2, 4, MAXP)
    info = lax.dynamic_index_in_dim(info, me, 2, keepdims=False).astype(jnp.int32)
    q_all = asked[:, : KVH * ROWS].reshape(4, KVH, ROWS, HD)
    fresh = new_kv.transpose(2, 0, 1, 3).reshape(2, RS, KVH * HD)
    fresh = jnp.pad(fresh, ((0, 0), (0, PAGE - RS), (0, 0)))
    page_out = page_part(
        slots, info[:, 0].reshape(-1), info[:, 1].reshape(-1), q_all, fresh, pool
    )

    kv_other = lax.all_to_all(kv_near, "z", 0, 0, tiled=True)
    q_rows = after(q_rows, page_out)
    state = prefix_first(q_rows, kv_mine, 1024, 256)
    pages = [page_out[0]] + [swap(page_out[i], "grp", g) for i, g in ((1, 2), (2, 1), (3, 3))]
    part = prefix_second(q_rows, kv_other, state, 1024, 256)
    part = lax.all_to_all(part, ("y", "z"), 0, 0, tiled=True)
    part = part.reshape(4, KVH, PACK, HD)
    return merge(part, pages).reshape(REQ, STEPS, HQ * HD)


def solution(mesh):
    fine = Mesh(mesh.devices.reshape(4, 4, 2, 4), AXES)
    every = P(AXES)
    dev = ("y", "xl", "z")
    placed = (every, P("grp", dev), every, every, every, every, every)
    return jax.shard_map(local, mesh=fine, in_specs=placed, out_specs=every, check_vma=False)
```

time: 140 us -> 109 us (0.78)
  Pallas kernels: 65.7 us -> 37.8 us
  waiting for transfers between devices: 34.3 us -> 20.3 us
  starting transfers between devices: 26 us -> 33.3 us
  local copies, waits for them, and re-layouts: 8.58 us -> 12.5 us
    pallas_call x1, Pallas kernels: 34.2 us -> 14.5 us  [prefix_second(): pl.pallas_call(functools.partial(second_kernel, tile=tile), grid=(n // bl...]
    all_to_all x2 -> x3, waiting for transfers between devices: 18.2 us -> 8.26 us  [the longest x1 6.9 us: local(): lax.all_to_all(copies, ('y', 'z'), 0, 0, tiled=True).reshape(16 * ROWS, HD)]
    pallas_call x1, Pallas kernels: 8.12 us -> 2.19 us  [merge(): pl.pallas_call(merge_kernel, grid=(KVH,), in_specs=[pl.BlockSpec((parts.s...]
    all_to_all x2 -> x3, starting transfers between devices: 10.2 us -> 15.7 us  [the longest x1 7.77 us: local(): lax.all_to_all(copies, ('y', 'z'), 0, 0, tiled=True).reshape(16 * ROWS, HD)]
    unnamed x21 -> x18, local copies, waits for them, and re-layouts: 0.75 us -> 5.89 us
    ppermute x6, waiting for transfers between devices: 16.1 us -> 12 us  [swap(): lax.ppermute(x, axis, [(i, i ^ mask) for i in range(lax.axis_size(axis))])]
    all_to_all x1, starting transfers between devices: 5.37 us -> 6.96 us  [local(): part = lax.all_to_all(part, ('y', 'z'), 0, 0, tiled=True)]
  transfers between devices with their start and end apart: 9 -> 10, of which waited for: 5 -> 5; matrix products, arithmetic and copies ran while one was open for 6% -> 9% of each run, Pallas kernels for 17% -> 20%
where the time goes in v2:
time: 109 us; the launch traced here: 108 us
  Pallas kernels  37.8 us (35%)
  starting transfers between devices  33.3 us (31%)
  waiting for transfers between devices  20.3 us (19%)
  local copies, waits for them, and re-layouts  12.5 us (11%)
  other arithmetic  3.53 us (3%)
    pallas_call x1, Pallas kernels, prefix_second(): pl.pallas_call(functools.partial(second_kernel, tile=tile), grid=(n // bl...  14.5 us
    pallas_call x1, Pallas kernels, prefix_first(): pl.pallas_call(functools.partial(first_kernel, tile=tile), grid=(n // blo...  12.2 us
    ppermute x6, waiting for transfers between devices, swap(): lax.ppermute(x, axis, [(i, i ^ mask) for i in range(lax.axis_size(axis))])  12 us
    ppermute x6, starting transfers between devices, swap(): lax.ppermute(x, axis, [(i, i ^ mask) for i in range(lax.axis_size(axis))])  10.6 us
    pallas_call x1, Pallas kernels, page_part(): pl.pallas_call(page_kernel, grid_spec=pltpu.PrefetchScalarGridSpec(num_sc...  8.88 us
    all_to_all x1, starting transfers between devices, local(): lax.all_to_all(copies, ('y', 'z'), 0, 0, tiled=True).reshape(16 * ROWS, HD)  7.77 us
    all_to_all x1, starting transfers between devices, local(): part = lax.all_to_all(part, ('y', 'z'), 0, 0, tiled=True)  6.96 us
    all_to_all x1, waiting for transfers between devices, local(): lax.all_to_all(copies, ('y', 'z'), 0, 0, tiled=True).reshape(16 * ROWS, HD)  6.9 us
  transfers between devices with their start and end apart: 10, of which 5 were waited for; matrix products, arithmetic and copies ran while one was open for 9% of the time, Pallas kernels for 20%

profile of v2, /device:TPU:1, one launch (start us, length us, event | category | flops | bytes accessed | tf_op | source)
XLA Modules:
  0.0 107.6 jit_solution(5840968208817269850)
XLA Ops:
  0.0 0.7 broadcast_in_dim.42
  0.8 1.2 %reshape.60 = bf16[16,4,16,128]{3,2,1,0:T(8,128)(2,1)S(1)} reshape(bf16[4,4,8192]{2,1,0:T(4,128)(2,1)} %param.8) | data formatting | bytes 524288 | tf_op jit(solution)/shard_map/reshape | solution.py:282
  2.3 0.7 select_reduce_fusion.1
  3.1 3.7 %collective-permute-start = (bf16[1,1040,128]{2,1,0:T(8,128)(2,1)S(1)}, bf16[1,1040,128]{2,1,0:T(8,128)(2,1)S(1)}, u32[]{:S(2)}, u32[]{:S(2)}) collective-permute-start(bf16[1,1040,128]{2,1,0:T(8,128)(2,1)S(1)} %maximum_bitcast_fusion), channel_id=1, source_target_pairs={{0,64},{32,96},{64,0},{96,32},{1,65},{33,97},{65,1},{97,33},{2,66}... | collective-permute-start | bytes 798728 | tf_op jit(solution)/shard_map/ppermute | solution.py:257
  6.7 1.2 %broadcast_in_dim.38 = bf16[4,4,256,128]{3,2,1,0:T(8,128)(2,1)} broadcast(bf16[4,256,128]{2,1,0:T(8,128)(2,1)S(1)} %bitcast.34), dimensions={1,2,3} | broadcast | bytes 1310720 | tf_op jit(solution)/shard_map/broadcast_in_dim | solution.py:283
  7.9 7.8 %all-to-all-start = ((bf16[16,256,128]{2,1,0:T(8,128)(2,1)}), bf16[16,256,128]{2,1,0:T(8,128)(2,1)S(1)}, u32[]{:S(2)}, u32[]{:S(2)}) async-start(bf16[16,256,128]{2,1,0:T(8,128)(2,1)} %bitcast.2), calls=%async_computation | async-start | bytes 2097152 | tf_op jit(solution)/shard_map/all_to_all | solution.py:284
  15.7 0.9 pad_maximum_fusion.2
  16.6 1.2 %collective-permute-start.1 = (bf16[2,1040,128]{2,1,0:T(8,128)(2,1)}, bf16[2,1040,128]{2,1,0:T(8,128)(2,1)S(1)}, u32[]{:S(2)}, u32[]{:S(2)}) collective-permute-start(bf16[2,1040,128]{2,1,0:T(8,128)(2,1)} %pad_maximum_fusion.2), channel_id=1, source_target_pairs={{0,32},{32,0},{64,96},{96,64},{1,33},{33,1},{65,97},{97,65},{2,34}... | collective-permute-start | bytes 1597448 | tf_op jit(solution)/shard_map/ppermute | solution.py:257
  17.8 2.4 %copy.26 = bf16[1,512,2,512]{1,3,2,0:T(8,128)(2,1)S(1)} copy(bf16[1,512,2,512]{3,2,1,0:T(2,128)(2,1)} %param.9) | data formatting | bytes 2097152 | tf_op args[1]
  20.3 1.3 %copy.27 = bf16[512,2,4,128]{3,0,1,2:T(8,128)(2,1)} copy(bf16[512,2,4,128]{0,3,2,1:T(8,128)(2,1)S(1)} %bitcast.32) | data formatting | bytes 2097152 | tf_op jit(solution)/shard_map/reshape;squeeze | solution.py:277
  21.6 0.3 collective-permute-start.2
  21.9 0.5 broadcast.92
  22.4 0.7 reduce.11
  23.2 0.6 gather_fusion
  24.0 6.9 %all-to-all-done = bf16[16,256,128]{2,1,0:T(8,128)(2,1)S(1)} async-done(((bf16[16,256,128]{2,1,0:T(8,128)(2,1)}), bf16[16,256,128]{2,1,0:T(8,128)(2,1)S(1)}, u32[]{:S(2)}, u32[]{:S(2)}) %all-to-all-start) | async-done | bytes 1048608 | tf_op jit(solution)/shard_map/all_to_all | solution.py:284
  31.0 3.5 %all-to-all-start.2 = ((bf16[4,2,512,128]{3,2,1,0:T(8,128)(2,1)}), bf16[4,2,512,128]{3,2,1,0:T(8,128)(2,1)S(1)}, u32[]{:S(2)}, u32[]{:S(2)}) async-start(bf16[4,2,512,128]{3,2,1,0:T(8,128)(2,1)} %bitcast.14), calls=%async_computation.2 | async-start | bytes 2097152 | tf_op jit(solution)/shard_map/all_to_all | solution.py:280
  34.7 1.1 %pad_maximum_fusion = bf16[4,1024,128]{2,1,0:T(8,128)(2,1)S(1)} fusion(bf16[2,1040,128]{2,1,0:T(8,128)(2,1)} %copy-done.4, bf16[1,1040,128]{2,1,0:T(8,128)(2,1)S(1)} %copy-done.3, bf16[1,1040,128]{2,1,0:T(8,128)(2,1)S(1)} %maximum_bitcast_fusion), kind=kLoop, calls=%fused_computation.1 | loop fusion | flops 3145728 | bytes 2113536 | tf_op jit(solution)/shard_map/concatenate | solution.py:290
  35.8 8.9 %page_part.1 = bf16[4,4,272,128]{3,2,1,0:T(8,128)(2,1)S(1)} custom-call(s32[24]{0:T(128)S(1)} %reshape.63.slot_ref, s32[24]{0:T(128)S(1)} %reshape_squeeze.13.req_ref, s32[24]{0:T(128)S(1)} %reshape_squeeze.14.len_ref, bf16[4,4,256,128]{3,2,1,0:T(8,128)(2,1)S(1)} %bitcast.29, bf16[2,128,512]{2,1,0:T(8,128)(2,1)S(1)} %pad.9.fresh_ref, ...), custom_call_target="tpu_custom_call" | custom-call | flops 6442450944 | bytes 8388608 | tf_op jit(solution)/shard_map/page_part/pallas_call | solution.py:198
  44.7 1.4 %all-to-all-done.2.kv_ref = bf16[4,2,512,128]{3,2,1,0:T(8,128)(2,1)S(1)} async-done(((bf16[4,2,512,128]{3,2,1,0:T(8,128)(2,1)}), bf16[4,2,512,128]{3,2,1,0:T(8,128)(2,1)S(1)}, u32[]{:S(2)}, u32[]{:S(2)}) %all-to-all-start.2) | async-done | bytes 1048608 | tf_op jit(solution)/shard_map/all_to_all | solution.py:280
  46.0 0.6 collective-permute-done.2
  46.7 4.4 %all-to-all-start.1 = ((bf16[4,2,512,128]{3,2,1,0:T(8,128)(2,1)}), bf16[4,2,512,128]{3,2,1,0:T(8,128)(2,1)}, u32[]{:S(2)}, u32[]{:S(2)}) async-start(bf16[4,2,512,128]{3,2,1,0:T(8,128)(2,1)} %collective-permute-done.2), calls=%async_computation.1 | async-start | bytes 2097152 | tf_op jit(solution)/shard_map/all_to_all | solution.py:303
  51.1 12.2 %prefix_first.1 = (f32[4096,128]{1,0:T(8,128)S(1)}, f32[4096,128]{1,0:T(8,128)}, f32[4096,128]{1,0:T(8,128)}) custom-call(bf16[4096,128]{1,0:T(8,128)(2,1)S(1)} %bitcast.30, bf16[4,2,512,128]{3,2,1,0:T(8,128)(2,1)S(1)} %all-to-all-done.2.kv_ref), custom_call_target="tpu_custom_call" | custom-call | flops 17179869184 | bytes 16777216 | tf_op jit(solution)/shard_map/prefix_first/pallas_call | solution.py:110
  63.3 1.3 %copy-done = f32[4096,128]{1,0:T(8,128)} copy-done((f32[4096,128]{1,0:T(8,128)}, f32[4096,128]{1,0:T(8,128)S(1)}, u32[]{:S(2)}) %copy-start) | copy-done | bytes 2097176
  64.6 1.6 %copy-done.1 = f32[4096,128]{1,0:T(8,128)S(1)} copy-done((f32[4096,128]{1,0:T(8,128)S(1)}, f32[4096,128]{1,0:T(8,128)}, u32[]{:S(2)}) %copy-start.1) | copy-done | bytes 2097176
  66.2 14.5 %prefix_second.1 = bf16[16,272,128]{2,1,0:T(8,128)(2,1)} custom-call(bf16[4096,128]{1,0:T(8,128)(2,1)S(1)} %bitcast.31, bf16[4,2,512,128]{3,2,1,0:T(8,128)(2,1)} %all-to-all-done.1.kv_ref, f32[4096,128]{1,0:T(8,128)S(1)} %copy-done.1, f32[4096,128]{1,0:T(8,128)} %get-tuple-element.11.m_ref, f32[4096,128]{1,0:T(8,128)} %get-tuple-element.12.l_ref), custom_call_target="tpu_custom_call" | custom-call | flops 17179869184 | bytes 16777216 | tf_op jit(solution)/shard_map/prefix_second/pallas_call | solution.py:126
  80.7 7.0 %all-to-all-start.3 = ((bf16[16,272,128]{2,1,0:T(8,128)(2,1)}), bf16[16,272,128]{2,1,0:T(8,128)(2,1)S(1)}, u32[]{:S(2)}, u32[]{:S(2)}) async-start(bf16[16,272,128]{2,1,0:T(8,128)(2,1)} %prefix_second.1), calls=%async_computation.3 | async-start | bytes 2228224 | tf_op jit(solution)/shard_map/all_to_all | solution.py:308
  87.8 2.7 %collective-permute-start.5 = (bf16[4,272,128]{2,1,0:T(8,128)(2,1)S(1)}, bf16[4,272,128]{2,1,0:T(8,128)(2,1)S(1)}, u32[]{:S(2)}, u32[]{:S(2)}) collective-permute-start(bf16[4,272,128]{2,1,0:T(8,128)(2,1)S(1)} %get-tuple-element.17), channel_id=1, source_target_pairs={{0,96},{32,64},{64,32},{96,0},{1,97},{33,65},{65,33},{97,1},{2,98}... | collective-permute-start | bytes 835592 | tf_op jit(solution)/shard_map/ppermute | solution.py:257
  90.5 2.7 %collective-permute-start.3 = (bf16[4,272,128]{2,1,0:T(8,128)(2,1)S(1)}, bf16[4,272,128]{2,1,0:T(8,128)(2,1)S(1)}, u32[]{:S(2)}, u32[]{:S(2)}) collective-permute-start(bf16[4,272,128]{2,1,0:T(8,128)(2,1)S(1)} %get-tuple-element.19), channel_id=1, source_target_pairs={{0,64},{32,96},{64,0},{96,32},{1,65},{33,97},{65,1},{97,33},{2,66}... | collective-permute-start | bytes 835592 | tf_op jit(solution)/shard_map/ppermute | solution.py:257
  93.2 3.7 %collective-permute-done.5.rest_3_ = bf16[4,272,128]{2,1,0:T(8,128)(2,1)S(1)} collective-permute-done((bf16[4,272,128]{2,1,0:T(8,128)(2,1)S(1)}, bf16[4,272,128]{2,1,0:T(8,128)(2,1)S(1)}, u32[]{:S(2)}, u32[]{:S(2)}) %collective-permute-start.5) | collective-permute-done | bytes 278560 | tf_op jit(solution)/shard_map/ppermute | solution.py:257
  96.9 7.7 %collective-permute-done.3.rest_1_ = bf16[4,272,128]{2,1,0:T(8,128)(2,1)S(1)} collective-permute-done((bf16[4,272,128]{2,1,0:T(8,128)(2,1)S(1)}, bf16[4,272,128]{2,1,0:T(8,128)(2,1)S(1)}, u32[]{:S(2)}, u32[]{:S(2)}) %collective-permute-start.3) | collective-permute-done | bytes 278560 | tf_op jit(solution)/shard_map/ppermute | solution.py:257
  104.6 2.2 %merge.1 = bf16[16,8192]{1,0:T(8,128)(2,1)S(1)} custom-call(bf16[4,4,272,128]{3,2,1,0:T(8,128)(2,1)S(1)} %bitcast.28, bf16[4,272,128]{2,1,0:T(8,128)(2,1)S(1)} %get-tuple-element.20.rest_0_, bf16[4,272,128]{2,1,0:T(8,128)(2,1)S(1)} %collective-permute-done.3.rest_1_, bf16[4,272,128]{2,1,0:T(8,128)(2,1)S(1)} %collective-permute-done.4.rest_2_, ...), custom_call_target="tpu_custom_call" | custom-call | tf_op jit(solution)/shard_map/merge/pallas_call | solution.py:244
  106.8 0.8 reshape.69
  (40 shorter events, 0.9 us)
Async XLA Ops:
  3.1 12.6 %collective-permute-start = (bf16[1,1040,128]{2,1,0:T(8,128)(2,1)S(1)}, bf16[1,1040,128]{2,1,0:T(8,128)(2,1)S(1)}, u32[]{:S(2)}, u32[]{:S(2)}) collective-permute-start(bf16[1,1040,128]{2,1,0:T(8,128)(2,1)S(1)} %maximum_bitcast_fusion), channel_id=1, source_target_pairs={{0,64},{32,96},{64,0},{96,32},{1,65},{33,97},{65,1},{97,33},{2,66}... | collective-permute-start | bytes 798728 | tf_op jit(solution)/shard_map/ppermute | solution.py:257
  7.9 23.0 %all-to-all-start = ((bf16[16,256,128]{2,1,0:T(8,128)(2,1)}), bf16[16,256,128]{2,1,0:T(8,128)(2,1)S(1)}, u32[]{:S(2)}, u32[]{:S(2)}) async-start(bf16[16,256,128]{2,1,0:T(8,128)(2,1)} %bitcast.2), calls=%async_computation | async-start | bytes 2097152 | tf_op jit(solution)/shard_map/all_to_all | solution.py:284
  15.7 8.2 %copy-start.2 = (bf16[1,1040,128]{2,1,0:T(8,128)(2,1)}, bf16[1,1040,128]{2,1,0:T(8,128)(2,1)S(1)}, u32[]{:S(2)}) copy-start(bf16[1,1040,128]{2,1,0:T(8,128)(2,1)S(1)} %collective-permute-done) | copy-start | bytes 798724
  16.6 5.8 %copy-start.6 = (s32[1,24]{1,0:T(1,128)S(1)}, s32[1,24]{1,0:T(1,128)}, u32[]{:S(2)}) copy-start(s32[1,24]{1,0:T(1,128)} %param.14) | copy-start | bytes 292
  16.6 6.6 %copy-start.7 = (s32[4]{0:T(128)S(1)}, s32[4]{0:T(128)}, u32[]{:S(2)}) copy-start(s32[4]{0:T(128)} %constant.41.clone) | copy-start | bytes 52
  16.6 7.3 %copy-start.5 = (bf16[4,4,2,512]{3,2,1,0:T(2,128)(2,1)S(1)}, bf16[4,4,2,512]{3,2,1,0:T(2,128)(2,1)}, u32[]{:S(2)}) copy-start(bf16[4,4,2,512]{3,2,1,0:T(2,128)(2,1)} %param.11) | copy-start | bytes 98308
  16.6 7.3 %collective-permute-start.1 = (bf16[2,1040,128]{2,1,0:T(8,128)(2,1)}, bf16[2,1040,128]{2,1,0:T(8,128)(2,1)S(1)}, u32[]{:S(2)}, u32[]{:S(2)}) collective-permute-start(bf16[2,1040,128]{2,1,0:T(8,128)(2,1)} %pad_maximum_fusion.2), channel_id=1, source_target_pairs={{0,32},{32,0},{64,96},{96,64},{1,33},{33,1},{65,97},{97,65},{2,34}... | collective-permute-start | bytes 1597448 | tf_op jit(solution)/shard_map/ppermute | solution.py:257
  21.6 25.1 %collective-permute-start.2 = (bf16[4,2,512,128]{3,2,1,0:T(8,128)(2,1)}, bf16[4,2,512,128]{3,2,1,0:T(8,128)(2,1)}, u32[]{:S(2)}, u32[]{:S(2)}) collective-permute-start(bf16[4,2,512,128]{3,2,1,0:T(8,128)(2,1)} %bitcast.14), channel_id=1, source_target_pairs={{0,4},{4,0},{1,5},{5,1},{2,6},{6,2},{3,7},{7,3},{8,12},{12,8},{9,1... | collective-permute-start | bytes 3145736 | tf_op jit(solution)/shard_map/ppermute | solution.py:257
  23.9 7.0 %copy-start.4 = (bf16[2,1040,128]{2,1,0:T(8,128)(2,1)}, bf16[2,1040,128]{2,1,0:T(8,128)(2,1)S(1)}, u32[]{:S(2)}) copy-start(bf16[2,1040,128]{2,1,0:T(8,128)(2,1)S(1)} %collective-permute-done.1) | copy-start | bytes 1597444
  23.9 10.7 %copy-start.3 = (bf16[1,1040,128]{2,1,0:T(8,128)(2,1)S(1)}, bf16[1,1040,128]{2,1,0:T(8,128)(2,1)}, u32[]{:S(2)}) copy-start(bf16[1,1040,128]{2,1,0:T(8,128)(2,1)} %copy-done.2) | copy-start | bytes 798724
  31.0 15.1 %all-to-all-start.2 = ((bf16[4,2,512,128]{3,2,1,0:T(8,128)(2,1)}), bf16[4,2,512,128]{3,2,1,0:T(8,128)(2,1)S(1)}, u32[]{:S(2)}, u32[]{:S(2)}) async-start(bf16[4,2,512,128]{3,2,1,0:T(8,128)(2,1)} %bitcast.14), calls=%async_computation.2 | async-start | bytes 2097152 | tf_op jit(solution)/shard_map/all_to_all | solution.py:280
  46.7 17.9 %all-to-all-start.1 = ((bf16[4,2,512,128]{3,2,1,0:T(8,128)(2,1)}), bf16[4,2,512,128]{3,2,1,0:T(8,128)(2,1)}, u32[]{:S(2)}, u32[]{:S(2)}) async-start(bf16[4,2,512,128]{3,2,1,0:T(8,128)(2,1)} %collective-permute-done.2), calls=%async_computation.1 | async-start | bytes 2097152 | tf_op jit(solution)/shard_map/all_to_all | solution.py:303
  63.3 1.3 %copy-start = (f32[4096,128]{1,0:T(8,128)}, f32[4096,128]{1,0:T(8,128)S(1)}, u32[]{:S(2)}) copy-start(f32[4096,128]{1,0:T(8,128)S(1)} %get-tuple-element.10.o_ref) | copy-start | bytes 6291460
  64.6 1.6 %copy-start.1 = (f32[4096,128]{1,0:T(8,128)S(1)}, f32[4096,128]{1,0:T(8,128)}, u32[]{:S(2)}) copy-start(f32[4096,128]{1,0:T(8,128)} %copy-done) | copy-start | bytes 6291460
  80.7 23.9 %all-to-all-start.3 = ((bf16[16,272,128]{2,1,0:T(8,128)(2,1)}), bf16[16,272,128]{2,1,0:T(8,128)(2,1)S(1)}, u32[]{:S(2)}, u32[]{:S(2)}) async-start(bf16[16,272,128]{2,1,0:T(8,128)(2,1)} %prefix_second.1), calls=%async_computation.3 | async-start | bytes 2228224 | tf_op jit(solution)/shard_map/all_to_all | solution.py:308
  87.8 9.1 %collective-permute-start.5 = (bf16[4,272,128]{2,1,0:T(8,128)(2,1)S(1)}, bf16[4,272,128]{2,1,0:T(8,128)(2,1)S(1)}, u32[]{:S(2)}, u32[]{:S(2)}) collective-permute-start(bf16[4,272,128]{2,1,0:T(8,128)(2,1)S(1)} %get-tuple-element.17), channel_id=1, source_target_pairs={{0,96},{32,64},{64,32},{96,0},{1,97},{33,65},{65,33},{97,1},{2,98}... | collective-permute-start | bytes 835592 | tf_op jit(solution)/shard_map/ppermute | solution.py:257
  90.5 6.4 %collective-permute-start.4 = (bf16[4,272,128]{2,1,0:T(8,128)(2,1)S(1)}, bf16[4,272,128]{2,1,0:T(8,128)(2,1)S(1)}, u32[]{:S(2)}, u32[]{:S(2)}) collective-permute-start(bf16[4,272,128]{2,1,0:T(8,128)(2,1)S(1)} %get-tuple-element.18), channel_id=1, source_target_pairs={{0,32},{32,0},{64,96},{96,64},{1,33},{33,1},{65,97},{97,65},{2,34}... | collective-permute-start | bytes 835592 | tf_op jit(solution)/shard_map/ppermute | solution.py:257
  90.5 14.1 %collective-permute-start.3 = (bf16[4,272,128]{2,1,0:T(8,128)(2,1)S(1)}, bf16[4,272,128]{2,1,0:T(8,128)(2,1)S(1)}, u32[]{:S(2)}, u32[]{:S(2)}) collective-permute-start(bf16[4,272,128]{2,1,0:T(8,128)(2,1)S(1)} %get-tuple-element.19), channel_id=1, source_target_pairs={{0,64},{32,96},{64,0},{96,32},{1,65},{33,97},{65,1},{97,33},{2,66}... | collective-permute-start | bytes 835592 | tf_op jit(solution)/shard_map/ppermute | solution.py:257

commit v3 on v2

--- a/solution.py
+++ b/solution.py
@@ -86,53 +86,45 @@
     return m, l, o
 
 
-def first_kernel(q_ref, kv_ref, o_ref, m_ref, l_ref, *, tile):
-    m_ref[...], l_ref[...], o_ref[...] = online(q_ref[...], kv_ref, (None, None, None), tile)
-
-
-def second_kernel(q_ref, kv_ref, o_ref, m_ref, l_ref, out_ref, *, tile):
-    m, l, o = online(q_ref[...], kv_ref, (m_ref[...], l_ref[...], o_ref[...]), tile)
-    for i in range(q_ref.shape[0] // ROWS):
-        rows = slice(i * ROWS, (i + 1) * ROWS)
-        out_ref[i, :ROWS, :] = o[rows].astype(BF16)
-        out_ref[i, ROWS:, :] = pack_stats(m[rows] * LOG2, l[rows])
-
-
-def prefix_cost(n):
-    return pl.CostEstimate(
-        flops=n * 2048 * HD * 16, bytes_accessed=16 << 20, transcendentals=n * 2048
-    )
-
-
-def prefix_first(q, kv, block, tile):
-    n = q.shape[0]
-    rows = pl.BlockSpec((block, HD), lambda i: (i, 0))
+def prefix_kernel(at_ref, *refs, tile):
+    q_refs, kv_ref, out_ref, held = refs[:4], refs[4], refs[5], refs[6]
+    i = pl.program_id(0)
+
+    @pl.when(i == 0)
+    def _():
+        for n, q_ref in enumerate(q_refs):
+            held[n] = q_ref[...]
+
+    m, l, o = online(held[i], kv_ref, (None, None, None), tile)
+    for n in range(4):
+        rows = slice(n * ROWS, (n + 1) * ROWS)
+        place = lax.rem(at_ref[1] + n, 4)
+        out_ref[place, :ROWS, :] = o[rows].astype(BF16)
+        out_ref[place, ROWS:, :] = pack_stats(m[rows] * LOG2, l[rows])
+
+
+def prefix_part(at, qs, kv, tile):
+    rows = qs[0].shape[0]
+    tokens = kv.shape[0] * kv.shape[2]
     return pl.pallas_call(
-        functools.partial(first_kernel, tile=tile),
-        grid=(n // block,),
-        in_specs=[rows, pl.BlockSpec(kv.shape, lambda i: (0, 0, 0, 0))],
-        out_specs=[rows] * 3,
-        out_shape=[jax.ShapeDtypeStruct((n, HD), F32)] * 3,
+        functools.partial(prefix_kernel, tile=tile),
+        grid_spec=pltpu.PrefetchScalarGridSpec(
+            num_scalar_prefetch=1,
+            grid=(4,),
+            in_specs=[pl.BlockSpec((rows, HD), lambda i, at: (0, 0))] * 4
+            + [pl.BlockSpec(kv.shape, lambda i, at: (0, 0, 0, 0))],
+            out_specs=pl.BlockSpec((4, PACK, HD), lambda i, at: (lax.rem(at[0] + i, 4), 0, 0)),
+            scratch_shapes=[pltpu.VMEM((4, rows, HD), BF16)],
+        ),
+        out_shape=jax.ShapeDtypeStruct((16, PACK, HD), BF16),
         compiler_params=pltpu.CompilerParams(vmem_limit_bytes=48 << 20),
-        cost_estimate=prefix_cost(n),
-        name="prefix_first",
-    )(q, kv)
-
-
-def prefix_second(q, kv, state, block, tile):
-    n = q.shape[0]
-    per = block // ROWS
-    rows = pl.BlockSpec((block, HD), lambda i: (i, 0))
-    return pl.pallas_call(
-        functools.partial(second_kernel, tile=tile),
-        grid=(n // block,),
-        in_specs=[rows, pl.BlockSpec(kv.shape, lambda i: (0, 0, 0, 0)), rows, rows, rows],
-        out_specs=pl.BlockSpec((per, PACK, HD), lambda i: (i, 0, 0)),
-        out_shape=jax.ShapeDtypeStruct((n // ROWS, PACK, HD), BF16),
-        compiler_params=pltpu.CompilerParams(vmem_limit_bytes=48 << 20),
-        cost_estimate=prefix_cost(n),
-        name="prefix_second",
-    )(q, kv, *state)
+        cost_estimate=pl.CostEstimate(
+            flops=rows * tokens * HD * 32,
+            bytes_accessed=8 << 20,
+            transcendentals=4 * rows * tokens,
+        ),
+        name="prefix_part",
+    )(at, *qs, kv)
 
 
 def page_kernel(slot_ref, req_ref, len_ref, q_ref, fresh_ref, *rest):
@@ -257,6 +249,11 @@
     return lax.ppermute(x, axis, [(i, i ^ mask) for i in range(lax.axis_size(axis))])
 
 
+def fetch(x, axis, by):
+    n = lax.axis_size(axis)
+    return lax.ppermute(x, axis, [((i + by) % n, i) for i in range(n)])
+
+
 def page_places(unique_len, page_table):
     slot = jnp.arange(REQ * MAXP, dtype=jnp.int32)
     alive = jnp.clip(
@@ -273,15 +270,19 @@
 
 
 def local(queries, prefix_kv, pool, new_kv, unique_len, page_table, send_slots):
-    me = lax.axis_index("grp")
+    me, y, z = (lax.axis_index(name) for name in ("grp", "y", "z"))
     kv = prefix_kv[0].reshape(-1, 2, KVH, HD).transpose(2, 1, 0, 3)
     tokens = kv.shape[2]
-    kv_near = swap(kv, "xl", 1)
-    kv_mine = lax.all_to_all(kv, "z", 0, 0, tiled=True)
-
-    q = queries.reshape(RS, KVH, GQA, HD).transpose(1, 2, 0, 3).reshape(KVH, ROWS, HD)
-    copies = jnp.broadcast_to(q[None], (4, KVH, ROWS, HD)).reshape(4 * KVH, ROWS, HD)
-    q_rows = lax.all_to_all(copies, ("y", "z"), 0, 0, tiled=True).reshape(16 * ROWS, HD)
+    kv = jnp.broadcast_to(kv[None], (2, *kv.shape)).reshape(8, 2, tokens, HD)
+    kv_all = lax.all_to_all(kv, ("xl", "z"), 0, 0, tiled=True)
+
+    q = after(queries, kv).reshape(RS, KVH, GQA, HD).transpose(1, 2, 0, 3).reshape(KVH, ROWS, HD)
+
+    def head_of(by):
+        return lax.dynamic_index_in_dim(q, lax.rem(z + 4 - by, 4), 0, keepdims=False)
+
+    rows = jnp.concatenate([head_of(0)] + [fetch(head_of(k), "z", k) for k in (1, 2, 3)], axis=0)
+    qs = [rows] + [fetch(rows, "y", k) for k in (1, 2, 3)]
 
     places = page_places(unique_len, page_table).astype(BF16)
     places = jnp.pad(places, ((0, 14), (0, HD - REQ * MAXP)))
@@ -300,11 +301,9 @@
         slots, info[:, 0].reshape(-1), info[:, 1].reshape(-1), q_all, fresh, pool
     )
 
-    kv_other = lax.all_to_all(kv_near, "z", 0, 0, tiled=True)
-    q_rows = after(q_rows, page_out)
-    state = prefix_first(q_rows, kv_mine, 1024, 256)
+    at = after(jnp.stack([y, z]), page_out)
+    part = prefix_part(at, qs, kv_all, 256)
     pages = [page_out[0]] + [swap(page_out[i], "grp", g) for i, g in ((1, 2), (2, 1), (3, 3))]
-    part = prefix_second(q_rows, kv_other, state, 1024, 256)
     part = lax.all_to_all(part, ("y", "z"), 0, 0, tiled=True)
     part = part.reshape(4, KVH, PACK, HD)
     return merge(part, pages).reshape(REQ, STEPS, HQ * HD)

time: 109 us -> 111 us (1.018)
  the two profiles are of different devices: /device:TPU:1 before, /device:TPU:6 now
where the time goes in v3:
time: 111 us
  Pallas kernels  34.4 us (31%)
  waiting for transfers between devices  32.9 us (30%)
  starting transfers between devices  29.3 us (26%)
  local copies, waits for them, and re-layouts  9.78 us (9%)
  other arithmetic  4.1 us (4%)
    pallas_call x1, Pallas kernels, prefix_part(): pl.pallas_call(functools.partial(prefix_kernel, tile=tile), grid_spec=plt...  23.4 us
    ppermute x6, waiting for transfers between devices, fetch(): return lax.ppermute(x, axis, [((i + by) % n, i) for i in range(n)])  18.7 us
    ppermute x5, waiting for transfers between devices, swap(): lax.ppermute(x, axis, [(i, i ^ mask) for i in range(lax.axis_size(axis))])  11.7 us
    ppermute x6, starting transfers between devices, fetch(): return lax.ppermute(x, axis, [((i + by) % n, i) for i in range(n)])  11.4 us
    pallas_call x1, Pallas kernels, page_part(): pl.pallas_call(page_kernel, grid_spec=pltpu.PrefetchScalarGridSpec(num_sc...  8.81 us
    all_to_all x1, starting transfers between devices, local(): kv_all = lax.all_to_all(kv, ('xl', 'z'), 0, 0, tiled=True)  6.77 us
    all_to_all x1, starting transfers between devices, local(): part = lax.all_to_all(part, ('y', 'z'), 0, 0, tiled=True)  5.94 us
    ppermute x5, starting transfers between devices, swap(): lax.ppermute(x, axis, [(i, i ^ mask) for i in range(lax.axis_size(axis))])  5.2 us
  transfers between devices with their start and end apart: 13, of which 6 were waited for; matrix products, arithmetic and copies ran while one was open for 6% of the time, Pallas kernels for 8%

profile of v3, /device:TPU:6, one launch (start us, length us, event | category | flops | bytes accessed | tf_op | source)
XLA Modules:
  0.0 110.7 jit_solution(5058832909336155595)
XLA Ops:
  0.0 0.7 broadcast_in_dim.40
  0.8 0.7 select_reduce_fusion.1
  1.6 1.7 %reshape_squeeze.13 = bf16[512,2,4,128]{3,2,1,0:T(4,128)(2,1)S(1)} reshape(bf16[1,512,2,512]{3,2,1,0:T(2,128)(2,1)} %param.9) | data formatting | bytes 2097152 | tf_op jit(solution)/shard_map/reshape;squeeze | solution.py:274
  3.5 1.7 %broadcast_in_dim.37 = bf16[2,4,2,512,128]{4,3,2,1,0:T(8,128)(2,1)} broadcast(bf16[4,2,512,128]{3,2,1,0:T(8,128)(2,1)S(1)} %copy.17), dimensions={1,2,3,4} | broadcast | bytes 3145728 | tf_op jit(solution)/shard_map/broadcast_in_dim | solution.py:276
  5.8 1.5 %collective-permute-start = (bf16[1,1040,128]{2,1,0:T(8,128)(2,1)S(1)}, bf16[1,1040,128]{2,1,0:T(8,128)(2,1)S(1)}, u32[]{:S(2)}, u32[]{:S(2)}) collective-permute-start(bf16[1,1040,128]{2,1,0:T(8,128)(2,1)S(1)} %maximum_bitcast_fusion), channel_id=1, source_target_pairs={{0,64},{32,96},{64,0},{96,32},{1,65},{33,97},{65,1},{97,33},{2,66}... | collective-permute-start | bytes 798728 | tf_op jit(solution)/shard_map/ppermute | solution.py:249
  7.3 6.8 %all-to-all-start = ((bf16[8,2,512,128]{3,2,1,0:T(8,128)(2,1)}), bf16[8,2,512,128]{3,2,1,0:T(8,128)(2,1)S(1)}, u32[]{:S(2)}, u32[]{:S(2)}) async-start(bf16[8,2,512,128]{3,2,1,0:T(8,128)(2,1)} %bitcast.38), calls=%async_computation | async-start | bytes 4194304 | tf_op jit(solution)/shard_map/all_to_all | solution.py:277
  14.1 0.7 dynamic-slice_bitcast_fusion.3
  14.7 1.5 %collective-permute-start.4 = (bf16[256,128]{1,0:T(8,128)(2,1)}, bf16[256,128]{1,0:T(8,128)(2,1)}, u32[]{:S(2)}, u32[]{:S(2)}) collective-permute-start(bf16[256,128]{1,0:T(8,128)(2,1)} %get-tuple-element.18), channel_id=1, source_target_pairs={{3,0},{0,1},{1,2},{2,3},{7,4},{4,5},{5,6},{6,7},{11,8},{8,9},{9,10... | collective-permute-start | bytes 196616 | tf_op jit(solution)/shard_map/ppermute | solution.py:254
  16.2 2.7 %collective-permute-start.3 = (bf16[256,128]{1,0:T(8,128)(2,1)}, bf16[256,128]{1,0:T(8,128)(2,1)}, u32[]{:S(2)}, u32[]{:S(2)}) collective-permute-start(bf16[256,128]{1,0:T(8,128)(2,1)} %get-tuple-element.19), channel_id=1, source_target_pairs={{2,0},{3,1},{0,2},{1,3},{6,4},{7,5},{4,6},{5,7},{10,8},{11,9},{8,1... | collective-permute-start | bytes 196616 | tf_op jit(solution)/shard_map/ppermute | solution.py:254
  18.9 1.5 %collective-permute-start.2 = (bf16[256,128]{1,0:T(8,128)(2,1)}, bf16[256,128]{1,0:T(8,128)(2,1)}, u32[]{:S(2)}, u32[]{:S(2)}) collective-permute-start(bf16[256,128]{1,0:T(8,128)(2,1)} %get-tuple-element.20), channel_id=1, source_target_pairs={{1,0},{2,1},{3,2},{0,3},{5,4},{6,5},{7,6},{4,7},{9,8},{10,9},{11,1... | collective-permute-start | bytes 196616 | tf_op jit(solution)/shard_map/ppermute | solution.py:254
  20.3 0.6 broadcast.101
  20.9 0.6 reduce.11
  21.6 0.9 pad_maximum_fusion.2
  22.5 0.6 gather_fusion
  23.1 0.8 copy.21
  24.0 17.5 %collective-permute-done.4 = bf16[256,128]{1,0:T(8,128)(2,1)} collective-permute-done((bf16[256,128]{1,0:T(8,128)(2,1)}, bf16[256,128]{1,0:T(8,128)(2,1)}, u32[]{:S(2)}, u32[]{:S(2)}) %collective-permute-start.4) | collective-permute-done | bytes 65568 | tf_op jit(solution)/shard_map/ppermute | solution.py:254
  41.5 1.0 collective-permute-done.3
  42.5 1.6 %pad_maximum_fusion.3.refs_0_ = bf16[1024,128]{1,0:T(8,128)(2,1)} fusion(bf16[256,128]{1,0:T(8,128)(2,1)} %collective-permute-done.4, bf16[256,128]{1,0:T(8,128)(2,1)} %collective-permute-done.3, bf16[256,128]{1,0:T(8,128)(2,1)} %collective-permute-done.2, bf16[256,128]{1,0:T(8,128)(2,1)S(1)} %get-tuple-element.17), kind=kLoop, calls=%fused_computation.9 | loop fusion | flops 1048576 | bytes 524288 | tf_op jit(solution)/shard_map/concatenate | solution.py:284
  44.1 1.6 %collective-permute-start.7 = (bf16[1024,128]{1,0:T(8,128)(2,1)}, bf16[1024,128]{1,0:T(8,128)(2,1)}, u32[]{:S(2)}, u32[]{:S(2)}) collective-permute-start(bf16[1024,128]{1,0:T(8,128)(2,1)} %pad_maximum_fusion.3.refs_0_), channel_id=1, source_target_pairs={{24,0},{0,8},{8,16},{16,24},{25,1},{1,9},{9,17},{17,25},{26,2},{2,... | collective-permute-start | bytes 786440 | tf_op jit(solution)/shard_map/ppermute | solution.py:254
  45.7 2.9 %collective-permute-start.6 = (bf16[1024,128]{1,0:T(8,128)(2,1)}, bf16[1024,128]{1,0:T(8,128)(2,1)}, u32[]{:S(2)}, u32[]{:S(2)}) collective-permute-start(bf16[1024,128]{1,0:T(8,128)(2,1)} %pad_maximum_fusion.3.refs_0_), channel_id=1, source_target_pairs={{16,0},{24,8},{0,16},{8,24},{17,1},{25,9},{1,17},{9,25},{18,2},{26... | collective-permute-start | bytes 786440 | tf_op jit(solution)/shard_map/ppermute | solution.py:254
  48.6 1.3 %collective-permute-start.5 = (bf16[1024,128]{1,0:T(8,128)(2,1)}, bf16[1024,128]{1,0:T(8,128)(2,1)}, u32[]{:S(2)}, u32[]{:S(2)}) collective-permute-start(bf16[1024,128]{1,0:T(8,128)(2,1)} %pad_maximum_fusion.3.refs_0_), channel_id=1, source_target_pairs={{8,0},{16,8},{24,16},{0,24},{9,1},{17,9},{25,17},{1,25},{10,2},{18... | collective-permute-start | bytes 786440 | tf_op jit(solution)/shard_map/ppermute | solution.py:254
  50.3 8.8 %page_part.1 = bf16[4,4,272,128]{3,2,1,0:T(8,128)(2,1)S(1)} custom-call(s32[24]{0:T(128)S(1)} %reshape.60.slot_ref, s32[24]{0:T(128)S(1)} %reshape_squeeze.14.req_ref, s32[24]{0:T(128)S(1)} %reshape_squeeze.15.len_ref, bf16[4,4,256,128]{3,2,1,0:T(8,128)(2,1)S(1)} %bitcast.37, bf16[2,128,512]{2,1,0:T(8,128)(2,1)S(1)} %pad.9.fresh_ref, ...), custom_call_target="tpu_custom_call" | custom-call | flops 6442450944 | bytes 8388608 | tf_op jit(solution)/shard_map/page_part/pallas_call | solution.py:190
  59.3 23.4 %prefix_part.1 = bf16[16,272,128]{2,1,0:T(8,128)(2,1)S(1)} custom-call(s32[2]{0:T(128)S(1)} %pad_add_fusion.at_ref, bf16[1024,128]{1,0:T(8,128)(2,1)} %pad_maximum_fusion.3.refs_0_, bf16[1024,128]{1,0:T(8,128)(2,1)} %collective-permute-done.5.refs_1_, bf16[1024,128]{1,0:T(8,128)(2,1)} %collective-permute-done.6.refs_2_, ...), custom_call_target="tpu_custom_call" | custom-call | flops 17179869184 | bytes 8388608 | tf_op jit(solution)/shard_map/prefix_part/pallas_call | solution.py:109
  82.7 1.0 copy-done
  83.7 5.9 %all-to-all-start.1 = ((bf16[16,272,128]{2,1,0:T(8,128)(2,1)}), bf16[16,272,128]{2,1,0:T(8,128)(2,1)S(1)}, u32[]{:S(2)}, u32[]{:S(2)}) async-start(bf16[16,272,128]{2,1,0:T(8,128)(2,1)} %copy-done), calls=%async_computation.1 | async-start | bytes 2228224 | tf_op jit(solution)/shard_map/all_to_all | solution.py:307
  89.8 1.2 %collective-permute-start.9 = (bf16[4,272,128]{2,1,0:T(8,128)(2,1)S(1)}, bf16[4,272,128]{2,1,0:T(8,128)(2,1)S(1)}, u32[]{:S(2)}, u32[]{:S(2)}) collective-permute-start(bf16[4,272,128]{2,1,0:T(8,128)(2,1)S(1)} %get-tuple-element.14), channel_id=1, source_target_pairs={{0,32},{32,0},{64,96},{96,64},{1,33},{33,1},{65,97},{97,65},{2,34}... | collective-permute-start | bytes 835592 | tf_op jit(solution)/shard_map/ppermute | solution.py:249
  91.1 2.4 %collective-permute-start.8 = (bf16[4,272,128]{2,1,0:T(8,128)(2,1)S(1)}, bf16[4,272,128]{2,1,0:T(8,128)(2,1)S(1)}, u32[]{:S(2)}, u32[]{:S(2)}) collective-permute-start(bf16[4,272,128]{2,1,0:T(8,128)(2,1)S(1)} %get-tuple-element.15), channel_id=1, source_target_pairs={{0,64},{32,96},{64,0},{96,32},{1,65},{33,97},{65,1},{97,33},{2,66}... | collective-permute-start | bytes 835592 | tf_op jit(solution)/shard_map/ppermute | solution.py:249
  93.5 6.8 %collective-permute-done.10.rest_3_ = bf16[4,272,128]{2,1,0:T(8,128)(2,1)S(1)} collective-permute-done((bf16[4,272,128]{2,1,0:T(8,128)(2,1)S(1)}, bf16[4,272,128]{2,1,0:T(8,128)(2,1)S(1)}, u32[]{:S(2)}, u32[]{:S(2)}) %collective-permute-start.10) | collective-permute-done | bytes 278560 | tf_op jit(solution)/shard_map/ppermute | solution.py:249
  100.2 4.9 %collective-permute-done.8.rest_1_ = bf16[4,272,128]{2,1,0:T(8,128)(2,1)S(1)} collective-permute-done((bf16[4,272,128]{2,1,0:T(8,128)(2,1)S(1)}, bf16[4,272,128]{2,1,0:T(8,128)(2,1)S(1)}, u32[]{:S(2)}, u32[]{:S(2)}) %collective-permute-start.8) | collective-permute-done | bytes 278560 | tf_op jit(solution)/shard_map/ppermute | solution.py:249
  105.1 2.6 %all-to-all-done.1 = bf16[16,272,128]{2,1,0:T(8,128)(2,1)S(1)} async-done(((bf16[16,272,128]{2,1,0:T(8,128)(2,1)}), bf16[16,272,128]{2,1,0:T(8,128)(2,1)S(1)}, u32[]{:S(2)}, u32[]{:S(2)}) %all-to-all-start.1) | async-done | bytes 1114144 | tf_op jit(solution)/shard_map/all_to_all | solution.py:307
  107.7 2.2 %merge.1 = bf16[16,8192]{1,0:T(8,128)(2,1)S(1)} custom-call(bf16[4,4,272,128]{3,2,1,0:T(8,128)(2,1)S(1)} %bitcast.36, bf16[4,272,128]{2,1,0:T(8,128)(2,1)S(1)} %get-tuple-element.16.rest_0_, bf16[4,272,128]{2,1,0:T(8,128)(2,1)S(1)} %collective-permute-done.8.rest_1_, bf16[4,272,128]{2,1,0:T(8,128)(2,1)S(1)} %collective-permute-done.9.rest_2_, ...), custom_call_target="tpu_custom_call" | custom-call | tf_op jit(solution)/shard_map/merge/pallas_call | solution.py:236
  109.9 0.8 reshape.69
  (40 shorter events, 1.8 us)
Async XLA Ops:
  3.5 1.8 %copy-start.1 = (bf16[4,4,8192]{2,1,0:T(4,128)(2,1)S(1)}, bf16[4,4,8192]{2,1,0:T(4,128)(2,1)}, u32[]{:S(2)}) copy-start(bf16[4,4,8192]{2,1,0:T(4,128)(2,1)} %param.8) | copy-start | bytes 786436
  5.8 15.1 %copy-start.2 = (s32[1,24]{1,0:T(1,128)S(1)}, s32[1,24]{1,0:T(1,128)}, u32[]{:S(2)}) copy-start(s32[1,24]{1,0:T(1,128)} %param.14) | copy-start | bytes 292
  5.8 16.7 %copy-start.3 = (s32[4]{0:T(128)S(1)}, s32[4]{0:T(128)}, u32[]{:S(2)}) copy-start(s32[4]{0:T(128)} %constant.76.clone) | copy-start | bytes 52
  5.8 15.8 %collective-permute-start = (bf16[1,1040,128]{2,1,0:T(8,128)(2,1)S(1)}, bf16[1,1040,128]{2,1,0:T(8,128)(2,1)S(1)}, u32[]{:S(2)}, u32[]{:S(2)}) collective-permute-start(bf16[1,1040,128]{2,1,0:T(8,128)(2,1)S(1)} %maximum_bitcast_fusion), channel_id=1, source_target_pairs={{0,64},{32,96},{64,0},{96,32},{1,65},{33,97},{65,1},{97,33},{2,66}... | collective-permute-start | bytes 798728 | tf_op jit(solution)/shard_map/ppermute | solution.py:249
  7.3 52.1 %all-to-all-start = ((bf16[8,2,512,128]{3,2,1,0:T(8,128)(2,1)}), bf16[8,2,512,128]{3,2,1,0:T(8,128)(2,1)S(1)}, u32[]{:S(2)}, u32[]{:S(2)}) async-start(bf16[8,2,512,128]{3,2,1,0:T(8,128)(2,1)} %bitcast.38), calls=%async_computation | async-start | bytes 4194304 | tf_op jit(solution)/shard_map/all_to_all | solution.py:277
  14.7 26.7 %collective-permute-start.4 = (bf16[256,128]{1,0:T(8,128)(2,1)}, bf16[256,128]{1,0:T(8,128)(2,1)}, u32[]{:S(2)}, u32[]{:S(2)}) collective-permute-start(bf16[256,128]{1,0:T(8,128)(2,1)} %get-tuple-element.18), channel_id=1, source_target_pairs={{3,0},{0,1},{1,2},{2,3},{7,4},{4,5},{5,6},{6,7},{11,8},{8,9},{9,10... | collective-permute-start | bytes 196616 | tf_op jit(solution)/shard_map/ppermute | solution.py:254
  16.2 26.3 %collective-permute-start.3 = (bf16[256,128]{1,0:T(8,128)(2,1)}, bf16[256,128]{1,0:T(8,128)(2,1)}, u32[]{:S(2)}, u32[]{:S(2)}) collective-permute-start(bf16[256,128]{1,0:T(8,128)(2,1)} %get-tuple-element.19), channel_id=1, source_target_pairs={{2,0},{3,1},{0,2},{1,3},{6,4},{7,5},{4,6},{5,7},{10,8},{11,9},{8,1... | collective-permute-start | bytes 196616 | tf_op jit(solution)/shard_map/ppermute | solution.py:254
  18.9 23.6 %collective-permute-start.2 = (bf16[256,128]{1,0:T(8,128)(2,1)}, bf16[256,128]{1,0:T(8,128)(2,1)}, u32[]{:S(2)}, u32[]{:S(2)}) collective-permute-start(bf16[256,128]{1,0:T(8,128)(2,1)} %get-tuple-element.20), channel_id=1, source_target_pairs={{1,0},{2,1},{3,2},{0,3},{5,4},{6,5},{7,6},{4,7},{9,8},{10,9},{11,1... | collective-permute-start | bytes 196616 | tf_op jit(solution)/shard_map/ppermute | solution.py:254
  22.5 27.5 %collective-permute-start.1 = (bf16[2,1040,128]{2,1,0:T(8,128)(2,1)}, bf16[2,1040,128]{2,1,0:T(8,128)(2,1)S(1)}, u32[]{:S(2)}, u32[]{:S(2)}) collective-permute-start(bf16[2,1040,128]{2,1,0:T(8,128)(2,1)} %pad_maximum_fusion.2), channel_id=1, source_target_pairs={{0,32},{32,0},{64,96},{96,64},{1,33},{33,1},{65,97},{97,65},{2,34}... | collective-permute-start | bytes 1597448 | tf_op jit(solution)/shard_map/ppermute | solution.py:249
  44.1 15.0 %collective-permute-start.7 = (bf16[1024,128]{1,0:T(8,128)(2,1)}, bf16[1024,128]{1,0:T(8,128)(2,1)}, u32[]{:S(2)}, u32[]{:S(2)}) collective-permute-start(bf16[1024,128]{1,0:T(8,128)(2,1)} %pad_maximum_fusion.3.refs_0_), channel_id=1, source_target_pairs={{24,0},{0,8},{8,16},{16,24},{25,1},{1,9},{9,17},{17,25},{26,2},{2,... | collective-permute-start | bytes 786440 | tf_op jit(solution)/shard_map/ppermute | solution.py:254
  45.7 13.6 %collective-permute-start.6 = (bf16[1024,128]{1,0:T(8,128)(2,1)}, bf16[1024,128]{1,0:T(8,128)(2,1)}, u32[]{:S(2)}, u32[]{:S(2)}) collective-permute-start(bf16[1024,128]{1,0:T(8,128)(2,1)} %pad_maximum_fusion.3.refs_0_), channel_id=1, source_target_pairs={{16,0},{24,8},{0,16},{8,24},{17,1},{25,9},{1,17},{9,25},{18,2},{26... | collective-permute-start | bytes 786440 | tf_op jit(solution)/shard_map/ppermute | solution.py:254
  48.6 10.7 %collective-permute-start.5 = (bf16[1024,128]{1,0:T(8,128)(2,1)}, bf16[1024,128]{1,0:T(8,128)(2,1)}, u32[]{:S(2)}, u32[]{:S(2)}) collective-permute-start(bf16[1024,128]{1,0:T(8,128)(2,1)} %pad_maximum_fusion.3.refs_0_), channel_id=1, source_target_pairs={{8,0},{16,8},{24,16},{0,24},{9,1},{17,9},{25,17},{1,25},{10,2},{18... | collective-permute-start | bytes 786440 | tf_op jit(solution)/shard_map/ppermute | solution.py:254
  82.7 1.0 copy-start
  83.7 24.0 %all-to-all-start.1 = ((bf16[16,272,128]{2,1,0:T(8,128)(2,1)}), bf16[16,272,128]{2,1,0:T(8,128)(2,1)S(1)}, u32[]{:S(2)}, u32[]{:S(2)}) async-start(bf16[16,272,128]{2,1,0:T(8,128)(2,1)} %copy-done), calls=%async_computation.1 | async-start | bytes 2228224 | tf_op jit(solution)/shard_map/all_to_all | solution.py:307
  89.7 10.5 %collective-permute-start.10 = (bf16[4,272,128]{2,1,0:T(8,128)(2,1)S(1)}, bf16[4,272,128]{2,1,0:T(8,128)(2,1)S(1)}, u32[]{:S(2)}, u32[]{:S(2)}) collective-permute-start(bf16[4,272,128]{2,1,0:T(8,128)(2,1)S(1)} %get-tuple-element.13), channel_id=1, source_target_pairs={{0,96},{32,64},{64,32},{96,0},{1,97},{33,65},{65,33},{97,1},{2,98}... | collective-permute-start | bytes 835592 | tf_op jit(solution)/shard_map/ppermute | solution.py:249
  89.8 10.4 %collective-permute-start.9 = (bf16[4,272,128]{2,1,0:T(8,128)(2,1)S(1)}, bf16[4,272,128]{2,1,0:T(8,128)(2,1)S(1)}, u32[]{:S(2)}, u32[]{:S(2)}) collective-permute-start(bf16[4,272,128]{2,1,0:T(8,128)(2,1)S(1)} %get-tuple-element.14), channel_id=1, source_target_pairs={{0,32},{32,0},{64,96},{96,64},{1,33},{33,1},{65,97},{97,65},{2,34}... | collective-permute-start | bytes 835592 | tf_op jit(solution)/shard_map/ppermute | solution.py:249
  91.1 14.1 %collective-permute-start.8 = (bf16[4,272,128]{2,1,0:T(8,128)(2,1)S(1)}, bf16[4,272,128]{2,1,0:T(8,128)(2,1)S(1)}, u32[]{:S(2)}, u32[]{:S(2)}) collective-permute-start(bf16[4,272,128]{2,1,0:T(8,128)(2,1)S(1)} %get-tuple-element.15), channel_id=1, source_target_pairs={{0,64},{32,96},{64,0},{96,32},{1,65},{33,97},{65,1},{97,33},{2,66}... | collective-permute-start | bytes 835592 | tf_op jit(solution)/shard_map/ppermute | solution.py:249

commit v4 on v3

v4 whole, which is shorter than its diff:
```python
import functools
import math

import jax
import jax.numpy as jnp
from jax import lax
from jax.experimental import pallas as pl
from jax.experimental.pallas import tpu as pltpu
from jax.sharding import Mesh, PartitionSpec as P

HQ = 64
KVH = 4
HD = 128
GQA = 16
STEPS = 4
PAGE = 128
MAXP = 6
REQ = 4
RS = REQ * STEPS
ROWS = RS * GQA
PACK = ROWS + 16
FLOOR = -1e29
LOWEST = -1e30
LOG2 = math.log2(math.e) / math.sqrt(HD)
AXES = ("grp", "y", "xl", "z")
F32 = jnp.float32
BF16 = jnp.bfloat16


def dot_t(a, b):
    return lax.dot_general(a, b, (((1,), (1,)), ((), ())), preferred_element_type=F32)


def split3(x):
    hi = x.astype(BF16).astype(F32)
    rest = x - hi
    mid = rest.astype(BF16).astype(F32)
    return hi, mid, rest - mid


def pack_stats(m, l):
    lane = lax.broadcasted_iota(jnp.int32, (128, 128), 1)
    row = lax.broadcasted_iota(jnp.int32, (8, 128), 0)
    parts = []
    for half in range(ROWS // 128):
        rows = slice(half * 128, half * 128 + 128)
        both = jnp.where(lane < 64, m[rows], l[rows]).T
        stats = jnp.zeros((8, 128), F32)
        for i, found in enumerate(split3(both[:8]) + split3(both[64:72])):
            stats = jnp.where(row == i, found, stats)
        parts.append(stats)
    return jnp.concatenate(parts, axis=0).astype(BF16)


def unpack_stats(packed, half):
    wide = packed.astype(F32)[half * 8 : half * 8 + 8]
    return wide[0:1] + wide[1:2] + wide[2:3], wide[3:4] + wide[4:5] + wide[5:6]


def widen(x, width):
    return jnp.concatenate([x] * (width // HD), axis=1)


def scaled(q):
    wide = q.astype(F32) * LOG2
    high = wide.astype(BF16)
    return jnp.concatenate([high, (wide - high.astype(F32)).astype(BF16)], axis=1)


def online(q, kv_ref, tile):
    m = l = o = None
    q = scaled(q)
    blocks, _, tokens, _ = kv_ref.shape
    for b in range(blocks):
        for t in range(0, tokens, tile):
            k = kv_ref[b, 0, t : t + tile, :]
            v = kv_ref[b, 1, t : t + tile, :]
            s = dot_t(q, jnp.concatenate([k, k], axis=1))
            top = jnp.broadcast_to(jnp.max(s, axis=-1, keepdims=True), (q.shape[0], HD))
            new = top if m is None else jnp.maximum(m, top)
            p = jnp.exp2(s - widen(new, tile))
            pv = jnp.dot(
                p.astype(BF16),
                jnp.concatenate([v, jnp.ones_like(v)], axis=1),
                preferred_element_type=F32,
            )
            if m is None:
                l, o = pv[:, HD:], pv[:, :HD]
            else:
                fade = jnp.exp2(m - new)
                l, o = l * fade + pv[:, HD:], o * fade + pv[:, :HD]
            m = new
    return m, l, o


def prefix_kernel(at_ref, *refs, count, tile):
    q_refs, kv_ref, out_ref, held = refs[:count], refs[count], refs[-2], refs[-1]
    i = pl.program_id(0)

    @pl.when(i == 0)
    def _():
        for n, q_ref in enumerate(q_refs):
            held[n] = q_ref[...].reshape(4 * ROWS, HD)

    m, l, o = online(held[i], kv_ref, tile)
    for n in range(4):
        part = slice(n * ROWS, (n + 1) * ROWS)
        place = lax.rem(at_ref[0] + n, 4)
        out_ref[place, :ROWS, :] = o[part].astype(BF16)
        out_ref[place, ROWS:, :] = pack_stats(m[part], l[part])


def prefix_part(at, qs, kv, first, done, tile):
    count = len(qs)
    tokens = kv.shape[0] * kv.shape[2]
    return pl.pallas_call(
        functools.partial(prefix_kernel, count=count, tile=tile),
        grid_spec=pltpu.PrefetchScalarGridSpec(
            num_scalar_prefetch=1,
            grid=(count,),
            in_specs=[pl.BlockSpec(qs[0].shape, lambda i, at: (0, 0, 0))] * count
            + [pl.BlockSpec(kv.shape, lambda i, at: (0, 0, 0, 0))]
            + [pl.BlockSpec(memory_space=pl.ANY)] * len(done),
            out_specs=pl.BlockSpec(
                (4, PACK, HD), lambda i, at: (lax.rem(at[1] + i + first, 4), 0, 0)
            ),
            scratch_shapes=[pltpu.VMEM((count, 4 * ROWS, HD), BF16)],
        ),
        out_shape=jax.ShapeDtypeStruct((16, PACK, HD), BF16),
        input_output_aliases={count + 2: 0} if done else {},
        compiler_params=pltpu.CompilerParams(vmem_limit_bytes=40 << 20),
        cost_estimate=pl.CostEstimate(
            flops=count * ROWS * tokens * HD * 32,
            bytes_accessed=8 << 20,
            transcendentals=count * ROWS * tokens * 4,
        ),
        name="prefix_part",
    )(at, *qs, kv, *done)


def prep_kernel(table_ref, size_ref, q_ref, kv_ref, asked_ref, dealt_ref):
    for c in range(GQA):
        tile = q_ref[:, :, c * HD : (c + 1) * HD].reshape(RS, HD)
        asked_ref[0, c * RS : (c + 1) * RS, :] = tile
    both = kv_ref[0].astype(F32)
    for i in range(2):
        half = both[:, i].astype(BF16)
        dealt_ref[0, 0, i] = half
        dealt_ref[1, 0, i] = half

    @pl.when(pl.program_id(0) == 0)
    def _():
        lane = lax.broadcasted_iota(jnp.int32, (16, HD), 1)
        row = lax.broadcasted_iota(jnp.int32, (16, HD), 0)
        notes = jnp.zeros((16, HD), jnp.int32)
        for slot in range(REQ * MAXP):
            req, page = divmod(slot, MAXP)
            alive = jnp.clip(size_ref[0:1, req : req + 1] - page * PAGE, 0, PAGE)
            here = jnp.where(row == 0, req, jnp.where(row == 1, alive, 0))
            notes = jnp.where(lane == table_ref[0:1, slot : slot + 1], here, notes)
        asked_ref[0, ROWS:, :] = notes.astype(F32).astype(BF16)

    @pl.when(pl.program_id(0) != 0)
    def _():
        asked_ref[0, ROWS:, :] = jnp.zeros((16, HD), BF16)


def prep(page_table, unique_len, queries, prefix_kv):
    tokens = prefix_kv.shape[1]
    return pl.pallas_call(
        prep_kernel,
        grid=(KVH,),
        in_specs=[
            pl.BlockSpec(page_table.shape, lambda k: (0, 0)),
            pl.BlockSpec((1, REQ), lambda k: (0, 0)),
            pl.BlockSpec((REQ, STEPS, GQA * HD), lambda k: (0, 0, k)),
            pl.BlockSpec((1, tokens, 2, HD), lambda k: (0, 0, 0, k)),
        ],
        out_specs=[
            pl.BlockSpec((1, PACK, HD), lambda k: (k, 0, 0)),
            pl.BlockSpec((2, 1, 2, tokens, HD), lambda k: (0, k, 0, 0, 0)),
        ],
        out_shape=[
            jax.ShapeDtypeStruct((KVH, PACK, HD), BF16),
            jax.ShapeDtypeStruct((2, KVH, 2, tokens, HD), BF16),
        ],
        compiler_params=pltpu.CompilerParams(vmem_limit_bytes=60 << 20),
        name="prep",
    )(page_table, unique_len.reshape(1, REQ), queries, prefix_kv)


def pick_kernel(at_ref, *refs):
    q_refs, out_refs = refs[:4], refs[4:]
    for k, out_ref in enumerate(out_refs):
        head = lax.rem(at_ref[1] + 4 - k, 4)
        for n, q_ref in enumerate(q_refs):
            out_ref[n] = q_ref[head, :ROWS, :]


def pick(at, asked):
    scalar = pl.BlockSpec(memory_space=pltpu.SMEM)
    whole = pl.BlockSpec(memory_space=pltpu.VMEM)
    return pl.pallas_call(
        pick_kernel,
        in_specs=[scalar] + [whole] * 4,
        out_specs=[whole] * 4,
        out_shape=[jax.ShapeDtypeStruct((4, ROWS, HD), BF16)] * 4,
        compiler_params=pltpu.CompilerParams(vmem_limit_bytes=32 << 20),
        name="pick",
    )(at, *asked)


def page_kernel(at_ref, slot_ref, *refs, first):
    q_refs, fresh_ref, pages = refs[:2], refs[2], refs[3 : 3 + MAXP]
    out_refs, (held, found) = refs[3 + MAXP : 5 + MAXP], refs[5 + MAXP :]
    t = pl.program_id(0)

    @pl.when(t == 0)
    def _():
        for n, q_ref in enumerate(q_refs):
            held[n] = q_ref[...]

    row = lax.broadcasted_iota(jnp.int32, (ROWS, PAGE), 0)
    token = lax.broadcasted_iota(jnp.int32, (ROWS, PAGE), 1)
    step = lax.rem(row, RS)
    owner = lax.div(step, STEPS)
    notes = held[t, 0, ROWS:, :].astype(F32)
    place = lax.broadcasted_iota(jnp.int32, (1, HD), 1)
    bounds = []
    for c in range(MAXP):
        here = place == at_ref[2] * MAXP + c
        req, size = (
            jnp.sum(jnp.where(here, notes[i : i + 1], 0.0), axis=1, keepdims=True).astype(jnp.int32)
            for i in range(2)
        )
        bounds.append(jnp.where(owner == req, size, 0))

    def attend(own):
        scores, vals = [], []
        for k in range(KVH):
            cols = slice(k * HD, (k + 1) * HD)
            keys = [page[0, 0, :, cols] for page in pages]
            values = [page[0, 1, :, cols] for page in pages]
            if own:
                keys.append(fresh_ref[0, :, cols])
                values.append(fresh_ref[1, :, cols])
            scores.append(dot_t(held[t, k, :ROWS, :], jnp.concatenate(keys, axis=0)))
            vals.append(jnp.concatenate(values, axis=0))
        if own:
            fresh_alive = (
                (lax.div(token, STEPS) == owner)
                & (lax.rem(token, STEPS) <= lax.rem(step, STEPS))
                & (token < RS)
            )
        weights = []
        for s in scores:
            parts = [
                jnp.where(token < bounds[c], s[:, c * PAGE : (c + 1) * PAGE], LOWEST)
                for c in range(MAXP)
            ]
            if own:
                parts.append(jnp.where(fresh_alive, s[:, MAXP * PAGE :], LOWEST))
            top = jnp.max(functools.reduce(jnp.maximum, parts), axis=-1, keepdims=True)
            m = jnp.maximum(jnp.broadcast_to(top, (ROWS, HD)), FLOOR) * LOG2
            p = [jnp.exp2(part * LOG2 - m).astype(BF16) for part in parts]
            weights.append((m, jnp.concatenate(p, axis=1)))
        for k, ((m, p), v) in enumerate(zip(weights, vals)):
            pv = jnp.dot(
                p,
                jnp.concatenate([v, jnp.ones_like(v)], axis=1),
                preferred_element_type=F32,
            )
            found[k, :ROWS, :] = pv[:, :HD].astype(BF16)
            found[k, ROWS:, :] = pack_stats(m, pv[:, HD:])

    if first:
        attend(False)
    else:

        @pl.when(t == 0)
        def _():
            attend(True)

        @pl.when(t != 0)
        def _():
            attend(False)

    for n, out_ref in enumerate(out_refs):

        @pl.when(t == n)
        def _():
            out_ref[...] = found[...]


def page_part(at, slots, asked, first, fresh, pool):
    n = len(asked)

    def page_spec(c):
        return pl.BlockSpec(
            (1, 2, PAGE, KVH * HD),
            lambda t, at, slot: (slot[0, (at[2] ^ (first + t)) * MAXP + c], 0, 0, 0),
        )

    return pl.pallas_call(
        functools.partial(page_kernel, first=first),
        grid_spec=pltpu.PrefetchScalarGridSpec(
            num_scalar_prefetch=2,
            grid=(n,),
            in_specs=[pl.BlockSpec(asked[0].shape, lambda t, at, slot: (0, 0, 0))] * n
            + [pl.BlockSpec(fresh.shape, lambda t, at, slot: (0, 0, 0))]
            + [page_spec(c) for c in range(MAXP)],
            out_specs=[pl.BlockSpec((KVH, PACK, HD), lambda t, at, slot: (0, 0, 0))] * n,
            scratch_shapes=[
                pltpu.VMEM((n, *asked[0].shape), BF16),
                pltpu.VMEM((KVH, PACK, HD), BF16),
            ],
        ),
        out_shape=[jax.ShapeDtypeStruct((KVH, PACK, HD), BF16)] * n,
        compiler_params=pltpu.CompilerParams(vmem_limit_bytes=48 << 20),
        cost_estimate=pl.CostEstimate(
            flops=n * KVH * ROWS * MAXP * PAGE * HD * 16,
            bytes_accessed=4 << 20,
            transcendentals=n * KVH * ROWS * MAXP * PAGE,
        ),
        name="page_part",
    )(at, slots, *asked, fresh, *([pool] * MAXP))


def merge_kernel(part_ref, *rest):
    page_refs, out_ref = rest[:-1], rest[-1]
    found = [part_ref.at[0, i] for i in range(part_ref.shape[1])]
    found += [ref.at[0] for ref in page_refs]
    for half in range(ROWS // 128):
        stats = [unpack_stats(ref[ROWS:, :], half) for ref in found]
        top = functools.reduce(jnp.maximum, [m for m, _ in stats])
        fades = [jnp.exp2(m - top) for m, _ in stats]
        weight_sum = functools.reduce(jnp.add, [l * f for (_, l), f in zip(stats, fades)])
        gains = jnp.concatenate(
            [f / weight_sum for f in fades] + [jnp.zeros((128 - len(fades), 128), F32)], axis=0
        ).T
        total = jnp.zeros((128, HD), F32)
        for i, ref in enumerate(found):
            gain = jnp.broadcast_to(gains[:, i : i + 1], (128, HD))
            total = total + ref[half * 128 : half * 128 + 128, :].astype(F32) * gain
        total = total.astype(BF16)
        for j in range(128 // RS):
            col = half * 128 // RS + j
            rows = total[j * RS : (j + 1) * RS].reshape(REQ, STEPS, HD)
            out_ref[:, :, col * HD : (col + 1) * HD] = rows


def merge(parts, pages):
    return pl.pallas_call(
        merge_kernel,
        grid=(KVH,),
        in_specs=[pl.BlockSpec((1, *parts.shape[1:]), lambda k: (k, 0, 0, 0))]
        + [pl.BlockSpec((1, PACK, HD), lambda k: (k, 0, 0))] * len(pages),
        out_specs=pl.BlockSpec((REQ, STEPS, GQA * HD), lambda k: (0, 0, k)),
        out_shape=jax.ShapeDtypeStruct((REQ, STEPS, HQ * HD), BF16),
        compiler_params=pltpu.CompilerParams(vmem_limit_bytes=32 << 20),
        name="merge",
    )(parts, *pages)


def swap(x, axis, mask):
    return lax.ppermute(x, axis, [(i, i ^ mask) for i in range(lax.axis_size(axis))])


def fetch(x, axis, by):
    n = lax.axis_size(axis)
    return lax.ppermute(x, axis, [((i + by) % n, i) for i in range(n)])


def after(x, *done):
    return lax.optimization_barrier((x, *done))[0]


def local(queries, prefix_kv, pool, new_kv, unique_len, page_table, send_slots):
    at = jnp.stack([lax.axis_index(name) for name in ("y", "z", "grp")])
    asked, dealt = prep(page_table, unique_len, queries, prefix_kv)
    tokens = prefix_kv.shape[1]
    dealt = dealt.reshape(2 * KVH, 2, tokens, HD)
    kv_all = lax.all_to_all(dealt, ("xl", "z"), 0, 0, tiled=True)
    chunks = [asked] + [fetch(asked, "y", k) for k in (1, 2, 3)]
    asked_1 = swap(asked, "grp", 1)
    asked_2 = swap(asked, "grp", 2)
    asked_3 = swap(asked_1, "grp", 2)
    fresh = new_kv.transpose(2, 0, 1, 3).reshape(2, RS, KVH * HD)
    fresh = jnp.pad(fresh, ((0, 0), (0, PAGE - RS), (0, 0)))
    near = page_part(at, send_slots, [asked, asked_1], 0, fresh, pool)
    mine, *sent = pick(after(at, near[0]), chunks)
    came = [fetch(x, "z", k) for k, x in enumerate(sent, 1)]
    part = prefix_part(at, [mine], kv_all, 0, [], 256)
    part = prefix_part(at, came, kv_all, 1, [part], 256)
    part = after(part, asked_2, asked_3)
    moved = lax.all_to_all(part, ("z", "y"), 0, 0, tiled=True)
    far = page_part(after(at, part), send_slots, [asked_2, asked_3], 2, fresh, pool)
    far_came = [swap(x, "grp", 2 + n) for n, x in enumerate(far)]
    pages = [near[0], swap(near[1], "grp", 1), *far_came]
    return merge(moved.reshape(KVH, 4, PACK, HD), pages)


def solution(mesh):
    fine = Mesh(mesh.devices.reshape(4, 4, 2, 4), AXES)
    every = P(AXES)
    dev = ("y", "xl", "z")
    placed = (every, P("grp", dev), every, every, every, every, every)
    return jax.shard_map(local, mesh=fine, in_specs=placed, out_specs=every, check_vma=False)
```

time: 111 us -> 101 us (0.910)
  the two profiles are of different devices: /device:TPU:6 before, /device:TPU:1 now
where the time goes in v4:
time: 101 us; the launch traced here: 100 us
  Pallas kernels  45 us (45%)
  starting transfers between devices  28.7 us (28%)
  waiting for transfers between devices  24.5 us (24%)
  local copies, waits for them, and re-layouts  1.7 us (2%)
    pallas_call x2, Pallas kernels, prefix_part(): pl.pallas_call(functools.partial(prefix_kernel, count=count, tile=tile),...  24.3 us
    ppermute x6, waiting for transfers between devices, swap(): lax.ppermute(x, axis, [(i, i ^ mask) for i in range(lax.axis_size(axis))])  12.7 us
    ppermute x6, waiting for transfers between devices, fetch(): return lax.ppermute(x, axis, [((i + by) % n, i) for i in range(n)])  11.8 us
    pallas_call x2, Pallas kernels, page_part(): pl.pallas_call(functools.partial(page_kernel, first=first), grid_spec=plt...  11.2 us
    ppermute x6, starting transfers between devices, fetch(): return lax.ppermute(x, axis, [((i + by) % n, i) for i in range(n)])  9.02 us
    ppermute x6, starting transfers between devices, swap(): lax.ppermute(x, axis, [(i, i ^ mask) for i in range(lax.axis_size(axis))])  8.34 us
    all_to_all x1, starting transfers between devices, local(): kv_all = lax.all_to_all(dealt, ('xl', 'z'), 0, 0, tiled=True)  6.93 us
    pallas_call x1, Pallas kernels, prep(): pl.pallas_call(prep_kernel, grid=(KVH,), in_specs=[pl.BlockSpec(page_tabl...  4.84 us
  transfers between devices with their start and end apart: 14, of which 4 were waited for; matrix products, arithmetic and copies ran while one was open for 0% of the time, Pallas kernels for 37%

profile of v4, /device:TPU:1, one launch (start us, length us, event | category | flops | bytes accessed | tf_op | source)
XLA Modules:
  0.0 100.1 jit_solution(10350604406104630047)
XLA Ops:
  0.0 4.8 %prep.1 = (bf16[4,272,128]{2,1,0:T(8,128)(2,1)}, bf16[2,4,2,512,128]{4,3,2,1,0:T(8,128)(2,1)}) custom-call(s32[1,24]{1,0:T(1,128)} %table_ref.1, s32[1,4]{1,0:T(1,128)} %bitcast.12, bf16[4,4,8192]{2,1,0:T(4,128)(2,1)} %q_ref.1, bf16[1,512,2,512]{3,2,1,0:T(2,128)(2,1)} %kv_ref.1), custom_call_target="tpu_custom_call" | custom-call | tf_op jit(solution)/shard_map/prep/pallas_call | solution.py:170
  4.8 0.0 copy-start.1
  4.9 6.9 %all-to-all-start = ((bf16[8,2,512,128]{3,2,1,0:T(8,128)(2,1)}), bf16[8,2,512,128]{3,2,1,0:T(8,128)(2,1)S(1)}, u32[]{:S(2)}, u32[]{:S(2)}) async-start(bf16[8,2,512,128]{3,2,1,0:T(8,128)(2,1)} %bitcast.10), calls=%async_computation | async-start | bytes 4194304 | tf_op jit(solution)/shard_map/all_to_all | solution.py:383
  11.8 1.0 %collective-permute-start = (bf16[4,272,128]{2,1,0:T(8,128)(2,1)S(1)}, bf16[4,272,128]{2,1,0:T(8,128)(2,1)}, u32[]{:S(2)}, u32[]{:S(2)}) collective-permute-start(bf16[4,272,128]{2,1,0:T(8,128)(2,1)S(1)} %copy-done), channel_id=1, source_target_pairs={{0,32},{32,0},{64,96},{96,64},{1,33},{33,1},{65,97},{97,65},{2,34}... | collective-permute-start | bytes 835592 | tf_op jit(solution)/shard_map/ppermute | solution.py:366
  12.8 2.5 %collective-permute-start.7 = (bf16[4,272,128]{2,1,0:T(8,128)(2,1)S(1)}, bf16[4,272,128]{2,1,0:T(8,128)(2,1)}, u32[]{:S(2)}, u32[]{:S(2)}) collective-permute-start(bf16[4,272,128]{2,1,0:T(8,128)(2,1)S(1)} %copy-done), channel_id=1, source_target_pairs={{0,64},{32,96},{64,0},{96,32},{1,65},{33,97},{65,1},{97,33},{2,66}... | collective-permute-start | bytes 835592 | tf_op jit(solution)/shard_map/ppermute | solution.py:366
  15.3 1.3 %collective-permute-start.3 = (bf16[4,272,128]{2,1,0:T(8,128)(2,1)S(1)}, bf16[4,272,128]{2,1,0:T(8,128)(2,1)S(1)}, u32[]{:S(2)}, u32[]{:S(2)}) collective-permute-start(bf16[4,272,128]{2,1,0:T(8,128)(2,1)S(1)} %copy-done), channel_id=1, source_target_pairs={{24,0},{0,8},{8,16},{16,24},{25,1},{1,9},{9,17},{17,25},{26,2},{2,... | collective-permute-start | bytes 835592 | tf_op jit(solution)/shard_map/ppermute | solution.py:371
  16.6 2.6 %collective-permute-start.2 = (bf16[4,272,128]{2,1,0:T(8,128)(2,1)S(1)}, bf16[4,272,128]{2,1,0:T(8,128)(2,1)S(1)}, u32[]{:S(2)}, u32[]{:S(2)}) collective-permute-start(bf16[4,272,128]{2,1,0:T(8,128)(2,1)S(1)} %copy-done), channel_id=1, source_target_pairs={{16,0},{24,8},{0,16},{8,24},{17,1},{25,9},{1,17},{9,25},{18,2},{26... | collective-permute-start | bytes 835592 | tf_op jit(solution)/shard_map/ppermute | solution.py:371
  19.2 1.1 %collective-permute-start.1 = (bf16[4,272,128]{2,1,0:T(8,128)(2,1)S(1)}, bf16[4,272,128]{2,1,0:T(8,128)(2,1)}, u32[]{:S(2)}, u32[]{:S(2)}) collective-permute-start(bf16[4,272,128]{2,1,0:T(8,128)(2,1)S(1)} %copy-done), channel_id=1, source_target_pairs={{8,0},{16,8},{24,16},{0,24},{9,1},{17,9},{25,17},{1,25},{10,2},{18... | collective-permute-start | bytes 835592 | tf_op jit(solution)/shard_map/ppermute | solution.py:371
  20.3 0.1 pad_add_fusion.at_ref
  20.4 5.9 %page_part.2 = (bf16[4,272,128]{2,1,0:T(8,128)(2,1)S(1)}, bf16[4,272,128]{2,1,0:T(8,128)(2,1)S(1)}) custom-call(s32[3]{0:T(128)S(1)} %pad_add_fusion.at_ref, s32[1,24]{1,0:T(1,128)S(1)} %copy-done.1, bf16[4,272,128]{2,1,0:T(8,128)(2,1)S(1)} %copy-done, bf16[4,272,128]{2,1,0:T(8,128)(2,1)} %collective-permute-done.refs_1_, ...), custom_call_target="tpu_custom_call" | custom-call | flops 3221225472 | bytes 4194304 | tf_op jit(solution)/shard_map/page_part/pallas_call | solution.py:304
  26.3 5.3 %collective-permute-done.2.refs_2_ = bf16[4,272,128]{2,1,0:T(8,128)(2,1)S(1)} collective-permute-done((bf16[4,272,128]{2,1,0:T(8,128)(2,1)S(1)}, bf16[4,272,128]{2,1,0:T(8,128)(2,1)S(1)}, u32[]{:S(2)}, u32[]{:S(2)}) %collective-permute-start.2) | collective-permute-done | bytes 278560 | tf_op jit(solution)/shard_map/ppermute | solution.py:371
  31.6 1.9 %pick.1 = (bf16[4,256,128]{2,1,0:T(8,128)(2,1)S(1)}, bf16[4,256,128]{2,1,0:T(8,128)(2,1)}, bf16[4,256,128]{2,1,0:T(8,128)(2,1)}, bf16[4,256,128]{2,1,0:T(8,128)(2,1)}) custom-call(s32[3]{0:T(128)S(1)} %pad_add_fusion.at_ref, bf16[4,272,128]{2,1,0:T(8,128)(2,1)S(1)} %copy-done, bf16[4,272,128]{2,1,0:T(8,128)(2,1)} %collective-permute-done.1.refs_1_, ...), custom_call_target="tpu_custom_call" | custom-call | tf_op jit(solution)/shard_map/pick/pallas_call | solution.py:203
  33.5 0.7 copy-done.4
  34.2 2.9 %collective-permute-start.4 = (bf16[4,256,128]{2,1,0:T(8,128)(2,1)}, bf16[4,256,128]{2,1,0:T(8,128)(2,1)S(1)}, u32[]{:S(2)}, u32[]{:S(2)}) collective-permute-start(bf16[4,256,128]{2,1,0:T(8,128)(2,1)} %get-tuple-element.21), channel_id=1, source_target_pairs={{1,0},{2,1},{3,2},{0,3},{5,4},{6,5},{7,6},{4,7},{9,8},{10,9},{11,1... | collective-permute-start | bytes 786440 | tf_op jit(solution)/shard_map/ppermute | solution.py:371
  37.1 0.6 collective-permute-start.5
  37.7 0.6 collective-permute-start.6
  38.2 0.5 collective-permute-start.8
  38.8 0.0 all-to-all-done.refs_1_.refs_3_
  38.8 0.9 copy-done.5
  39.7 6.5 %prefix_part.2.refs_4_ = bf16[16,272,128]{2,1,0:T(8,128)(2,1)} custom-call(s32[3]{0:T(128)S(1)} %pad_add_fusion.at_ref, bf16[4,256,128]{2,1,0:T(8,128)(2,1)S(1)} %copy-done.5, bf16[8,2,512,128]{3,2,1,0:T(8,128)(2,1)S(1)} %all-to-all-done.refs_1_.refs_3_), custom_call_target="tpu_custom_call" | custom-call | flops 4294967296 | bytes 8388608 | tf_op jit(solution)/shard_map/prefix_part/pallas_call | solution.py:116
  46.2 0.0 collective-permute-done.5.refs_1_
  46.2 6.5 %collective-permute-done.6.refs_2_ = bf16[4,256,128]{2,1,0:T(8,128)(2,1)} collective-permute-done((bf16[4,256,128]{2,1,0:T(8,128)(2,1)}, bf16[4,256,128]{2,1,0:T(8,128)(2,1)}, u32[]{:S(2)}, u32[]{:S(2)}) %collective-permute-start.6) | collective-permute-done | bytes 262176 | tf_op jit(solution)/shard_map/ppermute | solution.py:371
  52.7 17.8 %prefix_part.3 = bf16[16,272,128]{2,1,0:T(8,128)(2,1)} custom-call(s32[3]{0:T(128)S(1)} %pad_add_fusion.at_ref, bf16[4,256,128]{2,1,0:T(8,128)(2,1)S(1)} %collective-permute-done.4.refs_0_, bf16[4,256,128]{2,1,0:T(8,128)(2,1)} %collective-permute-done.5.refs_1_, bf16[4,256,128]{2,1,0:T(8,128)(2,1)} %collective-permute-done.6.refs_2_, ...), custom_call_target="tpu_custom_call", output_to_operand_aliasing={{}: (5, {})} | custom-call | flops 12884901888 | bytes 8388608 | tf_op jit(solution)/shard_map/prefix_part/pallas_call | solution.py:116
  70.6 0.0 collective-permute-done.7.refs_0_
  70.6 4.4 %all-to-all-start.1 = ((bf16[16,272,128]{2,1,0:T(8,128)(2,1)}), bf16[16,272,128]{2,1,0:T(8,128)(2,1)S(1)}, u32[]{:S(2)}, u32[]{:S(2)}) async-start(bf16[16,272,128]{2,1,0:T(8,128)(2,1)} %prefix_part.3), calls=%async_computation.1 | async-start | bytes 2228224 | tf_op jit(solution)/shard_map/all_to_all | solution.py:396
  75.0 1.1 %collective-permute-start.9 = (bf16[4,272,128]{2,1,0:T(8,128)(2,1)S(1)}, bf16[4,272,128]{2,1,0:T(8,128)(2,1)S(1)}, u32[]{:S(2)}, u32[]{:S(2)}) collective-permute-start(bf16[4,272,128]{2,1,0:T(8,128)(2,1)S(1)} %copy-done.3), channel_id=1, source_target_pairs={{0,32},{32,0},{64,96},{96,64},{1,33},{33,1},{65,97},{97,65},{2,34}... | collective-permute-start | bytes 835592 | tf_op jit(solution)/shard_map/ppermute | solution.py:366
  76.0 5.3 %page_part.3 = (bf16[4,272,128]{2,1,0:T(8,128)(2,1)S(1)}, bf16[4,272,128]{2,1,0:T(8,128)(2,1)S(1)}) custom-call(s32[3]{0:T(128)S(1)} %pad_add_fusion.at_ref, s32[1,24]{1,0:T(1,128)S(1)} %copy-done.1, bf16[4,272,128]{2,1,0:T(8,128)(2,1)} %collective-permute-done.7.refs_0_, bf16[4,272,128]{2,1,0:T(8,128)(2,1)S(1)} %collective-permute-done.8.refs_1_, ...), custom_call_target="tpu_custom_call" | custom-call | flops 3221225472 | bytes 4194304 | tf_op jit(solution)/shard_map/page_part/pallas_call | solution.py:304
  81.3 0.6 collective-permute-start.10
  81.9 2.6 %collective-permute-start.11 = (bf16[4,272,128]{2,1,0:T(8,128)(2,1)S(1)}, bf16[4,272,128]{2,1,0:T(8,128)(2,1)S(1)}, u32[]{:S(2)}, u32[]{:S(2)}) collective-permute-start(bf16[4,272,128]{2,1,0:T(8,128)(2,1)S(1)} %get-tuple-element.30), channel_id=1, source_target_pairs={{0,96},{32,64},{64,32},{96,0},{1,97},{33,65},{65,33},{97,1},{2,98}... | collective-permute-start | bytes 835592 | tf_op jit(solution)/shard_map/ppermute | solution.py:366
  84.6 6.6 %collective-permute-done.10.rest_2_ = bf16[4,272,128]{2,1,0:T(8,128)(2,1)S(1)} collective-permute-done((bf16[4,272,128]{2,1,0:T(8,128)(2,1)S(1)}, bf16[4,272,128]{2,1,0:T(8,128)(2,1)S(1)}, u32[]{:S(2)}, u32[]{:S(2)}) %collective-permute-start.10) | collective-permute-done | bytes 278560 | tf_op jit(solution)/shard_map/ppermute | solution.py:366
  91.2 6.1 %collective-permute-done.11.rest_3_ = bf16[4,272,128]{2,1,0:T(8,128)(2,1)S(1)} collective-permute-done((bf16[4,272,128]{2,1,0:T(8,128)(2,1)S(1)}, bf16[4,272,128]{2,1,0:T(8,128)(2,1)S(1)}, u32[]{:S(2)}, u32[]{:S(2)}) %collective-permute-start.11) | collective-permute-done | bytes 278560 | tf_op jit(solution)/shard_map/ppermute | solution.py:366
  97.3 2.8 %merge.1 = bf16[4,4,8192]{2,1,0:T(4,128)(2,1)} custom-call(bf16[4,4,272,128]{3,2,1,0:T(8,128)(2,1)S(1)} %bitcast.9, bf16[4,272,128]{2,1,0:T(8,128)(2,1)S(1)} %get-tuple-element.19.rest_0_, bf16[4,272,128]{2,1,0:T(8,128)(2,1)S(1)} %collective-permute-done.9.rest_1_, bf16[4,272,128]{2,1,0:T(8,128)(2,1)S(1)} %collective-permute-done.10.rest_2_, ...), custom_call_target="tpu_custom_call" | custom-call | tf_op jit(solution)/shard_map/merge/pallas_call | solution.py:353
  (20 shorter events, 0.1 us)
Async XLA Ops:
  4.8 7.0 %copy-start = (bf16[4,272,128]{2,1,0:T(8,128)(2,1)S(1)}, bf16[4,272,128]{2,1,0:T(8,128)(2,1)}, u32[]{:S(2)}) copy-start(bf16[4,272,128]{2,1,0:T(8,128)(2,1)} %get-tuple-element.18.refs_0_) | copy-start | bytes 835588
  4.8 15.4 %copy-start.6 = (bf16[4,4,2,512]{3,2,1,0:T(2,128)(2,1)S(1)}, bf16[4,4,2,512]{3,2,1,0:T(2,128)(2,1)}, u32[]{:S(2)}) copy-start(bf16[4,4,2,512]{3,2,1,0:T(2,128)(2,1)} %param.10) | copy-start | bytes 98308
  4.8 15.6 %copy-start.1 = (s32[1,24]{1,0:T(1,128)S(1)}, s32[1,24]{1,0:T(1,128)}, u32[]{:S(2)}) copy-start(s32[1,24]{1,0:T(1,128)} %slot_ref.3) | copy-start | bytes 292
  4.9 33.9 %all-to-all-start = ((bf16[8,2,512,128]{3,2,1,0:T(8,128)(2,1)}), bf16[8,2,512,128]{3,2,1,0:T(8,128)(2,1)S(1)}, u32[]{:S(2)}, u32[]{:S(2)}) async-start(bf16[8,2,512,128]{3,2,1,0:T(8,128)(2,1)} %bitcast.10), calls=%async_computation | async-start | bytes 4194304 | tf_op jit(solution)/shard_map/all_to_all | solution.py:383
  11.8 8.6 %collective-permute-start = (bf16[4,272,128]{2,1,0:T(8,128)(2,1)S(1)}, bf16[4,272,128]{2,1,0:T(8,128)(2,1)}, u32[]{:S(2)}, u32[]{:S(2)}) collective-permute-start(bf16[4,272,128]{2,1,0:T(8,128)(2,1)S(1)} %copy-done), channel_id=1, source_target_pairs={{0,32},{32,0},{64,96},{96,64},{1,33},{33,1},{65,97},{97,65},{2,34}... | collective-permute-start | bytes 835592 | tf_op jit(solution)/shard_map/ppermute | solution.py:366
  12.8 57.7 %collective-permute-start.7 = (bf16[4,272,128]{2,1,0:T(8,128)(2,1)S(1)}, bf16[4,272,128]{2,1,0:T(8,128)(2,1)}, u32[]{:S(2)}, u32[]{:S(2)}) collective-permute-start(bf16[4,272,128]{2,1,0:T(8,128)(2,1)S(1)} %copy-done), channel_id=1, source_target_pairs={{0,64},{32,96},{64,0},{96,32},{1,65},{33,97},{65,1},{97,33},{2,66}... | collective-permute-start | bytes 835592 | tf_op jit(solution)/shard_map/ppermute | solution.py:366
  15.3 11.0 %collective-permute-start.3 = (bf16[4,272,128]{2,1,0:T(8,128)(2,1)S(1)}, bf16[4,272,128]{2,1,0:T(8,128)(2,1)S(1)}, u32[]{:S(2)}, u32[]{:S(2)}) collective-permute-start(bf16[4,272,128]{2,1,0:T(8,128)(2,1)S(1)} %copy-done), channel_id=1, source_target_pairs={{24,0},{0,8},{8,16},{16,24},{25,1},{1,9},{9,17},{17,25},{26,2},{2,... | collective-permute-start | bytes 835592 | tf_op jit(solution)/shard_map/ppermute | solution.py:371
  16.6 15.0 %collective-permute-start.2 = (bf16[4,272,128]{2,1,0:T(8,128)(2,1)S(1)}, bf16[4,272,128]{2,1,0:T(8,128)(2,1)S(1)}, u32[]{:S(2)}, u32[]{:S(2)}) collective-permute-start(bf16[4,272,128]{2,1,0:T(8,128)(2,1)S(1)} %copy-done), channel_id=1, source_target_pairs={{16,0},{24,8},{0,16},{8,24},{17,1},{25,9},{1,17},{9,25},{18,2},{26... | collective-permute-start | bytes 835592 | tf_op jit(solution)/shard_map/ppermute | solution.py:371
  19.2 12.4 %collective-permute-start.1 = (bf16[4,272,128]{2,1,0:T(8,128)(2,1)S(1)}, bf16[4,272,128]{2,1,0:T(8,128)(2,1)}, u32[]{:S(2)}, u32[]{:S(2)}) collective-permute-start(bf16[4,272,128]{2,1,0:T(8,128)(2,1)S(1)} %copy-done), channel_id=1, source_target_pairs={{8,0},{16,8},{24,16},{0,24},{9,1},{17,9},{25,17},{1,25},{10,2},{18... | collective-permute-start | bytes 835592 | tf_op jit(solution)/shard_map/ppermute | solution.py:371
  26.3 11.9 %copy-start.2 = (bf16[4,272,128]{2,1,0:T(8,128)(2,1)}, bf16[4,272,128]{2,1,0:T(8,128)(2,1)S(1)}, u32[]{:S(2)}) copy-start(bf16[4,272,128]{2,1,0:T(8,128)(2,1)S(1)} %get-tuple-element.27) | copy-start | bytes 835588
  33.5 0.7 copy-start.4
  34.2 12.0 %collective-permute-start.4 = (bf16[4,256,128]{2,1,0:T(8,128)(2,1)}, bf16[4,256,128]{2,1,0:T(8,128)(2,1)S(1)}, u32[]{:S(2)}, u32[]{:S(2)}) collective-permute-start(bf16[4,256,128]{2,1,0:T(8,128)(2,1)} %get-tuple-element.21), channel_id=1, source_target_pairs={{1,0},{2,1},{3,2},{0,3},{5,4},{6,5},{7,6},{4,7},{9,8},{10,9},{11,1... | collective-permute-start | bytes 786440 | tf_op jit(solution)/shard_map/ppermute | solution.py:371
  37.1 9.1 %collective-permute-start.5 = (bf16[4,256,128]{2,1,0:T(8,128)(2,1)}, bf16[4,256,128]{2,1,0:T(8,128)(2,1)}, u32[]{:S(2)}, u32[]{:S(2)}) collective-permute-start(bf16[4,256,128]{2,1,0:T(8,128)(2,1)} %get-tuple-element.22), channel_id=1, source_target_pairs={{2,0},{3,1},{0,2},{1,3},{6,4},{7,5},{4,6},{5,7},{10,8},{11,9},{8,1... | collective-permute-start | bytes 786440 | tf_op jit(solution)/shard_map/ppermute | solution.py:371
  37.7 15.1 %collective-permute-start.6 = (bf16[4,256,128]{2,1,0:T(8,128)(2,1)}, bf16[4,256,128]{2,1,0:T(8,128)(2,1)}, u32[]{:S(2)}, u32[]{:S(2)}) collective-permute-start(bf16[4,256,128]{2,1,0:T(8,128)(2,1)} %get-tuple-element.23), channel_id=1, source_target_pairs={{3,0},{0,1},{1,2},{2,3},{7,4},{4,5},{5,6},{6,7},{11,8},{8,9},{9,10... | collective-permute-start | bytes 786440 | tf_op jit(solution)/shard_map/ppermute | solution.py:371
  38.2 32.3 %collective-permute-start.8 = (bf16[4,272,128]{2,1,0:T(8,128)(2,1)}, bf16[4,272,128]{2,1,0:T(8,128)(2,1)S(1)}, u32[]{:S(2)}, u32[]{:S(2)}) collective-permute-start(bf16[4,272,128]{2,1,0:T(8,128)(2,1)} %collective-permute-done.refs_1_), channel_id=1, source_target_pairs={{0,64},{32,96},{64,0},{96,32},{1,65},{33,97},{65,1},{97,33},{2,66}... | collective-permute-start | bytes 835592 | tf_op jit(solution)/shard_map/ppermute | solution.py:366
  38.8 1.0 copy-start.5
  70.6 4.4 %copy-start.3 = (bf16[4,272,128]{2,1,0:T(8,128)(2,1)S(1)}, bf16[4,272,128]{2,1,0:T(8,128)(2,1)}, u32[]{:S(2)}) copy-start(bf16[4,272,128]{2,1,0:T(8,128)(2,1)} %copy-done.2) | copy-start | bytes 835588
  70.6 26.7 %all-to-all-start.1 = ((bf16[16,272,128]{2,1,0:T(8,128)(2,1)}), bf16[16,272,128]{2,1,0:T(8,128)(2,1)S(1)}, u32[]{:S(2)}, u32[]{:S(2)}) async-start(bf16[16,272,128]{2,1,0:T(8,128)(2,1)} %prefix_part.3), calls=%async_computation.1 | async-start | bytes 2228224 | tf_op jit(solution)/shard_map/all_to_all | solution.py:396
  75.0 9.6 %collective-permute-start.9 = (bf16[4,272,128]{2,1,0:T(8,128)(2,1)S(1)}, bf16[4,272,128]{2,1,0:T(8,128)(2,1)S(1)}, u32[]{:S(2)}, u32[]{:S(2)}) collective-permute-start(bf16[4,272,128]{2,1,0:T(8,128)(2,1)S(1)} %copy-done.3), channel_id=1, source_target_pairs={{0,32},{32,0},{64,96},{96,64},{1,33},{33,1},{65,97},{97,65},{2,34}... | collective-permute-start | bytes 835592 | tf_op jit(solution)/shard_map/ppermute | solution.py:366
  81.3 9.8 %collective-permute-start.10 = (bf16[4,272,128]{2,1,0:T(8,128)(2,1)S(1)}, bf16[4,272,128]{2,1,0:T(8,128)(2,1)S(1)}, u32[]{:S(2)}, u32[]{:S(2)}) collective-permute-start(bf16[4,272,128]{2,1,0:T(8,128)(2,1)S(1)} %get-tuple-element.29), channel_id=1, source_target_pairs={{0,64},{32,96},{64,0},{96,32},{1,65},{33,97},{65,1},{97,33},{2,66}... | collective-permute-start | bytes 835592 | tf_op jit(solution)/shard_map/ppermute | solution.py:366
  81.9 15.3 %collective-permute-start.11 = (bf16[4,272,128]{2,1,0:T(8,128)(2,1)S(1)}, bf16[4,272,128]{2,1,0:T(8,128)(2,1)S(1)}, u32[]{:S(2)}, u32[]{:S(2)}) collective-permute-start(bf16[4,272,128]{2,1,0:T(8,128)(2,1)S(1)} %get-tuple-element.30), channel_id=1, source_target_pairs={{0,96},{32,64},{64,32},{96,0},{1,97},{33,65},{65,33},{97,1},{2,98}... | collective-permute-start | bytes 835592 | tf_op jit(solution)/shard_map/ppermute | solution.py:366

commit v5 on v4

--- a/solution.py
+++ b/solution.py
@@ -128,7 +128,7 @@
         ),
         out_shape=jax.ShapeDtypeStruct((16, PACK, HD), BF16),
         input_output_aliases={count + 2: 0} if done else {},
-        compiler_params=pltpu.CompilerParams(vmem_limit_bytes=40 << 20),
+        compiler_params=pltpu.CompilerParams(vmem_limit_bytes=48 << 20),
         cost_estimate=pl.CostEstimate(
             flops=count * ROWS * tokens * HD * 32,
             bytes_accessed=8 << 20,
@@ -211,8 +211,9 @@
 
 
 def page_kernel(at_ref, slot_ref, *refs, first):
-    q_refs, fresh_ref, pages = refs[:2], refs[2], refs[3 : 3 + MAXP]
-    out_refs, (held, found) = refs[3 + MAXP : 5 + MAXP], refs[5 + MAXP :]
+    count = (len(refs) - MAXP - 3) // 2
+    q_refs, fresh_ref, pages = refs[:count], refs[count], refs[count + 1 : count + 1 + MAXP]
+    out_refs, (held, found) = refs[count + 1 + MAXP : -2], refs[-2:]
     t = pl.program_id(0)
 
     @pl.when(t == 0)
@@ -318,7 +319,7 @@
         out_shape=[jax.ShapeDtypeStruct((KVH, PACK, HD), BF16)] * n,
         compiler_params=pltpu.CompilerParams(vmem_limit_bytes=48 << 20),
         cost_estimate=pl.CostEstimate(
-            flops=n * KVH * ROWS * MAXP * PAGE * HD * 16,
+            flops=n * KVH * ROWS * MAXP * PAGE * HD * 64,
             bytes_accessed=4 << 20,
             transcendentals=n * KVH * ROWS * MAXP * PAGE,
         ),
@@ -383,21 +384,22 @@
     kv_all = lax.all_to_all(dealt, ("xl", "z"), 0, 0, tiled=True)
     chunks = [asked] + [fetch(asked, "y", k) for k in (1, 2, 3)]
     asked_1 = swap(asked, "grp", 1)
-    asked_2 = swap(asked, "grp", 2)
-    asked_3 = swap(asked_1, "grp", 2)
     fresh = new_kv.transpose(2, 0, 1, 3).reshape(2, RS, KVH * HD)
     fresh = jnp.pad(fresh, ((0, 0), (0, PAGE - RS), (0, 0)))
     near = page_part(at, send_slots, [asked, asked_1], 0, fresh, pool)
     mine, *sent = pick(after(at, near[0]), chunks)
     came = [fetch(x, "z", k) for k, x in enumerate(sent, 1)]
+    asked_2 = swap(after(asked, mine), "grp", 2)
+    asked_3 = swap(after(asked_1, mine), "grp", 2)
     part = prefix_part(at, [mine], kv_all, 0, [], 256)
     part = prefix_part(at, came, kv_all, 1, [part], 256)
     part = after(part, asked_2, asked_3)
     moved = lax.all_to_all(part, ("z", "y"), 0, 0, tiled=True)
-    far = page_part(after(at, part), send_slots, [asked_2, asked_3], 2, fresh, pool)
-    far_came = [swap(x, "grp", 2 + n) for n, x in enumerate(far)]
-    pages = [near[0], swap(near[1], "grp", 1), *far_came]
-    return merge(moved.reshape(KVH, 4, PACK, HD), pages)
+    late = after(at, part)
+    (page_2,) = page_part(late, send_slots, [asked_2], 2, fresh, pool)
+    (page_3,) = page_part(late, send_slots, [asked_3], 3, fresh, pool)
+    found = [near[0], swap(near[1], "grp", 1), swap(page_3, "grp", 3), swap(page_2, "grp", 2)]
+    return merge(moved.reshape(KVH, 4, PACK, HD), found)
 
 
 def solution(mesh):

time: 101 us -> 97 us (0.960)
  waiting for transfers between devices: 24.5 us -> 15.6 us
  Pallas kernels: 45 us -> 47.2 us
  local copies, waits for them, and re-layouts: 1.7 us -> 3.34 us
  starting transfers between devices: 28.7 us -> 30.2 us
    ppermute x6, waiting for transfers between devices: 11.8 us -> 6.16 us  [fetch(): return lax.ppermute(x, axis, [((i + by) % n, i) for i in range(n)])]
    ppermute x6, waiting for transfers between devices: 12.7 us -> 9.43 us  [swap(): lax.ppermute(x, axis, [(i, i ^ mask) for i in range(lax.axis_size(axis))])]
    pallas_call x2 -> x3, Pallas kernels: 11.2 us -> 13.3 us  [page_part(): pl.pallas_call(functools.partial(page_kernel, first=first), grid_spec=plt...]
    unnamed x14, local copies, waits for them, and re-layouts: 1.67 us -> 3.32 us
    ppermute x6, starting transfers between devices: 8.34 us -> 9.81 us  [swap(): lax.ppermute(x, axis, [(i, i ^ mask) for i in range(lax.axis_size(axis))])]
  transfers between devices with their start and end apart: 14 -> 14, of which waited for: 4 -> 4; matrix products, arithmetic and copies ran while one was open for 0% -> 0% of each run, Pallas kernels for 37% -> 41%
where the time goes in v5:
time: 97 us; the launch traced here: 96.5 us
  Pallas kernels  47.2 us (49%)
  starting transfers between devices  30.2 us (31%)
  waiting for transfers between devices  15.6 us (16%)
  local copies, waits for them, and re-layouts  3.34 us (3%)
    pallas_call x2, Pallas kernels, prefix_part(): pl.pallas_call(functools.partial(prefix_kernel, count=count, tile=tile),...  24.3 us
    pallas_call x3, Pallas kernels, page_part(): pl.pallas_call(functools.partial(page_kernel, first=first), grid_spec=plt...  13.3 us
    ppermute x6, starting transfers between devices, swap(): lax.ppermute(x, axis, [(i, i ^ mask) for i in range(lax.axis_size(axis))])  9.81 us
    ppermute x6, waiting for transfers between devices, swap(): lax.ppermute(x, axis, [(i, i ^ mask) for i in range(lax.axis_size(axis))])  9.43 us
    ppermute x6, starting transfers between devices, fetch(): return lax.ppermute(x, axis, [((i + by) % n, i) for i in range(n)])  9 us
    all_to_all x1, starting transfers between devices, local(): kv_all = lax.all_to_all(dealt, ('xl', 'z'), 0, 0, tiled=True)  6.93 us
    ppermute x6, waiting for transfers between devices, fetch(): return lax.ppermute(x, axis, [((i + by) % n, i) for i in range(n)])  6.16 us
    pallas_call x1, Pallas kernels, prep(): pl.pallas_call(prep_kernel, grid=(KVH,), in_specs=[pl.BlockSpec(page_tabl...  4.82 us
  transfers between devices with their start and end apart: 14, of which 4 were waited for; matrix products, arithmetic and copies ran while one was open for 0% of the time, Pallas kernels for 41%

profile of v5, /device:TPU:1, one launch (start us, length us, event | category | flops | bytes accessed | tf_op | source)
XLA Modules:
  0.0 96.5 jit_solution(6846330896647003385)
XLA Ops:
  0.0 4.8 %prep.1 = (bf16[4,272,128]{2,1,0:T(8,128)(2,1)}, bf16[2,4,2,512,128]{4,3,2,1,0:T(8,128)(2,1)}) custom-call(s32[1,24]{1,0:T(1,128)} %table_ref.1, s32[1,4]{1,0:T(1,128)} %bitcast.12, bf16[4,4,8192]{2,1,0:T(4,128)(2,1)} %q_ref.1, bf16[1,512,2,512]{3,2,1,0:T(2,128)(2,1)} %kv_ref.1), custom_call_target="tpu_custom_call" | custom-call | tf_op jit(solution)/shard_map/prep/pallas_call | solution.py:170
  4.8 0.0 copy-start.1
  4.8 6.9 %all-to-all-start = ((bf16[8,2,512,128]{3,2,1,0:T(8,128)(2,1)}), bf16[8,2,512,128]{3,2,1,0:T(8,128)(2,1)S(1)}, u32[]{:S(2)}, u32[]{:S(2)}) async-start(bf16[8,2,512,128]{3,2,1,0:T(8,128)(2,1)} %bitcast.10), calls=%async_computation | async-start | bytes 4194304 | tf_op jit(solution)/shard_map/all_to_all | solution.py:384
  11.8 1.0 %collective-permute-start = (bf16[4,272,128]{2,1,0:T(8,128)(2,1)S(1)}, bf16[4,272,128]{2,1,0:T(8,128)(2,1)}, u32[]{:S(2)}, u32[]{:S(2)}) collective-permute-start(bf16[4,272,128]{2,1,0:T(8,128)(2,1)S(1)} %copy-done), channel_id=1, source_target_pairs={{0,32},{32,0},{64,96},{96,64},{1,33},{33,1},{65,97},{97,65},{2,34}... | collective-permute-start | bytes 835592 | tf_op jit(solution)/shard_map/ppermute | solution.py:367
  12.8 1.3 %collective-permute-start.3 = (bf16[4,272,128]{2,1,0:T(8,128)(2,1)S(1)}, bf16[4,272,128]{2,1,0:T(8,128)(2,1)S(1)}, u32[]{:S(2)}, u32[]{:S(2)}) collective-permute-start(bf16[4,272,128]{2,1,0:T(8,128)(2,1)S(1)} %copy-done), channel_id=1, source_target_pairs={{24,0},{0,8},{8,16},{16,24},{25,1},{1,9},{9,17},{17,25},{26,2},{2,... | collective-permute-start | bytes 835592 | tf_op jit(solution)/shard_map/ppermute | solution.py:372
  14.1 2.6 %collective-permute-start.2 = (bf16[4,272,128]{2,1,0:T(8,128)(2,1)S(1)}, bf16[4,272,128]{2,1,0:T(8,128)(2,1)S(1)}, u32[]{:S(2)}, u32[]{:S(2)}) collective-permute-start(bf16[4,272,128]{2,1,0:T(8,128)(2,1)S(1)} %copy-done), channel_id=1, source_target_pairs={{16,0},{24,8},{0,16},{8,24},{17,1},{25,9},{1,17},{9,25},{18,2},{26... | collective-permute-start | bytes 835592 | tf_op jit(solution)/shard_map/ppermute | solution.py:372
  16.8 1.1 %collective-permute-start.1 = (bf16[4,272,128]{2,1,0:T(8,128)(2,1)S(1)}, bf16[4,272,128]{2,1,0:T(8,128)(2,1)}, u32[]{:S(2)}, u32[]{:S(2)}) collective-permute-start(bf16[4,272,128]{2,1,0:T(8,128)(2,1)S(1)} %copy-done), channel_id=1, source_target_pairs={{8,0},{16,8},{24,16},{0,24},{9,1},{17,9},{25,17},{1,25},{10,2},{18... | collective-permute-start | bytes 835592 | tf_op jit(solution)/shard_map/ppermute | solution.py:372
  17.9 0.1 pad_add_fusion.at_ref
  17.9 6.5 %page_part.3 = (bf16[4,272,128]{2,1,0:T(8,128)(2,1)S(1)}, bf16[4,272,128]{2,1,0:T(8,128)(2,1)}) custom-call(s32[3]{0:T(128)S(1)} %pad_add_fusion.at_ref, s32[1,24]{1,0:T(1,128)S(1)} %copy-done.1, bf16[4,272,128]{2,1,0:T(8,128)(2,1)S(1)} %copy-done, bf16[4,272,128]{2,1,0:T(8,128)(2,1)} %collective-permute-done.refs_1_, ...), custom_call_target="tpu_custom_call" | custom-call | flops 12884901888 | bytes 4194304 | tf_op jit(solution)/shard_map/page_part/pallas_call | solution.py:305
  24.5 5.0 %collective-permute-done.2.refs_2_ = bf16[4,272,128]{2,1,0:T(8,128)(2,1)S(1)} collective-permute-done((bf16[4,272,128]{2,1,0:T(8,128)(2,1)S(1)}, bf16[4,272,128]{2,1,0:T(8,128)(2,1)S(1)}, u32[]{:S(2)}, u32[]{:S(2)}) %collective-permute-start.2) | collective-permute-done | bytes 278560 | tf_op jit(solution)/shard_map/ppermute | solution.py:372
  29.5 1.9 %pick.1 = (bf16[4,256,128]{2,1,0:T(8,128)(2,1)S(1)}, bf16[4,256,128]{2,1,0:T(8,128)(2,1)}, bf16[4,256,128]{2,1,0:T(8,128)(2,1)}, bf16[4,256,128]{2,1,0:T(8,128)(2,1)}) custom-call(s32[3]{0:T(128)S(1)} %pad_add_fusion.at_ref, bf16[4,272,128]{2,1,0:T(8,128)(2,1)S(1)} %copy-done, bf16[4,272,128]{2,1,0:T(8,128)(2,1)} %collective-permute-done.1.refs_1_, ...), custom_call_target="tpu_custom_call" | custom-call | tf_op jit(solution)/shard_map/pick/pallas_call | solution.py:203
  31.4 0.7 copy-done.4
  32.1 2.9 %collective-permute-start.4 = (bf16[4,256,128]{2,1,0:T(8,128)(2,1)}, bf16[4,256,128]{2,1,0:T(8,128)(2,1)S(1)}, u32[]{:S(2)}, u32[]{:S(2)}) collective-permute-start(bf16[4,256,128]{2,1,0:T(8,128)(2,1)} %get-tuple-element.21), channel_id=1, source_target_pairs={{1,0},{2,1},{3,2},{0,3},{5,4},{6,5},{7,6},{4,7},{9,8},{10,9},{11,1... | collective-permute-start | bytes 786440 | tf_op jit(solution)/shard_map/ppermute | solution.py:372
  34.9 0.6 collective-permute-start.5
  35.5 0.6 collective-permute-start.6
  36.1 2.5 %collective-permute-start.7 = (bf16[4,272,128]{2,1,0:T(8,128)(2,1)S(1)}, bf16[4,272,128]{2,1,0:T(8,128)(2,1)S(1)}, u32[]{:S(2)}, u32[]{:S(2)}) collective-permute-start(bf16[4,272,128]{2,1,0:T(8,128)(2,1)S(1)} %copy-done), channel_id=1, source_target_pairs={{0,64},{32,96},{64,0},{96,32},{1,65},{33,97},{65,1},{97,33},{2,66}... | collective-permute-start | bytes 835592 | tf_op jit(solution)/shard_map/ppermute | solution.py:367
  38.5 0.5 collective-permute-start.8
  39.1 0.9 copy-done.5
  40.0 6.5 %prefix_part.2.refs_4_ = bf16[16,272,128]{2,1,0:T(8,128)(2,1)} custom-call(s32[3]{0:T(128)S(1)} %pad_add_fusion.at_ref, bf16[4,256,128]{2,1,0:T(8,128)(2,1)S(1)} %copy-done.5, bf16[8,2,512,128]{3,2,1,0:T(8,128)(2,1)S(1)} %all-to-all-done.refs_1_.refs_3_), custom_call_target="tpu_custom_call" | custom-call | flops 4294967296 | bytes 8388608 | tf_op jit(solution)/shard_map/prefix_part/pallas_call | solution.py:116
  46.5 0.7 copy-done.2
  47.2 2.3 %collective-permute-start.9 = (bf16[4,272,128]{2,1,0:T(8,128)(2,1)}, bf16[4,272,128]{2,1,0:T(8,128)(2,1)S(1)}, u32[]{:S(2)}, u32[]{:S(2)}) collective-permute-start(bf16[4,272,128]{2,1,0:T(8,128)(2,1)} %get-tuple-element.29), channel_id=1, source_target_pairs={{0,32},{32,0},{64,96},{96,64},{1,33},{33,1},{65,97},{97,65},{2,34}... | collective-permute-start | bytes 835592 | tf_op jit(solution)/shard_map/ppermute | solution.py:367
  49.4 1.1 %collective-permute-done.6.refs_2_ = bf16[4,256,128]{2,1,0:T(8,128)(2,1)} collective-permute-done((bf16[4,256,128]{2,1,0:T(8,128)(2,1)}, bf16[4,256,128]{2,1,0:T(8,128)(2,1)}, u32[]{:S(2)}, u32[]{:S(2)}) %collective-permute-start.6) | collective-permute-done | bytes 262176 | tf_op jit(solution)/shard_map/ppermute | solution.py:372
  50.6 0.9 copy-done.3
  51.5 17.8 %prefix_part.3 = bf16[16,272,128]{2,1,0:T(8,128)(2,1)} custom-call(s32[3]{0:T(128)S(1)} %pad_add_fusion.at_ref, bf16[4,256,128]{2,1,0:T(8,128)(2,1)S(1)} %copy-done.3, bf16[4,256,128]{2,1,0:T(8,128)(2,1)} %collective-permute-done.5.refs_1_, bf16[4,256,128]{2,1,0:T(8,128)(2,1)} %collective-permute-done.6.refs_2_, ...), custom_call_target="tpu_custom_call", output_to_operand_aliasing={{}: (5, {})} | custom-call | flops 12884901888 | bytes 8388608 | tf_op jit(solution)/shard_map/prefix_part/pallas_call | solution.py:116
  69.3 4.5 %all-to-all-start.1 = ((bf16[16,272,128]{2,1,0:T(8,128)(2,1)}), bf16[16,272,128]{2,1,0:T(8,128)(2,1)S(1)}, u32[]{:S(2)}, u32[]{:S(2)}) async-start(bf16[16,272,128]{2,1,0:T(8,128)(2,1)} %prefix_part.3), calls=%async_computation.1 | async-start | bytes 2228224 | tf_op jit(solution)/shard_map/all_to_all | solution.py:397
  73.8 3.5 %page_part.4 = bf16[4,272,128]{2,1,0:T(8,128)(2,1)S(1)} custom-call(s32[3]{0:T(128)S(1)} %pad_add_fusion.at_ref, s32[1,24]{1,0:T(1,128)S(1)} %copy-done.1, bf16[4,272,128]{2,1,0:T(8,128)(2,1)} %collective-permute-done.8.refs_0_, bf16[2,128,512]{2,1,0:T(8,128)(2,1)S(1)} %pad.4.refs_2_.refs_1_, bf16[24,2,128,512]{3,2,1,0:T(8,128)(2,1)} %refs_7_.5, ...), custom_call_target="tpu_custom_call" | custom-call | flops 6442450944 | bytes 4194304 | tf_op jit(solution)/shard_map/page_part/pallas_call | solution.py:305
  77.3 2.9 %collective-permute-start.10 = (bf16[4,272,128]{2,1,0:T(8,128)(2,1)S(1)}, bf16[4,272,128]{2,1,0:T(8,128)(2,1)S(1)}, u32[]{:S(2)}, u32[]{:S(2)}) collective-permute-start(bf16[4,272,128]{2,1,0:T(8,128)(2,1)S(1)} %page_part.4), channel_id=1, source_target_pairs={{0,96},{32,64},{64,32},{96,0},{1,97},{33,65},{65,33},{97,1},{2,98}... | collective-permute-start | bytes 835592 | tf_op jit(solution)/shard_map/ppermute | solution.py:367
  80.2 3.4 %page_part.5 = bf16[4,272,128]{2,1,0:T(8,128)(2,1)S(1)} custom-call(s32[3]{0:T(128)S(1)} %pad_add_fusion.at_ref, s32[1,24]{1,0:T(1,128)S(1)} %copy-done.1, bf16[4,272,128]{2,1,0:T(8,128)(2,1)S(1)} %collective-permute-done.7.refs_0_, bf16[2,128,512]{2,1,0:T(8,128)(2,1)S(1)} %pad.4.refs_2_.refs_1_, bf16[24,2,128,512]{3,2,1,0:T(8,128)(2,1)} %refs_7_.5, ...), custom_call_target="tpu_custom_call" | custom-call | flops 6442450944 | bytes 4194304 | tf_op jit(solution)/shard_map/page_part/pallas_call | solution.py:305
  83.6 0.6 collective-permute-start.11
  84.2 3.8 %collective-permute-done.10.rest_2_ = bf16[4,272,128]{2,1,0:T(8,128)(2,1)S(1)} collective-permute-done((bf16[4,272,128]{2,1,0:T(8,128)(2,1)S(1)}, bf16[4,272,128]{2,1,0:T(8,128)(2,1)S(1)}, u32[]{:S(2)}, u32[]{:S(2)}) %collective-permute-start.10) | collective-permute-done | bytes 278560 | tf_op jit(solution)/shard_map/ppermute | solution.py:367
  88.0 5.7 %collective-permute-done.11.rest_3_ = bf16[4,272,128]{2,1,0:T(8,128)(2,1)S(1)} collective-permute-done((bf16[4,272,128]{2,1,0:T(8,128)(2,1)S(1)}, bf16[4,272,128]{2,1,0:T(8,128)(2,1)S(1)}, u32[]{:S(2)}, u32[]{:S(2)}) %collective-permute-start.11) | collective-permute-done | bytes 278560 | tf_op jit(solution)/shard_map/ppermute | solution.py:367
  93.6 2.8 %merge.1 = bf16[4,4,8192]{2,1,0:T(4,128)(2,1)} custom-call(bf16[4,4,272,128]{3,2,1,0:T(8,128)(2,1)S(1)} %bitcast.9, bf16[4,272,128]{2,1,0:T(8,128)(2,1)S(1)} %get-tuple-element.19.rest_0_, bf16[4,272,128]{2,1,0:T(8,128)(2,1)S(1)} %collective-permute-done.9.rest_1_, bf16[4,272,128]{2,1,0:T(8,128)(2,1)S(1)} %collective-permute-done.10.rest_2_, ...), custom_call_target="tpu_custom_call" | custom-call | tf_op jit(solution)/shard_map/merge/pallas_call | solution.py:354
  (21 shorter events, 0.1 us)
Async XLA Ops:
  4.8 7.0 %copy-start = (bf16[4,272,128]{2,1,0:T(8,128)(2,1)S(1)}, bf16[4,272,128]{2,1,0:T(8,128)(2,1)}, u32[]{:S(2)}) copy-start(bf16[4,272,128]{2,1,0:T(8,128)(2,1)} %get-tuple-element.26.refs_0_) | copy-start | bytes 835588
  4.8 13.0 %copy-start.6 = (bf16[4,4,2,512]{3,2,1,0:T(2,128)(2,1)S(1)}, bf16[4,4,2,512]{3,2,1,0:T(2,128)(2,1)}, u32[]{:S(2)}) copy-start(bf16[4,4,2,512]{3,2,1,0:T(2,128)(2,1)} %param.10) | copy-start | bytes 98308
  4.8 13.1 %copy-start.1 = (s32[1,24]{1,0:T(1,128)S(1)}, s32[1,24]{1,0:T(1,128)}, u32[]{:S(2)}) copy-start(s32[1,24]{1,0:T(1,128)} %slot_ref.5) | copy-start | bytes 292
  4.8 34.2 %all-to-all-start = ((bf16[8,2,512,128]{3,2,1,0:T(8,128)(2,1)}), bf16[8,2,512,128]{3,2,1,0:T(8,128)(2,1)S(1)}, u32[]{:S(2)}, u32[]{:S(2)}) async-start(bf16[8,2,512,128]{3,2,1,0:T(8,128)(2,1)} %bitcast.10), calls=%async_computation | async-start | bytes 4194304 | tf_op jit(solution)/shard_map/all_to_all | solution.py:384
  11.8 6.2 %collective-permute-start = (bf16[4,272,128]{2,1,0:T(8,128)(2,1)S(1)}, bf16[4,272,128]{2,1,0:T(8,128)(2,1)}, u32[]{:S(2)}, u32[]{:S(2)}) collective-permute-start(bf16[4,272,128]{2,1,0:T(8,128)(2,1)S(1)} %copy-done), channel_id=1, source_target_pairs={{0,32},{32,0},{64,96},{96,64},{1,33},{33,1},{65,97},{97,65},{2,34}... | collective-permute-start | bytes 835592 | tf_op jit(solution)/shard_map/ppermute | solution.py:367
  12.8 11.6 %collective-permute-start.3 = (bf16[4,272,128]{2,1,0:T(8,128)(2,1)S(1)}, bf16[4,272,128]{2,1,0:T(8,128)(2,1)S(1)}, u32[]{:S(2)}, u32[]{:S(2)}) collective-permute-start(bf16[4,272,128]{2,1,0:T(8,128)(2,1)S(1)} %copy-done), channel_id=1, source_target_pairs={{24,0},{0,8},{8,16},{16,24},{25,1},{1,9},{9,17},{17,25},{26,2},{2,... | collective-permute-start | bytes 835592 | tf_op jit(solution)/shard_map/ppermute | solution.py:372
  14.1 15.3 %collective-permute-start.2 = (bf16[4,272,128]{2,1,0:T(8,128)(2,1)S(1)}, bf16[4,272,128]{2,1,0:T(8,128)(2,1)S(1)}, u32[]{:S(2)}, u32[]{:S(2)}) collective-permute-start(bf16[4,272,128]{2,1,0:T(8,128)(2,1)S(1)} %copy-done), channel_id=1, source_target_pairs={{16,0},{24,8},{0,16},{8,24},{17,1},{25,9},{1,17},{9,25},{18,2},{26... | collective-permute-start | bytes 835592 | tf_op jit(solution)/shard_map/ppermute | solution.py:372
  16.8 12.7 %collective-permute-start.1 = (bf16[4,272,128]{2,1,0:T(8,128)(2,1)S(1)}, bf16[4,272,128]{2,1,0:T(8,128)(2,1)}, u32[]{:S(2)}, u32[]{:S(2)}) collective-permute-start(bf16[4,272,128]{2,1,0:T(8,128)(2,1)S(1)} %copy-done), channel_id=1, source_target_pairs={{8,0},{16,8},{24,16},{0,24},{9,1},{17,9},{25,17},{1,25},{10,2},{18... | collective-permute-start | bytes 835592 | tf_op jit(solution)/shard_map/ppermute | solution.py:372
  31.4 0.7 copy-start.4
  32.1 14.4 %collective-permute-start.4 = (bf16[4,256,128]{2,1,0:T(8,128)(2,1)}, bf16[4,256,128]{2,1,0:T(8,128)(2,1)S(1)}, u32[]{:S(2)}, u32[]{:S(2)}) collective-permute-start(bf16[4,256,128]{2,1,0:T(8,128)(2,1)} %get-tuple-element.21), channel_id=1, source_target_pairs={{1,0},{2,1},{3,2},{0,3},{5,4},{6,5},{7,6},{4,7},{9,8},{10,9},{11,1... | collective-permute-start | bytes 786440 | tf_op jit(solution)/shard_map/ppermute | solution.py:372
  34.9 14.5 %collective-permute-start.5 = (bf16[4,256,128]{2,1,0:T(8,128)(2,1)}, bf16[4,256,128]{2,1,0:T(8,128)(2,1)}, u32[]{:S(2)}, u32[]{:S(2)}) collective-permute-start(bf16[4,256,128]{2,1,0:T(8,128)(2,1)} %get-tuple-element.22), channel_id=1, source_target_pairs={{2,0},{3,1},{0,2},{1,3},{6,4},{7,5},{4,6},{5,7},{10,8},{11,9},{8,1... | collective-permute-start | bytes 786440 | tf_op jit(solution)/shard_map/ppermute | solution.py:372
  35.5 15.1 %collective-permute-start.6 = (bf16[4,256,128]{2,1,0:T(8,128)(2,1)}, bf16[4,256,128]{2,1,0:T(8,128)(2,1)}, u32[]{:S(2)}, u32[]{:S(2)}) collective-permute-start(bf16[4,256,128]{2,1,0:T(8,128)(2,1)} %get-tuple-element.23), channel_id=1, source_target_pairs={{3,0},{0,1},{1,2},{2,3},{7,4},{4,5},{5,6},{6,7},{11,8},{8,9},{9,10... | collective-permute-start | bytes 786440 | tf_op jit(solution)/shard_map/ppermute | solution.py:372
  36.1 33.3 %collective-permute-start.7 = (bf16[4,272,128]{2,1,0:T(8,128)(2,1)S(1)}, bf16[4,272,128]{2,1,0:T(8,128)(2,1)S(1)}, u32[]{:S(2)}, u32[]{:S(2)}) collective-permute-start(bf16[4,272,128]{2,1,0:T(8,128)(2,1)S(1)} %copy-done), channel_id=1, source_target_pairs={{0,64},{32,96},{64,0},{96,32},{1,65},{33,97},{65,1},{97,33},{2,66}... | collective-permute-start | bytes 835592 | tf_op jit(solution)/shard_map/ppermute | solution.py:367
  38.5 30.8 %collective-permute-start.8 = (bf16[4,272,128]{2,1,0:T(8,128)(2,1)}, bf16[4,272,128]{2,1,0:T(8,128)(2,1)}, u32[]{:S(2)}, u32[]{:S(2)}) collective-permute-start(bf16[4,272,128]{2,1,0:T(8,128)(2,1)} %collective-permute-done.refs_1_), channel_id=1, source_target_pairs={{0,64},{32,96},{64,0},{96,32},{1,65},{33,97},{65,1},{97,33},{2,66}... | collective-permute-start | bytes 835592 | tf_op jit(solution)/shard_map/ppermute | solution.py:367
  39.1 1.0 copy-start.5
  46.5 0.7 copy-start.2
  47.2 37.0 %collective-permute-start.9 = (bf16[4,272,128]{2,1,0:T(8,128)(2,1)}, bf16[4,272,128]{2,1,0:T(8,128)(2,1)S(1)}, u32[]{:S(2)}, u32[]{:S(2)}) collective-permute-start(bf16[4,272,128]{2,1,0:T(8,128)(2,1)} %get-tuple-element.29), channel_id=1, source_target_pairs={{0,32},{32,0},{64,96},{96,64},{1,33},{33,1},{65,97},{97,65},{2,34}... | collective-permute-start | bytes 835592 | tf_op jit(solution)/shard_map/ppermute | solution.py:367
  50.6 1.0 copy-start.3
  69.3 24.3 %all-to-all-start.1 = ((bf16[16,272,128]{2,1,0:T(8,128)(2,1)}), bf16[16,272,128]{2,1,0:T(8,128)(2,1)S(1)}, u32[]{:S(2)}, u32[]{:S(2)}) async-start(bf16[16,272,128]{2,1,0:T(8,128)(2,1)} %prefix_part.3), calls=%async_computation.1 | async-start | bytes 2228224 | tf_op jit(solution)/shard_map/all_to_all | solution.py:397
  77.3 10.7 %collective-permute-start.10 = (bf16[4,272,128]{2,1,0:T(8,128)(2,1)S(1)}, bf16[4,272,128]{2,1,0:T(8,128)(2,1)S(1)}, u32[]{:S(2)}, u32[]{:S(2)}) collective-permute-start(bf16[4,272,128]{2,1,0:T(8,128)(2,1)S(1)} %page_part.4), channel_id=1, source_target_pairs={{0,96},{32,64},{64,32},{96,0},{1,97},{33,65},{65,33},{97,1},{2,98}... | collective-permute-start | bytes 835592 | tf_op jit(solution)/shard_map/ppermute | solution.py:367
  83.6 10.0 %collective-permute-start.11 = (bf16[4,272,128]{2,1,0:T(8,128)(2,1)S(1)}, bf16[4,272,128]{2,1,0:T(8,128)(2,1)S(1)}, u32[]{:S(2)}, u32[]{:S(2)}) collective-permute-start(bf16[4,272,128]{2,1,0:T(8,128)(2,1)S(1)} %page_part.5), channel_id=1, source_target_pairs={{0,64},{32,96},{64,0},{96,32},{1,65},{33,97},{65,1},{97,33},{2,66}... | collective-permute-start | bytes 835592 | tf_op jit(solution)/shard_map/ppermute | solution.py:367

commit v6 on v5

--- a/solution.py
+++ b/solution.py
@@ -93,41 +93,52 @@
     return m, l, o
 
 
-def prefix_kernel(at_ref, *refs, count, tile):
-    q_refs, kv_ref, out_ref, held = refs[:count], refs[count], refs[-2], refs[-1]
+def prefix_kernel(at_ref, *refs, count, per, tile):
+    q_refs, kv_ref, done_refs, (out_ref, held) = (
+        refs[:count],
+        refs[count],
+        refs[count + 1 : -2],
+        refs[-2:],
+    )
     i = pl.program_id(0)
+    first = len(done_refs)
 
     @pl.when(i == 0)
     def _():
         for n, q_ref in enumerate(q_refs):
-            held[n] = q_ref[...].reshape(4 * ROWS, HD)
-
-    m, l, o = online(held[i], kv_ref, tile)
-    for n in range(4):
+            held[4 * n : 4 * n + 4] = q_ref[...]
+        for done_ref in done_refs:
+            for n in range(4):
+                out_ref[4 * at_ref[1] + n] = done_ref[n]
+
+    rows = held[pl.ds(i * per, per)].reshape(per * ROWS, HD)
+    m, l, o = online(rows, kv_ref, tile)
+    for n in range(per):
         part = slice(n * ROWS, (n + 1) * ROWS)
-        place = lax.rem(at_ref[0] + n, 4)
+        block = i * per + n
+        place = lax.rem(at_ref[0] + block, 4)
+        if first:
+            place = place + 4 * lax.rem(at_ref[1] + 1 + lax.div(block, 4), 4)
         out_ref[place, :ROWS, :] = o[part].astype(BF16)
         out_ref[place, ROWS:, :] = pack_stats(m[part], l[part])
 
 
-def prefix_part(at, qs, kv, first, done, tile):
+def prefix_part(at, qs, kv, done, per, tile):
     count = len(qs)
+    blocks = 16 if done else 4
     tokens = kv.shape[0] * kv.shape[2]
     return pl.pallas_call(
-        functools.partial(prefix_kernel, count=count, tile=tile),
+        functools.partial(prefix_kernel, count=count, per=per, tile=tile),
         grid_spec=pltpu.PrefetchScalarGridSpec(
             num_scalar_prefetch=1,
-            grid=(count,),
+            grid=(4 * count // per,),
             in_specs=[pl.BlockSpec(qs[0].shape, lambda i, at: (0, 0, 0))] * count
             + [pl.BlockSpec(kv.shape, lambda i, at: (0, 0, 0, 0))]
-            + [pl.BlockSpec(memory_space=pl.ANY)] * len(done),
-            out_specs=pl.BlockSpec(
-                (4, PACK, HD), lambda i, at: (lax.rem(at[1] + i + first, 4), 0, 0)
-            ),
-            scratch_shapes=[pltpu.VMEM((count, 4 * ROWS, HD), BF16)],
+            + [pl.BlockSpec((4, PACK, HD), lambda i, at: (0, 0, 0))] * len(done),
+            out_specs=pl.BlockSpec((blocks, PACK, HD), lambda i, at: (0, 0, 0)),
+            scratch_shapes=[pltpu.VMEM((4 * count, ROWS, HD), BF16)],
         ),
-        out_shape=jax.ShapeDtypeStruct((16, PACK, HD), BF16),
-        input_output_aliases={count + 2: 0} if done else {},
+        out_shape=jax.ShapeDtypeStruct((blocks, PACK, HD), BF16),
         compiler_params=pltpu.CompilerParams(vmem_limit_bytes=48 << 20),
         cost_estimate=pl.CostEstimate(
             flops=count * ROWS * tokens * HD * 32,
@@ -138,10 +149,11 @@
     )(at, *qs, kv, *done)
 
 
-def prep_kernel(table_ref, size_ref, q_ref, kv_ref, asked_ref, dealt_ref):
+def prep_kernel(table_ref, size_ref, q_ref, kv_ref, asked_ref, rows_ref, dealt_ref):
     for c in range(GQA):
         tile = q_ref[:, :, c * HD : (c + 1) * HD].reshape(RS, HD)
         asked_ref[0, c * RS : (c + 1) * RS, :] = tile
+        rows_ref[0, c * RS : (c + 1) * RS, :] = tile
     both = kv_ref[0].astype(F32)
     for i in range(2):
         half = both[:, i].astype(BF16)
@@ -178,10 +190,12 @@
         ],
         out_specs=[
             pl.BlockSpec((1, PACK, HD), lambda k: (k, 0, 0)),
+            pl.BlockSpec((1, ROWS, HD), lambda k: (k, 0, 0)),
             pl.BlockSpec((2, 1, 2, tokens, HD), lambda k: (0, k, 0, 0, 0)),
         ],
         out_shape=[
             jax.ShapeDtypeStruct((KVH, PACK, HD), BF16),
+            jax.ShapeDtypeStruct((KVH, ROWS, HD), BF16),
             jax.ShapeDtypeStruct((2, KVH, 2, tokens, HD), BF16),
         ],
         compiler_params=pltpu.CompilerParams(vmem_limit_bytes=60 << 20),
@@ -194,7 +208,7 @@
     for k, out_ref in enumerate(out_refs):
         head = lax.rem(at_ref[1] + 4 - k, 4)
         for n, q_ref in enumerate(q_refs):
-            out_ref[n] = q_ref[head, :ROWS, :]
+            out_ref[n] = q_ref[head]
 
 
 def pick(at, asked):
@@ -329,34 +343,36 @@
 
 def merge_kernel(part_ref, *rest):
     page_refs, out_ref = rest[:-1], rest[-1]
-    found = [part_ref.at[0, i] for i in range(part_ref.shape[1])]
-    found += [ref.at[0] for ref in page_refs]
-    for half in range(ROWS // 128):
-        stats = [unpack_stats(ref[ROWS:, :], half) for ref in found]
-        top = functools.reduce(jnp.maximum, [m for m, _ in stats])
-        fades = [jnp.exp2(m - top) for m, _ in stats]
-        weight_sum = functools.reduce(jnp.add, [l * f for (_, l), f in zip(stats, fades)])
-        gains = jnp.concatenate(
-            [f / weight_sum for f in fades] + [jnp.zeros((128 - len(fades), 128), F32)], axis=0
-        ).T
-        total = jnp.zeros((128, HD), F32)
-        for i, ref in enumerate(found):
-            gain = jnp.broadcast_to(gains[:, i : i + 1], (128, HD))
-            total = total + ref[half * 128 : half * 128 + 128, :].astype(F32) * gain
-        total = total.astype(BF16)
-        for j in range(128 // RS):
-            col = half * 128 // RS + j
-            rows = total[j * RS : (j + 1) * RS].reshape(REQ, STEPS, HD)
-            out_ref[:, :, col * HD : (col + 1) * HD] = rows
+    for head in range(part_ref.shape[0]):
+        found = [part_ref.at[head, i] for i in range(part_ref.shape[1])]
+        found += [ref.at[head] for ref in page_refs]
+        for half in range(ROWS // 128):
+            stats = [unpack_stats(ref[ROWS:, :], half) for ref in found]
+            top = functools.reduce(jnp.maximum, [m for m, _ in stats])
+            fades = [jnp.exp2(m - top) for m, _ in stats]
+            weight_sum = functools.reduce(jnp.add, [l * f for (_, l), f in zip(stats, fades)])
+            gains = jnp.concatenate(
+                [f / weight_sum for f in fades] + [jnp.zeros((128 - len(fades), 128), F32)], axis=0
+            ).T
+            total = jnp.zeros((128, HD), F32)
+            for i, ref in enumerate(found):
+                gain = jnp.broadcast_to(gains[:, i : i + 1], (128, HD))
+                total = total + ref[half * 128 : half * 128 + 128, :].astype(F32) * gain
+            total = total.astype(BF16)
+            for j in range(128 // RS):
+                col = head * GQA + half * 128 // RS + j
+                rows = total[j * RS : (j + 1) * RS].reshape(REQ, STEPS, HD)
+                out_ref[:, :, col * HD : (col + 1) * HD] = rows
 
 
 def merge(parts, pages):
+    heads = 2
     return pl.pallas_call(
         merge_kernel,
-        grid=(KVH,),
-        in_specs=[pl.BlockSpec((1, *parts.shape[1:]), lambda k: (k, 0, 0, 0))]
-        + [pl.BlockSpec((1, PACK, HD), lambda k: (k, 0, 0))] * len(pages),
-        out_specs=pl.BlockSpec((REQ, STEPS, GQA * HD), lambda k: (0, 0, k)),
+        grid=(KVH // heads,),
+        in_specs=[pl.BlockSpec((heads, *parts.shape[1:]), lambda k: (k, 0, 0, 0))]
+        + [pl.BlockSpec((heads, PACK, HD), lambda k: (k, 0, 0))] * len(pages),
+        out_specs=pl.BlockSpec((REQ, STEPS, heads * GQA * HD), lambda k: (0, 0, k)),
         out_shape=jax.ShapeDtypeStruct((REQ, STEPS, HQ * HD), BF16),
         compiler_params=pltpu.CompilerParams(vmem_limit_bytes=32 << 20),
         name="merge",
@@ -378,11 +394,11 @@
 
 def local(queries, prefix_kv, pool, new_kv, unique_len, page_table, send_slots):
     at = jnp.stack([lax.axis_index(name) for name in ("y", "z", "grp")])
-    asked, dealt = prep(page_table, unique_len, queries, prefix_kv)
+    asked, rows, dealt = prep(page_table, unique_len, queries, prefix_kv)
     tokens = prefix_kv.shape[1]
     dealt = dealt.reshape(2 * KVH, 2, tokens, HD)
     kv_all = lax.all_to_all(dealt, ("xl", "z"), 0, 0, tiled=True)
-    chunks = [asked] + [fetch(asked, "y", k) for k in (1, 2, 3)]
+    chunks = [rows] + [fetch(rows, "y", k) for k in (1, 2, 3)]
     asked_1 = swap(asked, "grp", 1)
     fresh = new_kv.transpose(2, 0, 1, 3).reshape(2, RS, KVH * HD)
     fresh = jnp.pad(fresh, ((0, 0), (0, PAGE - RS), (0, 0)))
@@ -391,8 +407,8 @@
     came = [fetch(x, "z", k) for k, x in enumerate(sent, 1)]
     asked_2 = swap(after(asked, mine), "grp", 2)
     asked_3 = swap(after(asked_1, mine), "grp", 2)
-    part = prefix_part(at, [mine], kv_all, 0, [], 256)
-    part = prefix_part(at, came, kv_all, 1, [part], 256)
+    part = prefix_part(at, [mine], kv_all, [], 4, 256)
+    part = prefix_part(at, came, kv_all, [part], 6, 256)
     part = after(part, asked_2, asked_3)
     moved = lax.all_to_all(part, ("z", "y"), 0, 0, tiled=True)
     late = after(at, part)

time: 97 us -> 96.3 us (level)
  Pallas kernels: 47.2 us -> 46.1 us
    pallas_call x3, Pallas kernels: 27.1 us -> 25.9 us  [the longest x2 23.3 us: prefix_part(): pl.pallas_call(functools.partial(prefix_kernel, count=count, per=per, til...]
    ppermute x6, starting transfers between devices: 9.81 us -> 10.8 us  [swap(): lax.ppermute(x, axis, [(i, i ^ mask) for i in range(lax.axis_size(axis))])]
  transfers between devices with their start and end apart: 14 -> 14, of which waited for: 4 -> 4; matrix products, arithmetic and copies ran while one was open for 0% -> 0% of each run, Pallas kernels for 41% -> 40%
where the time goes in v6:
time: 96.3 us; the launch traced here: 95.8 us
  Pallas kernels  46.1 us (48%)
  starting transfers between devices  30.9 us (32%)
  waiting for transfers between devices  15.4 us (16%)
  local copies, waits for them, and re-layouts  3.34 us (3%)
    pallas_call x2, Pallas kernels, prefix_part(): pl.pallas_call(functools.partial(prefix_kernel, count=count, per=per, til...  23.3 us
    pallas_call x3, Pallas kernels, page_part(): pl.pallas_call(functools.partial(page_kernel, first=first), grid_spec=plt...  13.4 us
    ppermute x6, starting transfers between devices, swap(): lax.ppermute(x, axis, [(i, i ^ mask) for i in range(lax.axis_size(axis))])  10.8 us
    ppermute x6, waiting for transfers between devices, swap(): lax.ppermute(x, axis, [(i, i ^ mask) for i in range(lax.axis_size(axis))])  9.28 us
    ppermute x6, starting transfers between devices, fetch(): return lax.ppermute(x, axis, [((i + by) % n, i) for i in range(n)])  9.09 us
    all_to_all x1, starting transfers between devices, local(): kv_all = lax.all_to_all(dealt, ('xl', 'z'), 0, 0, tiled=True)  6.93 us
    ppermute x6, waiting for transfers between devices, fetch(): return lax.ppermute(x, axis, [((i + by) % n, i) for i in range(n)])  6.09 us
    pallas_call x1, Pallas kernels, prep(): pl.pallas_call(prep_kernel, grid=(KVH,), in_specs=[pl.BlockSpec(page_tabl...  4.88 us
  transfers between devices with their start and end apart: 14, of which 4 were waited for; matrix products, arithmetic and copies ran while one was open for 0% of the time, Pallas kernels for 40%

profile of v6, /device:TPU:1, one launch (start us, length us, event | category | flops | bytes accessed | tf_op | source)
XLA Modules:
  0.0 95.8 jit_solution(11725276095026422210)
XLA Ops:
  0.0 4.9 %prep.1 = (bf16[4,272,128]{2,1,0:T(8,128)(2,1)}, bf16[4,256,128]{2,1,0:T(8,128)(2,1)}, bf16[2,4,2,512,128]{4,3,2,1,0:T(8,128)(2,1)}) custom-call(s32[1,24]{1,0:T(1,128)} %table_ref.1, s32[1,4]{1,0:T(1,128)} %bitcast.12, bf16[4,4,8192]{2,1,0:T(4,128)(2,1)} %q_ref.1, bf16[1,512,2,512]{3,2,1,0:T(2,128)(2,1)} %kv_ref.1), custom_call_target="tpu_custom_call" | custom-call | tf_op jit(solution)/shard_map/prep/pallas_call | solution.py:182
  4.9 0.0 copy-start.1
  4.9 6.9 %all-to-all-start = ((bf16[8,2,512,128]{3,2,1,0:T(8,128)(2,1)}), bf16[8,2,512,128]{3,2,1,0:T(8,128)(2,1)S(1)}, u32[]{:S(2)}, u32[]{:S(2)}) async-start(bf16[8,2,512,128]{3,2,1,0:T(8,128)(2,1)} %bitcast.10), calls=%async_computation | async-start | bytes 4194304 | tf_op jit(solution)/shard_map/all_to_all | solution.py:400
  11.8 1.0 collective-permute-start
  12.8 1.3 %collective-permute-start.3 = (bf16[4,256,128]{2,1,0:T(8,128)(2,1)S(1)}, bf16[4,256,128]{2,1,0:T(8,128)(2,1)S(1)}, u32[]{:S(2)}, u32[]{:S(2)}) collective-permute-start(bf16[4,256,128]{2,1,0:T(8,128)(2,1)S(1)} %copy-done), channel_id=1, source_target_pairs={{24,0},{0,8},{8,16},{16,24},{25,1},{1,9},{9,17},{17,25},{26,2},{2,... | collective-permute-start | bytes 786440 | tf_op jit(solution)/shard_map/ppermute | solution.py:388
  14.1 2.6 %collective-permute-start.2 = (bf16[4,256,128]{2,1,0:T(8,128)(2,1)S(1)}, bf16[4,256,128]{2,1,0:T(8,128)(2,1)S(1)}, u32[]{:S(2)}, u32[]{:S(2)}) collective-permute-start(bf16[4,256,128]{2,1,0:T(8,128)(2,1)S(1)} %copy-done), channel_id=1, source_target_pairs={{16,0},{24,8},{0,16},{8,24},{17,1},{25,9},{1,17},{9,25},{18,2},{26... | collective-permute-start | bytes 786440 | tf_op jit(solution)/shard_map/ppermute | solution.py:388
  16.7 1.1 %collective-permute-start.1 = (bf16[4,256,128]{2,1,0:T(8,128)(2,1)S(1)}, bf16[4,256,128]{2,1,0:T(8,128)(2,1)}, u32[]{:S(2)}, u32[]{:S(2)}) collective-permute-start(bf16[4,256,128]{2,1,0:T(8,128)(2,1)S(1)} %copy-done), channel_id=1, source_target_pairs={{8,0},{16,8},{24,16},{0,24},{9,1},{17,9},{25,17},{1,25},{10,2},{18... | collective-permute-start | bytes 786440 | tf_op jit(solution)/shard_map/ppermute | solution.py:388
  17.8 0.1 pad_add_fusion.at_ref
  17.9 6.6 %page_part.3 = (bf16[4,272,128]{2,1,0:T(8,128)(2,1)S(1)}, bf16[4,272,128]{2,1,0:T(8,128)(2,1)}) custom-call(s32[3]{0:T(128)S(1)} %pad_add_fusion.at_ref, s32[1,24]{1,0:T(1,128)S(1)} %copy-done.1, bf16[4,272,128]{2,1,0:T(8,128)(2,1)} %get-tuple-element.28.refs_0_, bf16[4,272,128]{2,1,0:T(8,128)(2,1)} %collective-permute-done.refs_1_, ...), custom_call_target="tpu_custom_call" | custom-call | flops 12884901888 | bytes 4194304 | tf_op jit(solution)/shard_map/page_part/pallas_call | solution.py:319
  24.6 4.2 %collective-permute-done.2.refs_2_ = bf16[4,256,128]{2,1,0:T(8,128)(2,1)S(1)} collective-permute-done((bf16[4,256,128]{2,1,0:T(8,128)(2,1)S(1)}, bf16[4,256,128]{2,1,0:T(8,128)(2,1)S(1)}, u32[]{:S(2)}, u32[]{:S(2)}) %collective-permute-start.2) | collective-permute-done | bytes 262176 | tf_op jit(solution)/shard_map/ppermute | solution.py:388
  28.7 1.9 %pick.1 = (bf16[4,256,128]{2,1,0:T(8,128)(2,1)S(1)}, bf16[4,256,128]{2,1,0:T(8,128)(2,1)}, bf16[4,256,128]{2,1,0:T(8,128)(2,1)}, bf16[4,256,128]{2,1,0:T(8,128)(2,1)}) custom-call(s32[3]{0:T(128)S(1)} %pad_add_fusion.at_ref, bf16[4,256,128]{2,1,0:T(8,128)(2,1)S(1)} %copy-done, bf16[4,256,128]{2,1,0:T(8,128)(2,1)} %collective-permute-done.1.refs_1_, ...), custom_call_target="tpu_custom_call" | custom-call | tf_op jit(solution)/shard_map/pick/pallas_call | solution.py:217
  30.7 0.7 copy-done.4
  31.4 2.9 %collective-permute-start.4 = (bf16[4,256,128]{2,1,0:T(8,128)(2,1)}, bf16[4,256,128]{2,1,0:T(8,128)(2,1)S(1)}, u32[]{:S(2)}, u32[]{:S(2)}) collective-permute-start(bf16[4,256,128]{2,1,0:T(8,128)(2,1)} %get-tuple-element.23), channel_id=1, source_target_pairs={{1,0},{2,1},{3,2},{0,3},{5,4},{6,5},{7,6},{4,7},{9,8},{10,9},{11,1... | collective-permute-start | bytes 786440 | tf_op jit(solution)/shard_map/ppermute | solution.py:388
  34.3 0.6 collective-permute-start.5
  34.9 0.6 collective-permute-start.6
  35.4 2.5 %collective-permute-start.7 = (bf16[4,272,128]{2,1,0:T(8,128)(2,1)}, bf16[4,272,128]{2,1,0:T(8,128)(2,1)S(1)}, u32[]{:S(2)}, u32[]{:S(2)}) collective-permute-start(bf16[4,272,128]{2,1,0:T(8,128)(2,1)} %get-tuple-element.28.refs_0_), channel_id=1, source_target_pairs={{0,64},{32,96},{64,0},{96,32},{1,65},{33,97},{65,1},{97,33},{2,66}... | collective-permute-start | bytes 835592 | tf_op jit(solution)/shard_map/ppermute | solution.py:383
  37.9 0.5 collective-permute-start.8
  38.4 0.9 copy-done.5
  39.4 5.7 %prefix_part.2.refs_4_ = bf16[4,272,128]{2,1,0:T(8,128)(2,1)S(1)} custom-call(s32[3]{0:T(128)S(1)} %pad_add_fusion.at_ref, bf16[4,256,128]{2,1,0:T(8,128)(2,1)S(1)} %copy-done.5, bf16[8,2,512,128]{3,2,1,0:T(8,128)(2,1)S(1)} %all-to-all-done.refs_1_.refs_3_), custom_call_target="tpu_custom_call" | custom-call | flops 4294967296 | bytes 8388608 | tf_op jit(solution)/shard_map/prefix_part/pallas_call | solution.py:130
  45.1 0.7 copy-done.2
  45.8 2.3 %collective-permute-start.9 = (bf16[4,272,128]{2,1,0:T(8,128)(2,1)}, bf16[4,272,128]{2,1,0:T(8,128)(2,1)S(1)}, u32[]{:S(2)}, u32[]{:S(2)}) collective-permute-start(bf16[4,272,128]{2,1,0:T(8,128)(2,1)} %get-tuple-element.31), channel_id=1, source_target_pairs={{0,32},{32,0},{64,96},{96,64},{1,33},{33,1},{65,97},{97,65},{2,34}... | collective-permute-start | bytes 835592 | tf_op jit(solution)/shard_map/ppermute | solution.py:383
  48.1 1.9 %collective-permute-done.6.refs_2_ = bf16[4,256,128]{2,1,0:T(8,128)(2,1)} collective-permute-done((bf16[4,256,128]{2,1,0:T(8,128)(2,1)}, bf16[4,256,128]{2,1,0:T(8,128)(2,1)}, u32[]{:S(2)}, u32[]{:S(2)}) %collective-permute-start.6) | collective-permute-done | bytes 262176 | tf_op jit(solution)/shard_map/ppermute | solution.py:388
  50.0 0.9 copy-done.3
  51.0 17.5 %prefix_part.3 = bf16[16,272,128]{2,1,0:T(8,128)(2,1)} custom-call(s32[3]{0:T(128)S(1)} %pad_add_fusion.at_ref, bf16[4,256,128]{2,1,0:T(8,128)(2,1)S(1)} %copy-done.3, bf16[4,256,128]{2,1,0:T(8,128)(2,1)} %collective-permute-done.5.refs_1_, bf16[4,256,128]{2,1,0:T(8,128)(2,1)} %collective-permute-done.6.refs_2_, ...), custom_call_target="tpu_custom_call" | custom-call | flops 12884901888 | bytes 8388608 | tf_op jit(solution)/shard_map/prefix_part/pallas_call | solution.py:130
  68.5 4.0 %all-to-all-start.1 = ((bf16[16,272,128]{2,1,0:T(8,128)(2,1)}), bf16[16,272,128]{2,1,0:T(8,128)(2,1)S(1)}, u32[]{:S(2)}, u32[]{:S(2)}) async-start(bf16[16,272,128]{2,1,0:T(8,128)(2,1)} %prefix_part.3), calls=%async_computation.1 | async-start | bytes 2228224 | tf_op jit(solution)/shard_map/all_to_all | solution.py:413
  72.5 3.4 %page_part.4 = bf16[4,272,128]{2,1,0:T(8,128)(2,1)S(1)} custom-call(s32[3]{0:T(128)S(1)} %pad_add_fusion.at_ref, s32[1,24]{1,0:T(1,128)S(1)} %copy-done.1, bf16[4,272,128]{2,1,0:T(8,128)(2,1)S(1)} %collective-permute-done.8.refs_0_, bf16[2,128,512]{2,1,0:T(8,128)(2,1)S(1)} %pad.4.refs_2_.refs_1_, bf16[24,2,128,512]{3,2,1,0:T(8,128)(2,1)} %refs_7_.5, ...), custom_call_target="tpu_custom_call" | custom-call | flops 6442450944 | bytes 4194304 | tf_op jit(solution)/shard_map/page_part/pallas_call | solution.py:319
  75.9 4.0 %collective-permute-start.10 = (bf16[4,272,128]{2,1,0:T(8,128)(2,1)S(1)}, bf16[4,272,128]{2,1,0:T(8,128)(2,1)S(1)}, u32[]{:S(2)}, u32[]{:S(2)}) collective-permute-start(bf16[4,272,128]{2,1,0:T(8,128)(2,1)S(1)} %page_part.4), channel_id=1, source_target_pairs={{0,96},{32,64},{64,32},{96,0},{1,97},{33,65},{65,33},{97,1},{2,98}... | collective-permute-start | bytes 835592 | tf_op jit(solution)/shard_map/ppermute | solution.py:383
  79.9 3.4 %page_part.5 = bf16[4,272,128]{2,1,0:T(8,128)(2,1)S(1)} custom-call(s32[3]{0:T(128)S(1)} %pad_add_fusion.at_ref, s32[1,24]{1,0:T(1,128)S(1)} %copy-done.1, bf16[4,272,128]{2,1,0:T(8,128)(2,1)S(1)} %collective-permute-done.7.refs_0_, bf16[2,128,512]{2,1,0:T(8,128)(2,1)S(1)} %pad.4.refs_2_.refs_1_, bf16[24,2,128,512]{3,2,1,0:T(8,128)(2,1)} %refs_7_.5, ...), custom_call_target="tpu_custom_call" | custom-call | flops 6442450944 | bytes 4194304 | tf_op jit(solution)/shard_map/page_part/pallas_call | solution.py:319
  83.3 0.6 collective-permute-start.11
  83.9 3.3 %collective-permute-done.10.rest_2_ = bf16[4,272,128]{2,1,0:T(8,128)(2,1)S(1)} collective-permute-done((bf16[4,272,128]{2,1,0:T(8,128)(2,1)S(1)}, bf16[4,272,128]{2,1,0:T(8,128)(2,1)S(1)}, u32[]{:S(2)}, u32[]{:S(2)}) %collective-permute-start.10) | collective-permute-done | bytes 278560 | tf_op jit(solution)/shard_map/ppermute | solution.py:383
  87.2 6.0 %collective-permute-done.11.rest_3_ = bf16[4,272,128]{2,1,0:T(8,128)(2,1)S(1)} collective-permute-done((bf16[4,272,128]{2,1,0:T(8,128)(2,1)S(1)}, bf16[4,272,128]{2,1,0:T(8,128)(2,1)S(1)}, u32[]{:S(2)}, u32[]{:S(2)}) %collective-permute-start.11) | collective-permute-done | bytes 278560 | tf_op jit(solution)/shard_map/ppermute | solution.py:383
  93.2 2.6 %merge.1 = bf16[4,4,8192]{2,1,0:T(4,128)(2,1)} custom-call(bf16[4,4,272,128]{3,2,1,0:T(8,128)(2,1)S(1)} %bitcast.9, bf16[4,272,128]{2,1,0:T(8,128)(2,1)S(1)} %get-tuple-element.20.rest_0_, bf16[4,272,128]{2,1,0:T(8,128)(2,1)S(1)} %collective-permute-done.9.rest_1_, bf16[4,272,128]{2,1,0:T(8,128)(2,1)S(1)} %collective-permute-done.10.rest_2_, ...), custom_call_target="tpu_custom_call" | custom-call | tf_op jit(solution)/shard_map/merge/pallas_call | solution.py:370
  (21 shorter events, 0.1 us)
Async XLA Ops:
  4.9 7.9 %copy-start = (bf16[4,256,128]{2,1,0:T(8,128)(2,1)S(1)}, bf16[4,256,128]{2,1,0:T(8,128)(2,1)}, u32[]{:S(2)}) copy-start(bf16[4,256,128]{2,1,0:T(8,128)(2,1)} %get-tuple-element.22.refs_0_) | copy-start | bytes 786436
  4.9 12.9 %copy-start.6 = (bf16[4,4,2,512]{3,2,1,0:T(2,128)(2,1)S(1)}, bf16[4,4,2,512]{3,2,1,0:T(2,128)(2,1)}, u32[]{:S(2)}) copy-start(bf16[4,4,2,512]{3,2,1,0:T(2,128)(2,1)} %param.10) | copy-start | bytes 98308
  4.9 13.0 %copy-start.1 = (s32[1,24]{1,0:T(1,128)S(1)}, s32[1,24]{1,0:T(1,128)}, u32[]{:S(2)}) copy-start(s32[1,24]{1,0:T(1,128)} %slot_ref.5) | copy-start | bytes 292
  4.9 33.5 %all-to-all-start = ((bf16[8,2,512,128]{3,2,1,0:T(8,128)(2,1)}), bf16[8,2,512,128]{3,2,1,0:T(8,128)(2,1)S(1)}, u32[]{:S(2)}, u32[]{:S(2)}) async-start(bf16[8,2,512,128]{3,2,1,0:T(8,128)(2,1)} %bitcast.10), calls=%async_computation | async-start | bytes 4194304 | tf_op jit(solution)/shard_map/all_to_all | solution.py:400
  11.8 6.1 %collective-permute-start = (bf16[4,272,128]{2,1,0:T(8,128)(2,1)}, bf16[4,272,128]{2,1,0:T(8,128)(2,1)}, u32[]{:S(2)}, u32[]{:S(2)}) collective-permute-start(bf16[4,272,128]{2,1,0:T(8,128)(2,1)} %get-tuple-element.28.refs_0_), channel_id=1, source_target_pairs={{0,32},{32,0},{64,96},{96,64},{1,33},{33,1},{65,97},{97,65},{2,34}... | collective-permute-start | bytes 835592 | tf_op jit(solution)/shard_map/ppermute | solution.py:383
  12.8 11.8 %collective-permute-start.3 = (bf16[4,256,128]{2,1,0:T(8,128)(2,1)S(1)}, bf16[4,256,128]{2,1,0:T(8,128)(2,1)S(1)}, u32[]{:S(2)}, u32[]{:S(2)}) collective-permute-start(bf16[4,256,128]{2,1,0:T(8,128)(2,1)S(1)} %copy-done), channel_id=1, source_target_pairs={{24,0},{0,8},{8,16},{16,24},{25,1},{1,9},{9,17},{17,25},{26,2},{2,... | collective-permute-start | bytes 786440 | tf_op jit(solution)/shard_map/ppermute | solution.py:388
  14.1 14.6 %collective-permute-start.2 = (bf16[4,256,128]{2,1,0:T(8,128)(2,1)S(1)}, bf16[4,256,128]{2,1,0:T(8,128)(2,1)S(1)}, u32[]{:S(2)}, u32[]{:S(2)}) collective-permute-start(bf16[4,256,128]{2,1,0:T(8,128)(2,1)S(1)} %copy-done), channel_id=1, source_target_pairs={{16,0},{24,8},{0,16},{8,24},{17,1},{25,9},{1,17},{9,25},{18,2},{26... | collective-permute-start | bytes 786440 | tf_op jit(solution)/shard_map/ppermute | solution.py:388
  16.7 12.0 %collective-permute-start.1 = (bf16[4,256,128]{2,1,0:T(8,128)(2,1)S(1)}, bf16[4,256,128]{2,1,0:T(8,128)(2,1)}, u32[]{:S(2)}, u32[]{:S(2)}) collective-permute-start(bf16[4,256,128]{2,1,0:T(8,128)(2,1)S(1)} %copy-done), channel_id=1, source_target_pairs={{8,0},{16,8},{24,16},{0,24},{9,1},{17,9},{25,17},{1,25},{10,2},{18... | collective-permute-start | bytes 786440 | tf_op jit(solution)/shard_map/ppermute | solution.py:388
  30.7 0.7 copy-start.4
  31.4 13.8 %collective-permute-start.4 = (bf16[4,256,128]{2,1,0:T(8,128)(2,1)}, bf16[4,256,128]{2,1,0:T(8,128)(2,1)S(1)}, u32[]{:S(2)}, u32[]{:S(2)}) collective-permute-start(bf16[4,256,128]{2,1,0:T(8,128)(2,1)} %get-tuple-element.23), channel_id=1, source_target_pairs={{1,0},{2,1},{3,2},{0,3},{5,4},{6,5},{7,6},{4,7},{9,8},{10,9},{11,1... | collective-permute-start | bytes 786440 | tf_op jit(solution)/shard_map/ppermute | solution.py:388
  34.3 13.8 %collective-permute-start.5 = (bf16[4,256,128]{2,1,0:T(8,128)(2,1)}, bf16[4,256,128]{2,1,0:T(8,128)(2,1)}, u32[]{:S(2)}, u32[]{:S(2)}) collective-permute-start(bf16[4,256,128]{2,1,0:T(8,128)(2,1)} %get-tuple-element.24), channel_id=1, source_target_pairs={{2,0},{3,1},{0,2},{1,3},{6,4},{7,5},{4,6},{5,7},{10,8},{11,9},{8,1... | collective-permute-start | bytes 786440 | tf_op jit(solution)/shard_map/ppermute | solution.py:388
  34.9 15.1 %collective-permute-start.6 = (bf16[4,256,128]{2,1,0:T(8,128)(2,1)}, bf16[4,256,128]{2,1,0:T(8,128)(2,1)}, u32[]{:S(2)}, u32[]{:S(2)}) collective-permute-start(bf16[4,256,128]{2,1,0:T(8,128)(2,1)} %get-tuple-element.25), channel_id=1, source_target_pairs={{3,0},{0,1},{1,2},{2,3},{7,4},{4,5},{5,6},{6,7},{11,8},{8,9},{9,10... | collective-permute-start | bytes 786440 | tf_op jit(solution)/shard_map/ppermute | solution.py:388
  35.4 33.1 %collective-permute-start.7 = (bf16[4,272,128]{2,1,0:T(8,128)(2,1)}, bf16[4,272,128]{2,1,0:T(8,128)(2,1)S(1)}, u32[]{:S(2)}, u32[]{:S(2)}) collective-permute-start(bf16[4,272,128]{2,1,0:T(8,128)(2,1)} %get-tuple-element.28.refs_0_), channel_id=1, source_target_pairs={{0,64},{32,96},{64,0},{96,32},{1,65},{33,97},{65,1},{97,33},{2,66}... | collective-permute-start | bytes 835592 | tf_op jit(solution)/shard_map/ppermute | solution.py:383
  37.9 30.6 %collective-permute-start.8 = (bf16[4,272,128]{2,1,0:T(8,128)(2,1)}, bf16[4,272,128]{2,1,0:T(8,128)(2,1)S(1)}, u32[]{:S(2)}, u32[]{:S(2)}) collective-permute-start(bf16[4,272,128]{2,1,0:T(8,128)(2,1)} %collective-permute-done.refs_1_), channel_id=1, source_target_pairs={{0,64},{32,96},{64,0},{96,32},{1,65},{33,97},{65,1},{97,33},{2,66}... | collective-permute-start | bytes 835592 | tf_op jit(solution)/shard_map/ppermute | solution.py:383
  38.4 1.0 copy-start.5
  45.1 0.7 copy-start.2
  45.8 38.1 %collective-permute-start.9 = (bf16[4,272,128]{2,1,0:T(8,128)(2,1)}, bf16[4,272,128]{2,1,0:T(8,128)(2,1)S(1)}, u32[]{:S(2)}, u32[]{:S(2)}) collective-permute-start(bf16[4,272,128]{2,1,0:T(8,128)(2,1)} %get-tuple-element.31), channel_id=1, source_target_pairs={{0,32},{32,0},{64,96},{96,64},{1,33},{33,1},{65,97},{97,65},{2,34}... | collective-permute-start | bytes 835592 | tf_op jit(solution)/shard_map/ppermute | solution.py:383
  50.0 1.0 copy-start.3
  68.5 24.7 %all-to-all-start.1 = ((bf16[16,272,128]{2,1,0:T(8,128)(2,1)}), bf16[16,272,128]{2,1,0:T(8,128)(2,1)S(1)}, u32[]{:S(2)}, u32[]{:S(2)}) async-start(bf16[16,272,128]{2,1,0:T(8,128)(2,1)} %prefix_part.3), calls=%async_computation.1 | async-start | bytes 2228224 | tf_op jit(solution)/shard_map/all_to_all | solution.py:413
  75.9 11.3 %collective-permute-start.10 = (bf16[4,272,128]{2,1,0:T(8,128)(2,1)S(1)}, bf16[4,272,128]{2,1,0:T(8,128)(2,1)S(1)}, u32[]{:S(2)}, u32[]{:S(2)}) collective-permute-start(bf16[4,272,128]{2,1,0:T(8,128)(2,1)S(1)} %page_part.4), channel_id=1, source_target_pairs={{0,96},{32,64},{64,32},{96,0},{1,97},{33,65},{65,33},{97,1},{2,98}... | collective-permute-start | bytes 835592 | tf_op jit(solution)/shard_map/ppermute | solution.py:383
  83.3 9.9 %collective-permute-start.11 = (bf16[4,272,128]{2,1,0:T(8,128)(2,1)S(1)}, bf16[4,272,128]{2,1,0:T(8,128)(2,1)S(1)}, u32[]{:S(2)}, u32[]{:S(2)}) collective-permute-start(bf16[4,272,128]{2,1,0:T(8,128)(2,1)S(1)} %page_part.5), channel_id=1, source_target_pairs={{0,64},{32,96},{64,0},{96,32},{1,65},{33,97},{65,1},{97,33},{2,66}... | collective-permute-start | bytes 835592 | tf_op jit(solution)/shard_map/ppermute | solution.py:383

commit v7 on v6

--- a/solution.py
+++ b/solution.py
@@ -341,42 +341,80 @@
     )(at, slots, *asked, fresh, *([pool] * MAXP))
 
 
+def weigh(stats):
+    top = functools.reduce(jnp.maximum, [m for m, _ in stats])
+    fades = [jnp.exp2(m - top) for m, _ in stats]
+    weight_sum = functools.reduce(jnp.add, [l * f for (_, l), f in zip(stats, fades)])
+    return top, fades, weight_sum
+
+
+def gather_up(gains, values):
+    tall = jnp.concatenate([*gains, jnp.zeros((128 - len(gains), 128), F32)], axis=0).T
+    total = jnp.zeros((128, HD), F32)
+    for i, value in enumerate(values):
+        total = total + value.astype(F32) * jnp.broadcast_to(tall[:, i : i + 1], (128, HD))
+    return total
+
+
 def merge_kernel(part_ref, *rest):
-    page_refs, out_ref = rest[:-1], rest[-1]
+    page_refs, o_ref, stat_ref = rest[:-2], rest[-2], rest[-1]
     for head in range(part_ref.shape[0]):
         found = [part_ref.at[head, i] for i in range(part_ref.shape[1])]
         found += [ref.at[head] for ref in page_refs]
+        rows = []
         for half in range(ROWS // 128):
-            stats = [unpack_stats(ref[ROWS:, :], half) for ref in found]
-            top = functools.reduce(jnp.maximum, [m for m, _ in stats])
-            fades = [jnp.exp2(m - top) for m, _ in stats]
-            weight_sum = functools.reduce(jnp.add, [l * f for (_, l), f in zip(stats, fades)])
-            gains = jnp.concatenate(
-                [f / weight_sum for f in fades] + [jnp.zeros((128 - len(fades), 128), F32)], axis=0
-            ).T
-            total = jnp.zeros((128, HD), F32)
-            for i, ref in enumerate(found):
-                gain = jnp.broadcast_to(gains[:, i : i + 1], (128, HD))
-                total = total + ref[half * 128 : half * 128 + 128, :].astype(F32) * gain
-            total = total.astype(BF16)
+            top, fades, weight_sum = weigh([unpack_stats(ref[ROWS:, :], half) for ref in found])
+            span = slice(half * 128, half * 128 + 128)
+            o_ref[head, span, :] = gather_up(fades, [ref[span, :] for ref in found])
+            rows += [top, weight_sum]
+        stat_ref[head] = jnp.concatenate([*rows, jnp.zeros((4, 128), F32)], axis=0)
+
+
+def last_kernel(o_ref, stat_ref, page_ref, out_ref):
+    for head in range(o_ref.shape[0]):
+        for half in range(ROWS // 128):
+            span = slice(half * 128, half * 128 + 128)
+            known = stat_ref[head, 2 * half : 2 * half + 1], stat_ref[head, 2 * half + 1 : 2 * half + 2]
+            _, fades, weight_sum = weigh([known, unpack_stats(page_ref[head, ROWS:, :], half)])
+            gains = [f / weight_sum for f in fades]
+            total = gather_up(gains, [o_ref[head, span, :], page_ref[head, span, :]]).astype(BF16)
             for j in range(128 // RS):
                 col = head * GQA + half * 128 // RS + j
                 rows = total[j * RS : (j + 1) * RS].reshape(REQ, STEPS, HD)
                 out_ref[:, :, col * HD : (col + 1) * HD] = rows
 
 
-def merge(parts, pages):
+def merge(parts, pages, last):
     heads = 2
+    steps = (KVH // heads,)
+    page = pl.BlockSpec((heads, PACK, HD), lambda k: (k, 0, 0))
+    known = [
+        pl.BlockSpec((heads, ROWS, HD), lambda k: (k, 0, 0)),
+        pl.BlockSpec((heads, 8, HD), lambda k: (k, 0, 0)),
+    ]
+    params = pltpu.CompilerParams(vmem_limit_bytes=32 << 20)
+    o, stats = pl.pallas_call(
+        merge_kernel,
+        grid=steps,
+        in_specs=[pl.BlockSpec((heads, *parts.shape[1:]), lambda k: (k, 0, 0, 0))]
+        + [page] * len(pages),
+        out_specs=known,
+        out_shape=[
+            jax.ShapeDtypeStruct((KVH, ROWS, HD), F32),
+            jax.ShapeDtypeStruct((KVH, 8, HD), F32),
+        ],
+        compiler_params=params,
+        name="merge",
+    )(parts, *pages)
     return pl.pallas_call(
-        merge_kernel,
-        grid=(KVH // heads,),
-        in_specs=[pl.BlockSpec((heads, *parts.shape[1:]), lambda k: (k, 0, 0, 0))]
-        + [pl.BlockSpec((heads, PACK, HD), lambda k: (k, 0, 0))] * len(pages),
+        last_kernel,
+        grid=steps,
+        in_specs=[*known, page],
         out_specs=pl.BlockSpec((REQ, STEPS, heads * GQA * HD), lambda k: (0, 0, k)),
         out_shape=jax.ShapeDtypeStruct((REQ, STEPS, HQ * HD), BF16),
-        compiler_params=pltpu.CompilerParams(vmem_limit_bytes=32 << 20),
-        name="merge",
-    )(parts, *pages)
+        compiler_params=params,
+        name="merge_last",
+    )(o, stats, last)
 
 
 def swap(x, axis, mask):
@@ -414,8 +452,8 @@
     late = after(at, part)
     (page_2,) = page_part(late, send_slots, [asked_2], 2, fresh, pool)
     (page_3,) = page_part(late, send_slots, [asked_3], 3, fresh, pool)
-    found = [near[0], swap(near[1], "grp", 1), swap(page_3, "grp", 3), swap(page_2, "grp", 2)]
-    return merge(moved.reshape(KVH, 4, PACK, HD), found)
+    pages = [near[0], swap(near[1], "grp", 1), swap(page_2, "grp", 2)]
+    return merge(moved.reshape(KVH, 4, PACK, HD), pages, swap(page_3, "grp", 3))
 
 
 def solution(mesh):

time: 96.3 us -> 95.1 us (0.988)
  waiting for transfers between devices: 15.4 us -> 11.9 us
  Pallas kernels: 46.1 us -> 47.4 us
    ppermute x6, waiting for transfers between devices: 9.28 us -> 2.07 us  [swap(): lax.ppermute(x, axis, [(i, i ^ mask) for i in range(lax.axis_size(axis))])]
    all_to_all x1, waiting for transfers between devices: 0.01 us -> 3.69 us  [local(): moved = lax.all_to_all(part, ('z', 'y'), 0, 0, tiled=True)]
    pallas_call x1 -> x2, Pallas kernels: 2.63 us -> 3.25 us  [the longest x1 1.67 us: merge(): pl.pallas_call(merge_kernel, grid=steps, in_specs=[pl.BlockSpec((heads, *...]
  transfers between devices with their start and end apart: 14 -> 14, of which waited for: 4 -> 4; matrix products, arithmetic and copies ran while one was open for 0% -> 0% of each run, Pallas kernels for 40% -> 44%
where the time goes in v7:
time: 95.1 us; the launch traced here: 93.9 us
  Pallas kernels  47.4 us (50%)
  starting transfers between devices  31.1 us (33%)
  waiting for transfers between devices  11.9 us (13%)
  local copies, waits for them, and re-layouts  3.33 us (4%)
    pallas_call x2, Pallas kernels, prefix_part(): pl.pallas_call(functools.partial(prefix_kernel, count=count, per=per, til...  23.3 us
    pallas_call x3, Pallas kernels, page_part(): pl.pallas_call(functools.partial(page_kernel, first=first), grid_spec=plt...  14.1 us
    ppermute x6, starting transfers between devices, swap(): lax.ppermute(x, axis, [(i, i ^ mask) for i in range(lax.axis_size(axis))])  11 us
    ppermute x6, starting transfers between devices, fetch(): return lax.ppermute(x, axis, [((i + by) % n, i) for i in range(n)])  9.09 us
    all_to_all x1, starting transfers between devices, local(): kv_all = lax.all_to_all(dealt, ('xl', 'z'), 0, 0, tiled=True)  6.93 us
    ppermute x6, waiting for transfers between devices, fetch(): return lax.ppermute(x, axis, [((i + by) % n, i) for i in range(n)])  6.11 us
    pallas_call x1, Pallas kernels, prep(): pl.pallas_call(prep_kernel, grid=(KVH,), in_specs=[pl.BlockSpec(page_tabl...  4.89 us
    all_to_all x1, starting transfers between devices, local(): moved = lax.all_to_all(part, ('z', 'y'), 0, 0, tiled=True)  4.01 us
  transfers between devices with their start and end apart: 14, of which 4 were waited for; matrix products, arithmetic and copies ran while one was open for 0% of the time, Pallas kernels for 44%

profile of v7, /device:TPU:1, one launch (start us, length us, event | category | flops | bytes accessed | tf_op | source)
XLA Modules:
  0.0 93.9 jit_solution(16271403477751097830)
XLA Ops:
  0.0 4.9 %prep.1 = (bf16[4,272,128]{2,1,0:T(8,128)(2,1)}, bf16[4,256,128]{2,1,0:T(8,128)(2,1)}, bf16[2,4,2,512,128]{4,3,2,1,0:T(8,128)(2,1)}) custom-call(s32[1,24]{1,0:T(1,128)} %table_ref.1, s32[1,4]{1,0:T(1,128)} %bitcast.12, bf16[4,4,8192]{2,1,0:T(4,128)(2,1)} %q_ref.1, bf16[1,512,2,512]{3,2,1,0:T(2,128)(2,1)} %kv_ref.1), custom_call_target="tpu_custom_call" | custom-call | tf_op jit(solution)/shard_map/prep/pallas_call | solution.py:182
  4.9 6.9 %all-to-all-start = ((bf16[8,2,512,128]{3,2,1,0:T(8,128)(2,1)}), bf16[8,2,512,128]{3,2,1,0:T(8,128)(2,1)S(1)}, u32[]{:S(2)}, u32[]{:S(2)}) async-start(bf16[8,2,512,128]{3,2,1,0:T(8,128)(2,1)} %bitcast.10), calls=%async_computation | async-start | bytes 4194304 | tf_op jit(solution)/shard_map/all_to_all | solution.py:438
  11.8 1.0 %collective-permute-start = (bf16[4,272,128]{2,1,0:T(8,128)(2,1)}, bf16[4,272,128]{2,1,0:T(8,128)(2,1)}, u32[]{:S(2)}, u32[]{:S(2)}) collective-permute-start(bf16[4,272,128]{2,1,0:T(8,128)(2,1)} %get-tuple-element.30.refs_0_), channel_id=1, source_target_pairs={{0,32},{32,0},{64,96},{96,64},{1,33},{33,1},{65,97},{97,65},{2,34}... | collective-permute-start | bytes 835592 | tf_op jit(solution)/shard_map/ppermute | solution.py:421
  12.8 1.3 %collective-permute-start.3 = (bf16[4,256,128]{2,1,0:T(8,128)(2,1)S(1)}, bf16[4,256,128]{2,1,0:T(8,128)(2,1)S(1)}, u32[]{:S(2)}, u32[]{:S(2)}) collective-permute-start(bf16[4,256,128]{2,1,0:T(8,128)(2,1)S(1)} %copy-done), channel_id=1, source_target_pairs={{24,0},{0,8},{8,16},{16,24},{25,1},{1,9},{9,17},{17,25},{26,2},{2,... | collective-permute-start | bytes 786440 | tf_op jit(solution)/shard_map/ppermute | solution.py:426
  14.1 2.6 %collective-permute-start.2 = (bf16[4,256,128]{2,1,0:T(8,128)(2,1)S(1)}, bf16[4,256,128]{2,1,0:T(8,128)(2,1)S(1)}, u32[]{:S(2)}, u32[]{:S(2)}) collective-permute-start(bf16[4,256,128]{2,1,0:T(8,128)(2,1)S(1)} %copy-done), channel_id=1, source_target_pairs={{16,0},{24,8},{0,16},{8,24},{17,1},{25,9},{1,17},{9,25},{18,2},{26... | collective-permute-start | bytes 786440 | tf_op jit(solution)/shard_map/ppermute | solution.py:426
  16.7 1.1 %collective-permute-start.1 = (bf16[4,256,128]{2,1,0:T(8,128)(2,1)S(1)}, bf16[4,256,128]{2,1,0:T(8,128)(2,1)}, u32[]{:S(2)}, u32[]{:S(2)}) collective-permute-start(bf16[4,256,128]{2,1,0:T(8,128)(2,1)S(1)} %copy-done), channel_id=1, source_target_pairs={{8,0},{16,8},{24,16},{0,24},{9,1},{17,9},{25,17},{1,25},{10,2},{18... | collective-permute-start | bytes 786440 | tf_op jit(solution)/shard_map/ppermute | solution.py:426
  17.8 0.1 pad_add_fusion.at_ref
  17.9 6.6 %page_part.3 = (bf16[4,272,128]{2,1,0:T(8,128)(2,1)S(1)}, bf16[4,272,128]{2,1,0:T(8,128)(2,1)}) custom-call(s32[3]{0:T(128)S(1)} %pad_add_fusion.at_ref, s32[1,24]{1,0:T(1,128)S(1)} %copy-done.1, bf16[4,272,128]{2,1,0:T(8,128)(2,1)} %get-tuple-element.30.refs_0_, bf16[4,272,128]{2,1,0:T(8,128)(2,1)} %collective-permute-done.refs_1_, ...), custom_call_target="tpu_custom_call" | custom-call | flops 12884901888 | bytes 4194304 | tf_op jit(solution)/shard_map/page_part/pallas_call | solution.py:319
  24.6 4.2 %collective-permute-done.2.refs_2_ = bf16[4,256,128]{2,1,0:T(8,128)(2,1)S(1)} collective-permute-done((bf16[4,256,128]{2,1,0:T(8,128)(2,1)S(1)}, bf16[4,256,128]{2,1,0:T(8,128)(2,1)S(1)}, u32[]{:S(2)}, u32[]{:S(2)}) %collective-permute-start.2) | collective-permute-done | bytes 262176 | tf_op jit(solution)/shard_map/ppermute | solution.py:426
  28.8 1.9 %pick.1 = (bf16[4,256,128]{2,1,0:T(8,128)(2,1)S(1)}, bf16[4,256,128]{2,1,0:T(8,128)(2,1)}, bf16[4,256,128]{2,1,0:T(8,128)(2,1)}, bf16[4,256,128]{2,1,0:T(8,128)(2,1)}) custom-call(s32[3]{0:T(128)S(1)} %pad_add_fusion.at_ref, bf16[4,256,128]{2,1,0:T(8,128)(2,1)S(1)} %copy-done, bf16[4,256,128]{2,1,0:T(8,128)(2,1)} %collective-permute-done.1.refs_1_, ...), custom_call_target="tpu_custom_call" | custom-call | tf_op jit(solution)/shard_map/pick/pallas_call | solution.py:217
  30.7 0.7 copy-done.4
  31.4 2.9 %collective-permute-start.4 = (bf16[4,256,128]{2,1,0:T(8,128)(2,1)}, bf16[4,256,128]{2,1,0:T(8,128)(2,1)S(1)}, u32[]{:S(2)}, u32[]{:S(2)}) collective-permute-start(bf16[4,256,128]{2,1,0:T(8,128)(2,1)} %get-tuple-element.25), channel_id=1, source_target_pairs={{1,0},{2,1},{3,2},{0,3},{5,4},{6,5},{7,6},{4,7},{9,8},{10,9},{11,1... | collective-permute-start | bytes 786440 | tf_op jit(solution)/shard_map/ppermute | solution.py:426
  34.3 0.6 collective-permute-start.5
  34.9 0.6 collective-permute-start.6
  35.4 2.5 %collective-permute-start.7 = (bf16[4,272,128]{2,1,0:T(8,128)(2,1)}, bf16[4,272,128]{2,1,0:T(8,128)(2,1)S(1)}, u32[]{:S(2)}, u32[]{:S(2)}) collective-permute-start(bf16[4,272,128]{2,1,0:T(8,128)(2,1)} %get-tuple-element.30.refs_0_), channel_id=1, source_target_pairs={{0,64},{32,96},{64,0},{96,32},{1,65},{33,97},{65,1},{97,33},{2,66}... | collective-permute-start | bytes 835592 | tf_op jit(solution)/shard_map/ppermute | solution.py:421
  37.9 0.5 collective-permute-start.8
  38.4 0.9 %copy-done.5 = bf16[4,256,128]{2,1,0:T(8,128)(2,1)S(1)} copy-done((bf16[4,256,128]{2,1,0:T(8,128)(2,1)S(1)}, bf16[4,256,128]{2,1,0:T(8,128)(2,1)}, u32[]{:S(2)}) %copy-start.5) | copy-done | bytes 262168
  39.4 5.7 %prefix_part.2.refs_4_ = bf16[4,272,128]{2,1,0:T(8,128)(2,1)S(1)} custom-call(s32[3]{0:T(128)S(1)} %pad_add_fusion.at_ref, bf16[4,256,128]{2,1,0:T(8,128)(2,1)S(1)} %copy-done.5, bf16[8,2,512,128]{3,2,1,0:T(8,128)(2,1)S(1)} %all-to-all-done.refs_1_.refs_3_), custom_call_target="tpu_custom_call" | custom-call | flops 4294967296 | bytes 8388608 | tf_op jit(solution)/shard_map/prefix_part/pallas_call | solution.py:130
  45.1 0.7 copy-done.2
  45.8 2.3 %collective-permute-start.9 = (bf16[4,272,128]{2,1,0:T(8,128)(2,1)}, bf16[4,272,128]{2,1,0:T(8,128)(2,1)S(1)}, u32[]{:S(2)}, u32[]{:S(2)}) collective-permute-start(bf16[4,272,128]{2,1,0:T(8,128)(2,1)} %get-tuple-element.33), channel_id=1, source_target_pairs={{0,32},{32,0},{64,96},{96,64},{1,33},{33,1},{65,97},{97,65},{2,34}... | collective-permute-start | bytes 835592 | tf_op jit(solution)/shard_map/ppermute | solution.py:421
  48.1 1.9 %collective-permute-done.6.refs_2_ = bf16[4,256,128]{2,1,0:T(8,128)(2,1)} collective-permute-done((bf16[4,256,128]{2,1,0:T(8,128)(2,1)}, bf16[4,256,128]{2,1,0:T(8,128)(2,1)}, u32[]{:S(2)}, u32[]{:S(2)}) %collective-permute-start.6) | collective-permute-done | bytes 262176 | tf_op jit(solution)/shard_map/ppermute | solution.py:426
  50.0 0.9 %copy-done.3 = bf16[4,256,128]{2,1,0:T(8,128)(2,1)S(1)} copy-done((bf16[4,256,128]{2,1,0:T(8,128)(2,1)S(1)}, bf16[4,256,128]{2,1,0:T(8,128)(2,1)}, u32[]{:S(2)}) %copy-start.3) | copy-done | bytes 262168
  51.0 17.5 %prefix_part.3 = bf16[16,272,128]{2,1,0:T(8,128)(2,1)} custom-call(s32[3]{0:T(128)S(1)} %pad_add_fusion.at_ref, bf16[4,256,128]{2,1,0:T(8,128)(2,1)S(1)} %copy-done.3, bf16[4,256,128]{2,1,0:T(8,128)(2,1)} %collective-permute-done.5.refs_1_, bf16[4,256,128]{2,1,0:T(8,128)(2,1)} %collective-permute-done.6.refs_2_, ...), custom_call_target="tpu_custom_call" | custom-call | flops 12884901888 | bytes 8388608 | tf_op jit(solution)/shard_map/prefix_part/pallas_call | solution.py:130
  68.5 4.0 %all-to-all-start.1 = ((bf16[16,272,128]{2,1,0:T(8,128)(2,1)}), bf16[16,272,128]{2,1,0:T(8,128)(2,1)S(1)}, u32[]{:S(2)}, u32[]{:S(2)}) async-start(bf16[16,272,128]{2,1,0:T(8,128)(2,1)} %prefix_part.3), calls=%async_computation.1 | async-start | bytes 2228224 | tf_op jit(solution)/shard_map/all_to_all | solution.py:451
  72.5 3.4 %page_part.4 = bf16[4,272,128]{2,1,0:T(8,128)(2,1)S(1)} custom-call(s32[3]{0:T(128)S(1)} %pad_add_fusion.at_ref, s32[1,24]{1,0:T(1,128)S(1)} %copy-done.1, bf16[4,272,128]{2,1,0:T(8,128)(2,1)S(1)} %collective-permute-done.7.refs_0_, bf16[2,128,512]{2,1,0:T(8,128)(2,1)S(1)} %pad.4.refs_2_.refs_1_, bf16[24,2,128,512]{3,2,1,0:T(8,128)(2,1)} %refs_7_.5, ...), custom_call_target="tpu_custom_call" | custom-call | flops 6442450944 | bytes 4194304 | tf_op jit(solution)/shard_map/page_part/pallas_call | solution.py:319
  75.9 2.5 %collective-permute-start.10 = (bf16[4,272,128]{2,1,0:T(8,128)(2,1)S(1)}, bf16[4,272,128]{2,1,0:T(8,128)(2,1)S(1)}, u32[]{:S(2)}, u32[]{:S(2)}) collective-permute-start(bf16[4,272,128]{2,1,0:T(8,128)(2,1)S(1)} %page_part.4), channel_id=1, source_target_pairs={{0,64},{32,96},{64,0},{96,32},{1,65},{33,97},{65,1},{97,33},{2,66}... | collective-permute-start | bytes 835592 | tf_op jit(solution)/shard_map/ppermute | solution.py:421
  78.5 4.1 %page_part.5 = bf16[4,272,128]{2,1,0:T(8,128)(2,1)} custom-call(s32[3]{0:T(128)S(1)} %pad_add_fusion.at_ref, s32[1,24]{1,0:T(1,128)S(1)} %copy-done.1, bf16[4,272,128]{2,1,0:T(8,128)(2,1)S(1)} %collective-permute-done.8.refs_0_, bf16[2,128,512]{2,1,0:T(8,128)(2,1)S(1)} %pad.4.refs_2_.refs_1_, bf16[24,2,128,512]{3,2,1,0:T(8,128)(2,1)} %refs_7_.5, ...), custom_call_target="tpu_custom_call" | custom-call | flops 6442450944 | bytes 4194304 | tf_op jit(solution)/shard_map/page_part/pallas_call | solution.py:319
  82.6 2.3 %collective-permute-start.11 = (bf16[4,272,128]{2,1,0:T(8,128)(2,1)}, bf16[4,272,128]{2,1,0:T(8,128)(2,1)S(1)}, u32[]{:S(2)}, u32[]{:S(2)}) collective-permute-start(bf16[4,272,128]{2,1,0:T(8,128)(2,1)} %page_part.5), channel_id=1, source_target_pairs={{0,96},{32,64},{64,32},{96,0},{1,97},{33,65},{65,33},{97,1},{2,98}... | collective-permute-start | bytes 835592 | tf_op jit(solution)/shard_map/ppermute | solution.py:421
  84.9 3.7 %all-to-all-done.1 = bf16[16,272,128]{2,1,0:T(8,128)(2,1)S(1)} async-done(((bf16[16,272,128]{2,1,0:T(8,128)(2,1)}), bf16[16,272,128]{2,1,0:T(8,128)(2,1)S(1)}, u32[]{:S(2)}, u32[]{:S(2)}) %all-to-all-start.1) | async-done | bytes 1114144 | tf_op jit(solution)/shard_map/all_to_all | solution.py:451
  88.6 1.7 %merge.1 = (f32[4,256,128]{2,1,0:T(8,128)S(1)}, f32[4,8,128]{2,1,0:T(8,128)S(1)}) custom-call(bf16[4,4,272,128]{3,2,1,0:T(8,128)(2,1)S(1)} %bitcast.9, bf16[4,272,128]{2,1,0:T(8,128)(2,1)S(1)} %get-tuple-element.22.rest_0_, bf16[4,272,128]{2,1,0:T(8,128)(2,1)S(1)} %collective-permute-done.9.rest_1_, bf16[4,272,128]{2,1,0:T(8,128)(2,1)S(1)} %collective-permute-done.10.rest_2_), custom_call_target="tpu_custom_call" | custom-call | tf_op jit(solution)/shard_map/merge/pallas_call | solution.py:396
  90.2 2.1 %collective-permute-done.11.page_ref = bf16[4,272,128]{2,1,0:T(8,128)(2,1)S(1)} collective-permute-done((bf16[4,272,128]{2,1,0:T(8,128)(2,1)}, bf16[4,272,128]{2,1,0:T(8,128)(2,1)S(1)}, u32[]{:S(2)}, u32[]{:S(2)}) %collective-permute-start.11) | collective-permute-done | bytes 278560 | tf_op jit(solution)/shard_map/ppermute | solution.py:421
  92.3 1.6 %merge_last.1 = bf16[4,4,8192]{2,1,0:T(4,128)(2,1)} custom-call(f32[4,256,128]{2,1,0:T(8,128)S(1)} %get-tuple-element.35.o_ref, f32[4,8,128]{2,1,0:T(8,128)S(1)} %get-tuple-element.36.stat_ref, bf16[4,272,128]{2,1,0:T(8,128)(2,1)S(1)} %collective-permute-done.11.page_ref), custom_call_target="tpu_custom_call" | custom-call | tf_op jit(solution)/shard_map/merge_last/pallas_call | solution.py:409
  (22 shorter events, 0.1 us)
Async XLA Ops:
  4.9 7.9 %copy-start = (bf16[4,256,128]{2,1,0:T(8,128)(2,1)S(1)}, bf16[4,256,128]{2,1,0:T(8,128)(2,1)}, u32[]{:S(2)}) copy-start(bf16[4,256,128]{2,1,0:T(8,128)(2,1)} %get-tuple-element.24.refs_0_) | copy-start | bytes 786436
  4.9 12.9 %copy-start.6 = (bf16[4,4,2,512]{3,2,1,0:T(2,128)(2,1)S(1)}, bf16[4,4,2,512]{3,2,1,0:T(2,128)(2,1)}, u32[]{:S(2)}) copy-start(bf16[4,4,2,512]{3,2,1,0:T(2,128)(2,1)} %param.10) | copy-start | bytes 98308
  4.9 13.0 %copy-start.1 = (s32[1,24]{1,0:T(1,128)S(1)}, s32[1,24]{1,0:T(1,128)}, u32[]{:S(2)}) copy-start(s32[1,24]{1,0:T(1,128)} %slot_ref.5) | copy-start | bytes 292
  4.9 33.5 %all-to-all-start = ((bf16[8,2,512,128]{3,2,1,0:T(8,128)(2,1)}), bf16[8,2,512,128]{3,2,1,0:T(8,128)(2,1)S(1)}, u32[]{:S(2)}, u32[]{:S(2)}) async-start(bf16[8,2,512,128]{3,2,1,0:T(8,128)(2,1)} %bitcast.10), calls=%async_computation | async-start | bytes 4194304 | tf_op jit(solution)/shard_map/all_to_all | solution.py:438
  11.8 6.1 %collective-permute-start = (bf16[4,272,128]{2,1,0:T(8,128)(2,1)}, bf16[4,272,128]{2,1,0:T(8,128)(2,1)}, u32[]{:S(2)}, u32[]{:S(2)}) collective-permute-start(bf16[4,272,128]{2,1,0:T(8,128)(2,1)} %get-tuple-element.30.refs_0_), channel_id=1, source_target_pairs={{0,32},{32,0},{64,96},{96,64},{1,33},{33,1},{65,97},{97,65},{2,34}... | collective-permute-start | bytes 835592 | tf_op jit(solution)/shard_map/ppermute | solution.py:421
  12.8 11.8 %collective-permute-start.3 = (bf16[4,256,128]{2,1,0:T(8,128)(2,1)S(1)}, bf16[4,256,128]{2,1,0:T(8,128)(2,1)S(1)}, u32[]{:S(2)}, u32[]{:S(2)}) collective-permute-start(bf16[4,256,128]{2,1,0:T(8,128)(2,1)S(1)} %copy-done), channel_id=1, source_target_pairs={{24,0},{0,8},{8,16},{16,24},{25,1},{1,9},{9,17},{17,25},{26,2},{2,... | collective-permute-start | bytes 786440 | tf_op jit(solution)/shard_map/ppermute | solution.py:426
  14.1 14.6 %collective-permute-start.2 = (bf16[4,256,128]{2,1,0:T(8,128)(2,1)S(1)}, bf16[4,256,128]{2,1,0:T(8,128)(2,1)S(1)}, u32[]{:S(2)}, u32[]{:S(2)}) collective-permute-start(bf16[4,256,128]{2,1,0:T(8,128)(2,1)S(1)} %copy-done), channel_id=1, source_target_pairs={{16,0},{24,8},{0,16},{8,24},{17,1},{25,9},{1,17},{9,25},{18,2},{26... | collective-permute-start | bytes 786440 | tf_op jit(solution)/shard_map/ppermute | solution.py:426
  16.7 12.0 %collective-permute-start.1 = (bf16[4,256,128]{2,1,0:T(8,128)(2,1)S(1)}, bf16[4,256,128]{2,1,0:T(8,128)(2,1)}, u32[]{:S(2)}, u32[]{:S(2)}) collective-permute-start(bf16[4,256,128]{2,1,0:T(8,128)(2,1)S(1)} %copy-done), channel_id=1, source_target_pairs={{8,0},{16,8},{24,16},{0,24},{9,1},{17,9},{25,17},{1,25},{10,2},{18... | collective-permute-start | bytes 786440 | tf_op jit(solution)/shard_map/ppermute | solution.py:426
  30.7 0.7 copy-start.4
  31.4 13.8 %collective-permute-start.4 = (bf16[4,256,128]{2,1,0:T(8,128)(2,1)}, bf16[4,256,128]{2,1,0:T(8,128)(2,1)S(1)}, u32[]{:S(2)}, u32[]{:S(2)}) collective-permute-start(bf16[4,256,128]{2,1,0:T(8,128)(2,1)} %get-tuple-element.25), channel_id=1, source_target_pairs={{1,0},{2,1},{3,2},{0,3},{5,4},{6,5},{7,6},{4,7},{9,8},{10,9},{11,1... | collective-permute-start | bytes 786440 | tf_op jit(solution)/shard_map/ppermute | solution.py:426
  34.3 13.8 %collective-permute-start.5 = (bf16[4,256,128]{2,1,0:T(8,128)(2,1)}, bf16[4,256,128]{2,1,0:T(8,128)(2,1)}, u32[]{:S(2)}, u32[]{:S(2)}) collective-permute-start(bf16[4,256,128]{2,1,0:T(8,128)(2,1)} %get-tuple-element.26), channel_id=1, source_target_pairs={{2,0},{3,1},{0,2},{1,3},{6,4},{7,5},{4,6},{5,7},{10,8},{11,9},{8,1... | collective-permute-start | bytes 786440 | tf_op jit(solution)/shard_map/ppermute | solution.py:426
  34.9 15.2 %collective-permute-start.6 = (bf16[4,256,128]{2,1,0:T(8,128)(2,1)}, bf16[4,256,128]{2,1,0:T(8,128)(2,1)}, u32[]{:S(2)}, u32[]{:S(2)}) collective-permute-start(bf16[4,256,128]{2,1,0:T(8,128)(2,1)} %get-tuple-element.27), channel_id=1, source_target_pairs={{3,0},{0,1},{1,2},{2,3},{7,4},{4,5},{5,6},{6,7},{11,8},{8,9},{9,10... | collective-permute-start | bytes 786440 | tf_op jit(solution)/shard_map/ppermute | solution.py:426
  35.4 33.1 %collective-permute-start.7 = (bf16[4,272,128]{2,1,0:T(8,128)(2,1)}, bf16[4,272,128]{2,1,0:T(8,128)(2,1)S(1)}, u32[]{:S(2)}, u32[]{:S(2)}) collective-permute-start(bf16[4,272,128]{2,1,0:T(8,128)(2,1)} %get-tuple-element.30.refs_0_), channel_id=1, source_target_pairs={{0,64},{32,96},{64,0},{96,32},{1,65},{33,97},{65,1},{97,33},{2,66}... | collective-permute-start | bytes 835592 | tf_op jit(solution)/shard_map/ppermute | solution.py:421
  37.9 30.6 %collective-permute-start.8 = (bf16[4,272,128]{2,1,0:T(8,128)(2,1)}, bf16[4,272,128]{2,1,0:T(8,128)(2,1)S(1)}, u32[]{:S(2)}, u32[]{:S(2)}) collective-permute-start(bf16[4,272,128]{2,1,0:T(8,128)(2,1)} %collective-permute-done.refs_1_), channel_id=1, source_target_pairs={{0,64},{32,96},{64,0},{96,32},{1,65},{33,97},{65,1},{97,33},{2,66}... | collective-permute-start | bytes 835592 | tf_op jit(solution)/shard_map/ppermute | solution.py:421
  38.4 1.0 %copy-start.5 = (bf16[4,256,128]{2,1,0:T(8,128)(2,1)S(1)}, bf16[4,256,128]{2,1,0:T(8,128)(2,1)}, u32[]{:S(2)}) copy-start(bf16[4,256,128]{2,1,0:T(8,128)(2,1)} %copy-done.4) | copy-start | bytes 786436
  45.1 0.7 copy-start.2
  45.8 39.0 %collective-permute-start.9 = (bf16[4,272,128]{2,1,0:T(8,128)(2,1)}, bf16[4,272,128]{2,1,0:T(8,128)(2,1)S(1)}, u32[]{:S(2)}, u32[]{:S(2)}) collective-permute-start(bf16[4,272,128]{2,1,0:T(8,128)(2,1)} %get-tuple-element.33), channel_id=1, source_target_pairs={{0,32},{32,0},{64,96},{96,64},{1,33},{33,1},{65,97},{97,65},{2,34}... | collective-permute-start | bytes 835592 | tf_op jit(solution)/shard_map/ppermute | solution.py:421
  50.0 1.0 %copy-start.3 = (bf16[4,256,128]{2,1,0:T(8,128)(2,1)S(1)}, bf16[4,256,128]{2,1,0:T(8,128)(2,1)}, u32[]{:S(2)}) copy-start(bf16[4,256,128]{2,1,0:T(8,128)(2,1)} %copy-done.2) | copy-start | bytes 786436
  68.5 20.0 %all-to-all-start.1 = ((bf16[16,272,128]{2,1,0:T(8,128)(2,1)}), bf16[16,272,128]{2,1,0:T(8,128)(2,1)S(1)}, u32[]{:S(2)}, u32[]{:S(2)}) async-start(bf16[16,272,128]{2,1,0:T(8,128)(2,1)} %prefix_part.3), calls=%async_computation.1 | async-start | bytes 2228224 | tf_op jit(solution)/shard_map/all_to_all | solution.py:451
  75.9 8.9 %collective-permute-start.10 = (bf16[4,272,128]{2,1,0:T(8,128)(2,1)S(1)}, bf16[4,272,128]{2,1,0:T(8,128)(2,1)S(1)}, u32[]{:S(2)}, u32[]{:S(2)}) collective-permute-start(bf16[4,272,128]{2,1,0:T(8,128)(2,1)S(1)} %page_part.4), channel_id=1, source_target_pairs={{0,64},{32,96},{64,0},{96,32},{1,65},{33,97},{65,1},{97,33},{2,66}... | collective-permute-start | bytes 835592 | tf_op jit(solution)/shard_map/ppermute | solution.py:421
  82.6 9.7 %collective-permute-start.11 = (bf16[4,272,128]{2,1,0:T(8,128)(2,1)}, bf16[4,272,128]{2,1,0:T(8,128)(2,1)S(1)}, u32[]{:S(2)}, u32[]{:S(2)}) collective-permute-start(bf16[4,272,128]{2,1,0:T(8,128)(2,1)} %page_part.5), channel_id=1, source_target_pairs={{0,96},{32,64},{64,32},{96,0},{1,97},{33,65},{65,33},{97,1},{2,98}... | collective-permute-start | bytes 835592 | tf_op jit(solution)/shard_map/ppermute | solution.py:421

commit v8 on v7

--- a/solution.py
+++ b/solution.py
@@ -20,6 +20,7 @@
 ROWS = RS * GQA
 PACK = ROWS + 16
 FLOOR = -1e29
+HEADS = 2
 LOWEST = -1e30
 LOG2 = math.log2(math.e) / math.sqrt(HD)
 AXES = ("grp", "y", "xl", "z")
@@ -150,15 +151,19 @@
 
 
 def prep_kernel(table_ref, size_ref, q_ref, kv_ref, asked_ref, rows_ref, dealt_ref):
-    for c in range(GQA):
-        tile = q_ref[:, :, c * HD : (c + 1) * HD].reshape(RS, HD)
-        asked_ref[0, c * RS : (c + 1) * RS, :] = tile
-        rows_ref[0, c * RS : (c + 1) * RS, :] = tile
-    both = kv_ref[0].astype(F32)
-    for i in range(2):
-        half = both[:, i].astype(BF16)
-        dealt_ref[0, 0, i] = half
-        dealt_ref[1, 0, i] = half
+    for head in range(HEADS):
+        for c in range(GQA):
+            col = (head * GQA + c) * HD
+            tile = q_ref[:, :, col : col + HD].reshape(RS, HD)
+            asked_ref[head, c * RS : (c + 1) * RS, :] = tile
+            rows_ref[head, c * RS : (c + 1) * RS, :] = tile
+        both = kv_ref[0, :, :, head * HD : (head + 1) * HD].astype(F32)
+        for i in range(2):
+            half = both[:, i].astype(BF16)
+            dealt_ref[0, head, i] = half
+            dealt_ref[1, head, i] = half
+        if head:
+            asked_ref[head, ROWS:, :] = jnp.zeros((16, HD), BF16)
 
     @pl.when(pl.program_id(0) == 0)
     def _():
@@ -181,17 +186,17 @@
     tokens = prefix_kv.shape[1]
     return pl.pallas_call(
         prep_kernel,
-        grid=(KVH,),
+        grid=(KVH // HEADS,),
         in_specs=[
             pl.BlockSpec(page_table.shape, lambda k: (0, 0)),
             pl.BlockSpec((1, REQ), lambda k: (0, 0)),
-            pl.BlockSpec((REQ, STEPS, GQA * HD), lambda k: (0, 0, k)),
-            pl.BlockSpec((1, tokens, 2, HD), lambda k: (0, 0, 0, k)),
+            pl.BlockSpec((REQ, STEPS, HEADS * GQA * HD), lambda k: (0, 0, k)),
+            pl.BlockSpec((1, tokens, 2, HEADS * HD), lambda k: (0, 0, 0, k)),
         ],
         out_specs=[
-            pl.BlockSpec((1, PACK, HD), lambda k: (k, 0, 0)),
-            pl.BlockSpec((1, ROWS, HD), lambda k: (k, 0, 0)),
-            pl.BlockSpec((2, 1, 2, tokens, HD), lambda k: (0, k, 0, 0, 0)),
+            pl.BlockSpec((HEADS, PACK, HD), lambda k: (k, 0, 0)),
+            pl.BlockSpec((HEADS, ROWS, HD), lambda k: (k, 0, 0)),
+            pl.BlockSpec((2, HEADS, 2, tokens, HD), lambda k: (0, k, 0, 0, 0)),
         ],
         out_shape=[
             jax.ShapeDtypeStruct((KVH, PACK, HD), BF16),

time: 95.1 us -> 94.6 us (level)
  no operation moved by 1% of the time
where the time goes in v8:
time: 94.6 us; the launch traced here: 93.4 us
  Pallas kernels  47 us (50%)
  starting transfers between devices  31.1 us (33%)
  waiting for transfers between devices  11.9 us (13%)
  local copies, waits for them, and re-layouts  3.33 us (4%)
    pallas_call x2, Pallas kernels, prefix_part(): pl.pallas_call(functools.partial(prefix_kernel, count=count, per=per, til...  23.3 us
    pallas_call x3, Pallas kernels, page_part(): pl.pallas_call(functools.partial(page_kernel, first=first), grid_spec=plt...  14.1 us
    ppermute x6, starting transfers between devices, swap(): lax.ppermute(x, axis, [(i, i ^ mask) for i in range(lax.axis_size(axis))])  11 us
    ppermute x6, starting transfers between devices, fetch(): return lax.ppermute(x, axis, [((i + by) % n, i) for i in range(n)])  9.09 us
    all_to_all x1, starting transfers between devices, local(): kv_all = lax.all_to_all(dealt, ('xl', 'z'), 0, 0, tiled=True)  6.93 us
    ppermute x6, waiting for transfers between devices, fetch(): return lax.ppermute(x, axis, [((i + by) % n, i) for i in range(n)])  6.11 us
    pallas_call x1, Pallas kernels, prep(): pl.pallas_call(prep_kernel, grid=(KVH // HEADS,), in_specs=[pl.BlockSpec(...  4.46 us
    all_to_all x1, starting transfers between devices, local(): moved = lax.all_to_all(part, ('z', 'y'), 0, 0, tiled=True)  4.01 us
  transfers between devices with their start and end apart: 14, of which 4 were waited for; matrix products, arithmetic and copies ran while one was open for 0% of the time, Pallas kernels for 44%

profile of v8, /device:TPU:1, one launch (start us, length us, event | category | flops | bytes accessed | tf_op | source)
XLA Modules:
  0.0 93.4 jit_solution(15222458890230358008)
XLA Ops:
  0.0 4.5 %prep.1 = (bf16[4,272,128]{2,1,0:T(8,128)(2,1)}, bf16[4,256,128]{2,1,0:T(8,128)(2,1)}, bf16[2,4,2,512,128]{4,3,2,1,0:T(8,128)(2,1)}) custom-call(s32[1,24]{1,0:T(1,128)} %table_ref.1, s32[1,4]{1,0:T(1,128)} %bitcast.12, bf16[4,4,8192]{2,1,0:T(4,128)(2,1)} %q_ref.1, bf16[1,512,2,512]{3,2,1,0:T(2,128)(2,1)} %kv_ref.1), custom_call_target="tpu_custom_call" | custom-call | tf_op jit(solution)/shard_map/prep/pallas_call | solution.py:187
  4.5 6.9 %all-to-all-start = ((bf16[8,2,512,128]{3,2,1,0:T(8,128)(2,1)}), bf16[8,2,512,128]{3,2,1,0:T(8,128)(2,1)S(1)}, u32[]{:S(2)}, u32[]{:S(2)}) async-start(bf16[8,2,512,128]{3,2,1,0:T(8,128)(2,1)} %bitcast.10), calls=%async_computation | async-start | bytes 4194304 | tf_op jit(solution)/shard_map/all_to_all | solution.py:443
  11.4 1.0 %collective-permute-start = (bf16[4,272,128]{2,1,0:T(8,128)(2,1)}, bf16[4,272,128]{2,1,0:T(8,128)(2,1)}, u32[]{:S(2)}, u32[]{:S(2)}) collective-permute-start(bf16[4,272,128]{2,1,0:T(8,128)(2,1)} %get-tuple-element.30.refs_0_), channel_id=1, source_target_pairs={{0,32},{32,0},{64,96},{96,64},{1,33},{33,1},{65,97},{97,65},{2,34}... | collective-permute-start | bytes 835592 | tf_op jit(solution)/shard_map/ppermute | solution.py:426
  12.4 1.3 %collective-permute-start.3 = (bf16[4,256,128]{2,1,0:T(8,128)(2,1)S(1)}, bf16[4,256,128]{2,1,0:T(8,128)(2,1)S(1)}, u32[]{:S(2)}, u32[]{:S(2)}) collective-permute-start(bf16[4,256,128]{2,1,0:T(8,128)(2,1)S(1)} %copy-done), channel_id=1, source_target_pairs={{24,0},{0,8},{8,16},{16,24},{25,1},{1,9},{9,17},{17,25},{26,2},{2,... | collective-permute-start | bytes 786440 | tf_op jit(solution)/shard_map/ppermute | solution.py:431
  13.7 2.6 %collective-permute-start.2 = (bf16[4,256,128]{2,1,0:T(8,128)(2,1)S(1)}, bf16[4,256,128]{2,1,0:T(8,128)(2,1)S(1)}, u32[]{:S(2)}, u32[]{:S(2)}) collective-permute-start(bf16[4,256,128]{2,1,0:T(8,128)(2,1)S(1)} %copy-done), channel_id=1, source_target_pairs={{16,0},{24,8},{0,16},{8,24},{17,1},{25,9},{1,17},{9,25},{18,2},{26... | collective-permute-start | bytes 786440 | tf_op jit(solution)/shard_map/ppermute | solution.py:431
  16.3 1.1 %collective-permute-start.1 = (bf16[4,256,128]{2,1,0:T(8,128)(2,1)S(1)}, bf16[4,256,128]{2,1,0:T(8,128)(2,1)}, u32[]{:S(2)}, u32[]{:S(2)}) collective-permute-start(bf16[4,256,128]{2,1,0:T(8,128)(2,1)S(1)} %copy-done), channel_id=1, source_target_pairs={{8,0},{16,8},{24,16},{0,24},{9,1},{17,9},{25,17},{1,25},{10,2},{18... | collective-permute-start | bytes 786440 | tf_op jit(solution)/shard_map/ppermute | solution.py:431
  17.4 0.1 pad_add_fusion.at_ref
  17.5 6.6 %page_part.3 = (bf16[4,272,128]{2,1,0:T(8,128)(2,1)S(1)}, bf16[4,272,128]{2,1,0:T(8,128)(2,1)}) custom-call(s32[3]{0:T(128)S(1)} %pad_add_fusion.at_ref, s32[1,24]{1,0:T(1,128)S(1)} %copy-done.1, bf16[4,272,128]{2,1,0:T(8,128)(2,1)} %get-tuple-element.30.refs_0_, bf16[4,272,128]{2,1,0:T(8,128)(2,1)} %collective-permute-done.refs_1_, ...), custom_call_target="tpu_custom_call" | custom-call | flops 12884901888 | bytes 4194304 | tf_op jit(solution)/shard_map/page_part/pallas_call | solution.py:324
  24.1 4.2 %collective-permute-done.2.refs_2_ = bf16[4,256,128]{2,1,0:T(8,128)(2,1)S(1)} collective-permute-done((bf16[4,256,128]{2,1,0:T(8,128)(2,1)S(1)}, bf16[4,256,128]{2,1,0:T(8,128)(2,1)S(1)}, u32[]{:S(2)}, u32[]{:S(2)}) %collective-permute-start.2) | collective-permute-done | bytes 262176 | tf_op jit(solution)/shard_map/ppermute | solution.py:431
  28.3 1.9 %pick.1 = (bf16[4,256,128]{2,1,0:T(8,128)(2,1)S(1)}, bf16[4,256,128]{2,1,0:T(8,128)(2,1)}, bf16[4,256,128]{2,1,0:T(8,128)(2,1)}, bf16[4,256,128]{2,1,0:T(8,128)(2,1)}) custom-call(s32[3]{0:T(128)S(1)} %pad_add_fusion.at_ref, bf16[4,256,128]{2,1,0:T(8,128)(2,1)S(1)} %copy-done, bf16[4,256,128]{2,1,0:T(8,128)(2,1)} %collective-permute-done.1.refs_1_, ...), custom_call_target="tpu_custom_call" | custom-call | tf_op jit(solution)/shard_map/pick/pallas_call | solution.py:222
  30.2 0.7 copy-done.4
  30.9 2.9 %collective-permute-start.4 = (bf16[4,256,128]{2,1,0:T(8,128)(2,1)}, bf16[4,256,128]{2,1,0:T(8,128)(2,1)S(1)}, u32[]{:S(2)}, u32[]{:S(2)}) collective-permute-start(bf16[4,256,128]{2,1,0:T(8,128)(2,1)} %get-tuple-element.25), channel_id=1, source_target_pairs={{1,0},{2,1},{3,2},{0,3},{5,4},{6,5},{7,6},{4,7},{9,8},{10,9},{11,1... | collective-permute-start | bytes 786440 | tf_op jit(solution)/shard_map/ppermute | solution.py:431
  33.9 0.6 collective-permute-start.5
  34.4 0.6 collective-permute-start.6
  35.0 2.5 %collective-permute-start.7 = (bf16[4,272,128]{2,1,0:T(8,128)(2,1)}, bf16[4,272,128]{2,1,0:T(8,128)(2,1)S(1)}, u32[]{:S(2)}, u32[]{:S(2)}) collective-permute-start(bf16[4,272,128]{2,1,0:T(8,128)(2,1)} %get-tuple-element.30.refs_0_), channel_id=1, source_target_pairs={{0,64},{32,96},{64,0},{96,32},{1,65},{33,97},{65,1},{97,33},{2,66}... | collective-permute-start | bytes 835592 | tf_op jit(solution)/shard_map/ppermute | solution.py:426
  37.5 0.5 collective-permute-start.8
  38.0 0.9 %copy-done.5 = bf16[4,256,128]{2,1,0:T(8,128)(2,1)S(1)} copy-done((bf16[4,256,128]{2,1,0:T(8,128)(2,1)S(1)}, bf16[4,256,128]{2,1,0:T(8,128)(2,1)}, u32[]{:S(2)}) %copy-start.5) | copy-done | bytes 262168
  38.9 5.7 %prefix_part.2.refs_4_ = bf16[4,272,128]{2,1,0:T(8,128)(2,1)S(1)} custom-call(s32[3]{0:T(128)S(1)} %pad_add_fusion.at_ref, bf16[4,256,128]{2,1,0:T(8,128)(2,1)S(1)} %copy-done.5, bf16[8,2,512,128]{3,2,1,0:T(8,128)(2,1)S(1)} %all-to-all-done.refs_1_.refs_3_), custom_call_target="tpu_custom_call" | custom-call | flops 4294967296 | bytes 8388608 | tf_op jit(solution)/shard_map/prefix_part/pallas_call | solution.py:131
  44.7 0.7 copy-done.2
  45.4 2.3 %collective-permute-start.9 = (bf16[4,272,128]{2,1,0:T(8,128)(2,1)}, bf16[4,272,128]{2,1,0:T(8,128)(2,1)S(1)}, u32[]{:S(2)}, u32[]{:S(2)}) collective-permute-start(bf16[4,272,128]{2,1,0:T(8,128)(2,1)} %get-tuple-element.33), channel_id=1, source_target_pairs={{0,32},{32,0},{64,96},{96,64},{1,33},{33,1},{65,97},{97,65},{2,34}... | collective-permute-start | bytes 835592 | tf_op jit(solution)/shard_map/ppermute | solution.py:426
  47.7 1.9 %collective-permute-done.6.refs_2_ = bf16[4,256,128]{2,1,0:T(8,128)(2,1)} collective-permute-done((bf16[4,256,128]{2,1,0:T(8,128)(2,1)}, bf16[4,256,128]{2,1,0:T(8,128)(2,1)}, u32[]{:S(2)}, u32[]{:S(2)}) %collective-permute-start.6) | collective-permute-done | bytes 262176 | tf_op jit(solution)/shard_map/ppermute | solution.py:431
  49.6 0.9 %copy-done.3 = bf16[4,256,128]{2,1,0:T(8,128)(2,1)S(1)} copy-done((bf16[4,256,128]{2,1,0:T(8,128)(2,1)S(1)}, bf16[4,256,128]{2,1,0:T(8,128)(2,1)}, u32[]{:S(2)}) %copy-start.3) | copy-done | bytes 262168
  50.5 17.5 %prefix_part.3 = bf16[16,272,128]{2,1,0:T(8,128)(2,1)} custom-call(s32[3]{0:T(128)S(1)} %pad_add_fusion.at_ref, bf16[4,256,128]{2,1,0:T(8,128)(2,1)S(1)} %copy-done.3, bf16[4,256,128]{2,1,0:T(8,128)(2,1)} %collective-permute-done.5.refs_1_, bf16[4,256,128]{2,1,0:T(8,128)(2,1)} %collective-permute-done.6.refs_2_, ...), custom_call_target="tpu_custom_call" | custom-call | flops 12884901888 | bytes 8388608 | tf_op jit(solution)/shard_map/prefix_part/pallas_call | solution.py:131
  68.1 4.0 %all-to-all-start.1 = ((bf16[16,272,128]{2,1,0:T(8,128)(2,1)}), bf16[16,272,128]{2,1,0:T(8,128)(2,1)S(1)}, u32[]{:S(2)}, u32[]{:S(2)}) async-start(bf16[16,272,128]{2,1,0:T(8,128)(2,1)} %prefix_part.3), calls=%async_computation.1 | async-start | bytes 2228224 | tf_op jit(solution)/shard_map/all_to_all | solution.py:456
  72.1 3.4 %page_part.4 = bf16[4,272,128]{2,1,0:T(8,128)(2,1)S(1)} custom-call(s32[3]{0:T(128)S(1)} %pad_add_fusion.at_ref, s32[1,24]{1,0:T(1,128)S(1)} %copy-done.1, bf16[4,272,128]{2,1,0:T(8,128)(2,1)S(1)} %collective-permute-done.7.refs_0_, bf16[2,128,512]{2,1,0:T(8,128)(2,1)S(1)} %pad.4.refs_2_.refs_1_, bf16[24,2,128,512]{3,2,1,0:T(8,128)(2,1)} %refs_7_.5, ...), custom_call_target="tpu_custom_call" | custom-call | flops 6442450944 | bytes 4194304 | tf_op jit(solution)/shard_map/page_part/pallas_call | solution.py:324
  75.5 2.5 %collective-permute-start.10 = (bf16[4,272,128]{2,1,0:T(8,128)(2,1)S(1)}, bf16[4,272,128]{2,1,0:T(8,128)(2,1)S(1)}, u32[]{:S(2)}, u32[]{:S(2)}) collective-permute-start(bf16[4,272,128]{2,1,0:T(8,128)(2,1)S(1)} %page_part.4), channel_id=1, source_target_pairs={{0,64},{32,96},{64,0},{96,32},{1,65},{33,97},{65,1},{97,33},{2,66}... | collective-permute-start | bytes 835592 | tf_op jit(solution)/shard_map/ppermute | solution.py:426
  78.0 4.1 %page_part.5 = bf16[4,272,128]{2,1,0:T(8,128)(2,1)} custom-call(s32[3]{0:T(128)S(1)} %pad_add_fusion.at_ref, s32[1,24]{1,0:T(1,128)S(1)} %copy-done.1, bf16[4,272,128]{2,1,0:T(8,128)(2,1)S(1)} %collective-permute-done.8.refs_0_, bf16[2,128,512]{2,1,0:T(8,128)(2,1)S(1)} %pad.4.refs_2_.refs_1_, bf16[24,2,128,512]{3,2,1,0:T(8,128)(2,1)} %refs_7_.5, ...), custom_call_target="tpu_custom_call" | custom-call | flops 6442450944 | bytes 4194304 | tf_op jit(solution)/shard_map/page_part/pallas_call | solution.py:324
  82.1 2.3 %collective-permute-start.11 = (bf16[4,272,128]{2,1,0:T(8,128)(2,1)}, bf16[4,272,128]{2,1,0:T(8,128)(2,1)S(1)}, u32[]{:S(2)}, u32[]{:S(2)}) collective-permute-start(bf16[4,272,128]{2,1,0:T(8,128)(2,1)} %page_part.5), channel_id=1, source_target_pairs={{0,96},{32,64},{64,32},{96,0},{1,97},{33,65},{65,33},{97,1},{2,98}... | collective-permute-start | bytes 835592 | tf_op jit(solution)/shard_map/ppermute | solution.py:426
  84.4 3.7 %all-to-all-done.1 = bf16[16,272,128]{2,1,0:T(8,128)(2,1)S(1)} async-done(((bf16[16,272,128]{2,1,0:T(8,128)(2,1)}), bf16[16,272,128]{2,1,0:T(8,128)(2,1)S(1)}, u32[]{:S(2)}, u32[]{:S(2)}) %all-to-all-start.1) | async-done | bytes 1114144 | tf_op jit(solution)/shard_map/all_to_all | solution.py:456
  88.1 1.7 %merge.1 = (f32[4,256,128]{2,1,0:T(8,128)S(1)}, f32[4,8,128]{2,1,0:T(8,128)S(1)}) custom-call(bf16[4,4,272,128]{3,2,1,0:T(8,128)(2,1)S(1)} %bitcast.9, bf16[4,272,128]{2,1,0:T(8,128)(2,1)S(1)} %get-tuple-element.22.rest_0_, bf16[4,272,128]{2,1,0:T(8,128)(2,1)S(1)} %collective-permute-done.9.rest_1_, bf16[4,272,128]{2,1,0:T(8,128)(2,1)S(1)} %collective-permute-done.10.rest_2_), custom_call_target="tpu_custom_call" | custom-call | tf_op jit(solution)/shard_map/merge/pallas_call | solution.py:401
  89.8 2.1 %collective-permute-done.11.page_ref = bf16[4,272,128]{2,1,0:T(8,128)(2,1)S(1)} collective-permute-done((bf16[4,272,128]{2,1,0:T(8,128)(2,1)}, bf16[4,272,128]{2,1,0:T(8,128)(2,1)S(1)}, u32[]{:S(2)}, u32[]{:S(2)}) %collective-permute-start.11) | collective-permute-done | bytes 278560 | tf_op jit(solution)/shard_map/ppermute | solution.py:426
  91.9 1.6 %merge_last.1 = bf16[4,4,8192]{2,1,0:T(4,128)(2,1)} custom-call(f32[4,256,128]{2,1,0:T(8,128)S(1)} %get-tuple-element.35.o_ref, f32[4,8,128]{2,1,0:T(8,128)S(1)} %get-tuple-element.36.stat_ref, bf16[4,272,128]{2,1,0:T(8,128)(2,1)S(1)} %collective-permute-done.11.page_ref), custom_call_target="tpu_custom_call" | custom-call | tf_op jit(solution)/shard_map/merge_last/pallas_call | solution.py:414
  (22 shorter events, 0.1 us)
Async XLA Ops:
  4.5 7.9 %copy-start = (bf16[4,256,128]{2,1,0:T(8,128)(2,1)S(1)}, bf16[4,256,128]{2,1,0:T(8,128)(2,1)}, u32[]{:S(2)}) copy-start(bf16[4,256,128]{2,1,0:T(8,128)(2,1)} %get-tuple-element.24.refs_0_) | copy-start | bytes 786436
  4.5 12.9 %copy-start.6 = (bf16[4,4,2,512]{3,2,1,0:T(2,128)(2,1)S(1)}, bf16[4,4,2,512]{3,2,1,0:T(2,128)(2,1)}, u32[]{:S(2)}) copy-start(bf16[4,4,2,512]{3,2,1,0:T(2,128)(2,1)} %param.10) | copy-start | bytes 98308
  4.5 13.0 %copy-start.1 = (s32[1,24]{1,0:T(1,128)S(1)}, s32[1,24]{1,0:T(1,128)}, u32[]{:S(2)}) copy-start(s32[1,24]{1,0:T(1,128)} %slot_ref.5) | copy-start | bytes 292
  4.5 33.5 %all-to-all-start = ((bf16[8,2,512,128]{3,2,1,0:T(8,128)(2,1)}), bf16[8,2,512,128]{3,2,1,0:T(8,128)(2,1)S(1)}, u32[]{:S(2)}, u32[]{:S(2)}) async-start(bf16[8,2,512,128]{3,2,1,0:T(8,128)(2,1)} %bitcast.10), calls=%async_computation | async-start | bytes 4194304 | tf_op jit(solution)/shard_map/all_to_all | solution.py:443
  11.4 6.1 %collective-permute-start = (bf16[4,272,128]{2,1,0:T(8,128)(2,1)}, bf16[4,272,128]{2,1,0:T(8,128)(2,1)}, u32[]{:S(2)}, u32[]{:S(2)}) collective-permute-start(bf16[4,272,128]{2,1,0:T(8,128)(2,1)} %get-tuple-element.30.refs_0_), channel_id=1, source_target_pairs={{0,32},{32,0},{64,96},{96,64},{1,33},{33,1},{65,97},{97,65},{2,34}... | collective-permute-start | bytes 835592 | tf_op jit(solution)/shard_map/ppermute | solution.py:426
  12.4 11.8 %collective-permute-start.3 = (bf16[4,256,128]{2,1,0:T(8,128)(2,1)S(1)}, bf16[4,256,128]{2,1,0:T(8,128)(2,1)S(1)}, u32[]{:S(2)}, u32[]{:S(2)}) collective-permute-start(bf16[4,256,128]{2,1,0:T(8,128)(2,1)S(1)} %copy-done), channel_id=1, source_target_pairs={{24,0},{0,8},{8,16},{16,24},{25,1},{1,9},{9,17},{17,25},{26,2},{2,... | collective-permute-start | bytes 786440 | tf_op jit(solution)/shard_map/ppermute | solution.py:431
  13.7 14.6 %collective-permute-start.2 = (bf16[4,256,128]{2,1,0:T(8,128)(2,1)S(1)}, bf16[4,256,128]{2,1,0:T(8,128)(2,1)S(1)}, u32[]{:S(2)}, u32[]{:S(2)}) collective-permute-start(bf16[4,256,128]{2,1,0:T(8,128)(2,1)S(1)} %copy-done), channel_id=1, source_target_pairs={{16,0},{24,8},{0,16},{8,24},{17,1},{25,9},{1,17},{9,25},{18,2},{26... | collective-permute-start | bytes 786440 | tf_op jit(solution)/shard_map/ppermute | solution.py:431
  16.3 12.0 %collective-permute-start.1 = (bf16[4,256,128]{2,1,0:T(8,128)(2,1)S(1)}, bf16[4,256,128]{2,1,0:T(8,128)(2,1)}, u32[]{:S(2)}, u32[]{:S(2)}) collective-permute-start(bf16[4,256,128]{2,1,0:T(8,128)(2,1)S(1)} %copy-done), channel_id=1, source_target_pairs={{8,0},{16,8},{24,16},{0,24},{9,1},{17,9},{25,17},{1,25},{10,2},{18... | collective-permute-start | bytes 786440 | tf_op jit(solution)/shard_map/ppermute | solution.py:431
  30.2 0.7 copy-start.4
  30.9 13.8 %collective-permute-start.4 = (bf16[4,256,128]{2,1,0:T(8,128)(2,1)}, bf16[4,256,128]{2,1,0:T(8,128)(2,1)S(1)}, u32[]{:S(2)}, u32[]{:S(2)}) collective-permute-start(bf16[4,256,128]{2,1,0:T(8,128)(2,1)} %get-tuple-element.25), channel_id=1, source_target_pairs={{1,0},{2,1},{3,2},{0,3},{5,4},{6,5},{7,6},{4,7},{9,8},{10,9},{11,1... | collective-permute-start | bytes 786440 | tf_op jit(solution)/shard_map/ppermute | solution.py:431
  33.9 13.8 %collective-permute-start.5 = (bf16[4,256,128]{2,1,0:T(8,128)(2,1)}, bf16[4,256,128]{2,1,0:T(8,128)(2,1)}, u32[]{:S(2)}, u32[]{:S(2)}) collective-permute-start(bf16[4,256,128]{2,1,0:T(8,128)(2,1)} %get-tuple-element.26), channel_id=1, source_target_pairs={{2,0},{3,1},{0,2},{1,3},{6,4},{7,5},{4,6},{5,7},{10,8},{11,9},{8,1... | collective-permute-start | bytes 786440 | tf_op jit(solution)/shard_map/ppermute | solution.py:431
  34.4 15.2 %collective-permute-start.6 = (bf16[4,256,128]{2,1,0:T(8,128)(2,1)}, bf16[4,256,128]{2,1,0:T(8,128)(2,1)}, u32[]{:S(2)}, u32[]{:S(2)}) collective-permute-start(bf16[4,256,128]{2,1,0:T(8,128)(2,1)} %get-tuple-element.27), channel_id=1, source_target_pairs={{3,0},{0,1},{1,2},{2,3},{7,4},{4,5},{5,6},{6,7},{11,8},{8,9},{9,10... | collective-permute-start | bytes 786440 | tf_op jit(solution)/shard_map/ppermute | solution.py:431
  35.0 33.1 %collective-permute-start.7 = (bf16[4,272,128]{2,1,0:T(8,128)(2,1)}, bf16[4,272,128]{2,1,0:T(8,128)(2,1)S(1)}, u32[]{:S(2)}, u32[]{:S(2)}) collective-permute-start(bf16[4,272,128]{2,1,0:T(8,128)(2,1)} %get-tuple-element.30.refs_0_), channel_id=1, source_target_pairs={{0,64},{32,96},{64,0},{96,32},{1,65},{33,97},{65,1},{97,33},{2,66}... | collective-permute-start | bytes 835592 | tf_op jit(solution)/shard_map/ppermute | solution.py:426
  37.5 30.6 %collective-permute-start.8 = (bf16[4,272,128]{2,1,0:T(8,128)(2,1)}, bf16[4,272,128]{2,1,0:T(8,128)(2,1)S(1)}, u32[]{:S(2)}, u32[]{:S(2)}) collective-permute-start(bf16[4,272,128]{2,1,0:T(8,128)(2,1)} %collective-permute-done.refs_1_), channel_id=1, source_target_pairs={{0,64},{32,96},{64,0},{96,32},{1,65},{33,97},{65,1},{97,33},{2,66}... | collective-permute-start | bytes 835592 | tf_op jit(solution)/shard_map/ppermute | solution.py:426
  38.0 1.0 %copy-start.5 = (bf16[4,256,128]{2,1,0:T(8,128)(2,1)S(1)}, bf16[4,256,128]{2,1,0:T(8,128)(2,1)}, u32[]{:S(2)}) copy-start(bf16[4,256,128]{2,1,0:T(8,128)(2,1)} %copy-done.4) | copy-start | bytes 786436
  44.7 0.7 copy-start.2
  45.4 39.0 %collective-permute-start.9 = (bf16[4,272,128]{2,1,0:T(8,128)(2,1)}, bf16[4,272,128]{2,1,0:T(8,128)(2,1)S(1)}, u32[]{:S(2)}, u32[]{:S(2)}) collective-permute-start(bf16[4,272,128]{2,1,0:T(8,128)(2,1)} %get-tuple-element.33), channel_id=1, source_target_pairs={{0,32},{32,0},{64,96},{96,64},{1,33},{33,1},{65,97},{97,65},{2,34}... | collective-permute-start | bytes 835592 | tf_op jit(solution)/shard_map/ppermute | solution.py:426
  49.6 1.0 %copy-start.3 = (bf16[4,256,128]{2,1,0:T(8,128)(2,1)S(1)}, bf16[4,256,128]{2,1,0:T(8,128)(2,1)}, u32[]{:S(2)}) copy-start(bf16[4,256,128]{2,1,0:T(8,128)(2,1)} %copy-done.2) | copy-start | bytes 786436
  68.1 20.0 %all-to-all-start.1 = ((bf16[16,272,128]{2,1,0:T(8,128)(2,1)}), bf16[16,272,128]{2,1,0:T(8,128)(2,1)S(1)}, u32[]{:S(2)}, u32[]{:S(2)}) async-start(bf16[16,272,128]{2,1,0:T(8,128)(2,1)} %prefix_part.3), calls=%async_computation.1 | async-start | bytes 2228224 | tf_op jit(solution)/shard_map/all_to_all | solution.py:456
  75.5 8.9 %collective-permute-start.10 = (bf16[4,272,128]{2,1,0:T(8,128)(2,1)S(1)}, bf16[4,272,128]{2,1,0:T(8,128)(2,1)S(1)}, u32[]{:S(2)}, u32[]{:S(2)}) collective-permute-start(bf16[4,272,128]{2,1,0:T(8,128)(2,1)S(1)} %page_part.4), channel_id=1, source_target_pairs={{0,64},{32,96},{64,0},{96,32},{1,65},{33,97},{65,1},{97,33},{2,66}... | collective-permute-start | bytes 835592 | tf_op jit(solution)/shard_map/ppermute | solution.py:426
  82.1 9.7 %collective-permute-start.11 = (bf16[4,272,128]{2,1,0:T(8,128)(2,1)}, bf16[4,272,128]{2,1,0:T(8,128)(2,1)S(1)}, u32[]{:S(2)}, u32[]{:S(2)}) collective-permute-start(bf16[4,272,128]{2,1,0:T(8,128)(2,1)} %page_part.5), channel_id=1, source_target_pairs={{0,96},{32,64},{64,32},{96,0},{1,97},{33,65},{65,33},{97,1},{2,98}... | collective-permute-start | bytes 835592 | tf_op jit(solution)/shard_map/ppermute | solution.py:426
